TPU v7x, 32 devices: a whole 2x2x4 slice. The times are simulated.
32 devices in a mesh: dp: 8 (over z, core), ctx: 4 (over y, x).
Axes of the slice: x: 2, y: 2, z: 4, core: 2. Of those that a mesh axis runs over, the one named last changes fastest.
Arguments:
- proj_read: bfloat16 [4096, 2048], P(('dp', 'ctx')), may hold values from -6 to 6
- norm_gain: float32 [512], replicated, may hold values from 0.1 to 1.9
- owner_of: int32 [16], replicated, may hold values from 0 to 7, as said below
- user_of: int32 [4096], P(('dp', 'ctx')), may hold values from -1 to 15, as said below
- grad_output: bfloat16 [4096, 512], P(('dp', 'ctx')), may hold values from -6 to 6
Outputs:
- layer_out: bfloat16 [4096, 512], P(('dp', 'ctx'))
- grad_read: bfloat16 [4096, 2048], P(('dp', 'ctx'))
Inputs may be any that keep to these rules, and one draw needn't show every extreme that they name: `owner_of`: every owner index names exactly 2 users. `user_of`: -1 marks an empty row; at most 16 rows of one reader device hold users of one owner.
All inputs are finite; a program needn't handle non-finite values.
Results may differ from a plain program's by a relative error of at most 0.0085.
Values may be sent and summed in bfloat16 or wider, within the bound.
No kernel may reach another device: no remote copies, remote signals or barrier semaphores. Data moves between devices by JAX's collectives and lax.ppermute only.
A program may use at most 64 MiB of HBM per device.

v0:
```python
import jax
import jax.numpy as jnp
from jax import lax
from jax.sharding import PartitionSpec as P

HEADS = 4
HD = 128


epsilon = 1e-05


def block_length(total_rows, shard_rows):
    shard_total = total_rows // shard_rows
    best_factor = 1
    for factor in range(1, shard_total + 1):
        if shard_total % factor == 0 and factor * shard_rows <= 1024:
            best_factor = factor
    return best_factor * shard_rows


def silu_slope(scores):
    sigmoid_part = jax.nn.sigmoid(scores)
    return sigmoid_part * (1.0 + scores * (1.0 - sigmoid_part))


def visible_pairs(query_users, query_places, key_users, key_places):
    same_user = (query_users[:, None] == key_users[None, :]) & (query_users[:, None] >= 0)
    return same_user & (key_places[None, :] <= query_places[:, None])


def run_blocks(carry_now, shard_piece, block_rows, step_fn):
    total_rows = shard_piece[0].shape[0]

    def one_block(block_index, carry_here):
        offset = block_index * block_rows
        block_part = tuple(
            (
                lax.dynamic_slice_in_dim(array_item, offset, block_rows, 0)
                for array_item in shard_piece
            )
        )
        return step_fn(carry_here, block_part, offset)

    return lax.fori_loop(0, total_rows // block_rows, one_block, carry_now)


def local(proj_read, norm_gain, owner_of, user_of, grad_output):
    slot_rows = proj_read.shape[0]
    reader_peers = lax.axis_size("dp")
    per_pair = slot_rows // reader_peers
    feature_width = HEADS * HD
    score_scale = HD ** (-0.5)
    group_rows = slot_rows * lax.axis_size("ctx")
    user_range = jnp.arange(owner_of.shape[0], dtype=jnp.int32)
    owners = jnp.sum(
        jnp.where(user_of[:, None] == user_range[None, :], owner_of[None, :], 0), axis=1
    )
    is_live = user_of >= 0
    owner_hits = (owners[:, None] == jnp.arange(reader_peers, dtype=jnp.int32)[None, :]) & is_live[
        :, None
    ]
    running = jnp.cumsum(owner_hits.astype(jnp.int32), axis=0) - 1
    ranks_mine = jnp.sum(jnp.where(owner_hits, running, 0), axis=1)
    send_slot = jnp.where(is_live, owners * per_pair + ranks_mine, -1)
    slot_range = jnp.arange(slot_rows, dtype=jnp.int32)
    slot_match = send_slot[None, :] == slot_range[:, None]
    filled = jnp.any(slot_match, axis=1)
    source_row = jnp.sum(jnp.where(slot_match, slot_range[None, :], 0), axis=1)
    outgoing = jnp.where(
        filled[:, None], jnp.take(proj_read, source_row, axis=0), jnp.zeros((), jnp.bfloat16)
    )
    outgoing_users = jnp.where(filled, jnp.take(user_of, source_row), -1)
    arrived, arrived_users = (
        lax.all_to_all(outgoing, "dp", split_axis=0, concat_axis=0, tiled=True),
        lax.all_to_all(outgoing_users, "dp", split_axis=0, concat_axis=0, tiled=True),
    )
    own_start = lax.axis_index("ctx") * slot_rows
    own_places = own_start + slot_range
    unit_rows = arrived[:, :feature_width]
    queries = arrived[:, feature_width : 2 * feature_width]
    key_values = arrived[:, 2 * feature_width :]
    query_heads = queries.reshape(slot_rows, HEADS, HD)
    key_heads = key_values[:, :feature_width].reshape(slot_rows, HEADS, HD)
    value_heads = key_values[:, feature_width:].reshape(slot_rows, HEADS, HD)

    def forward_step(total_out, block_part, first_row):
        block_kv, block_users = block_part
        block_size = block_kv.shape[0]
        remote_keys = block_kv[:, :feature_width].reshape(block_size, HEADS, HD)
        remote_values = block_kv[:, feature_width:].reshape(block_size, HEADS, HD)
        scores = (
            jnp.einsum("qhd,khd->hqk", query_heads, remote_keys, preferred_element_type=jnp.float32)
            * score_scale
        )
        visible = visible_pairs(
            arrived_users,
            own_places,
            block_users,
            first_row + jnp.arange(block_size, dtype=jnp.int32),
        )
        weights = jnp.where(visible[None], jax.nn.silu(scores), 0.0).astype(jnp.bfloat16)
        summed = jnp.einsum(
            "hqk,khd->qhd", weights, remote_values, preferred_element_type=jnp.float32
        )
        return total_out + summed.reshape(slot_rows, feature_width)

    zero_rows = jnp.zeros((slot_rows, feature_width), jnp.float32)
    shard_piece = (
        lax.all_gather(key_values, "ctx", axis=0, tiled=True),
        lax.all_gather(arrived_users, "ctx", axis=0, tiled=True),
    )
    block_rows = block_length(shard_piece[0].shape[0], slot_rows)
    forward_result = run_blocks(zero_rows, shard_piece, block_rows, forward_step)
    mean_out = jnp.mean(forward_result, axis=1, keepdims=True)
    centered = forward_result - mean_out
    inv_std = lax.rsqrt(jnp.mean(centered * centered, axis=1, keepdims=True) + epsilon)
    normed = centered * inv_std
    unit_float = unit_rows.astype(jnp.float32)
    layer_out = (normed * norm_gain * unit_float).astype(jnp.bfloat16)
    grad_float = grad_output.astype(jnp.float32)
    unit_grads = (grad_float * norm_gain * normed).astype(jnp.bfloat16)
    grad_normed = grad_float * norm_gain * unit_float
    mean_grad = jnp.mean(grad_normed, axis=1, keepdims=True)
    mean_cross = jnp.mean(grad_normed * normed, axis=1, keepdims=True)
    out_grads = (inv_std * (grad_normed - mean_grad - normed * mean_cross)).astype(jnp.bfloat16)

    def backward_step(carry_here, block_part, first_row):
        block_queries, block_grads, block_users = block_part
        block_size = block_queries.shape[0]
        remote_queries = block_queries.reshape(block_size, HEADS, HD)
        remote_grads = block_grads.reshape(block_size, HEADS, HD)
        scores = (
            jnp.einsum(
                "qhd,khd->hqk", remote_queries, key_heads, preferred_element_type=jnp.float32
            )
            * score_scale
        )
        visible = visible_pairs(
            block_users,
            first_row + jnp.arange(block_size, dtype=jnp.int32),
            arrived_users,
            own_places,
        )[None]
        weights = jnp.where(visible, jax.nn.silu(scores), 0.0).astype(jnp.bfloat16)
        weight_grads = jnp.einsum(
            "qhd,khd->hqk", remote_grads, value_heads, preferred_element_type=jnp.float32
        )
        score_grads = jnp.where(
            visible, weight_grads * silu_slope(scores) * score_scale, 0.0
        ).astype(jnp.bfloat16)
        value_sum = jnp.einsum(
            "hqk,qhd->khd", weights, remote_grads, preferred_element_type=jnp.float32
        ).reshape(slot_rows, feature_width)
        key_sum = jnp.einsum(
            "hqk,qhd->khd", score_grads, remote_queries, preferred_element_type=jnp.float32
        ).reshape(slot_rows, feature_width)
        new_keys = carry_here[0] + key_sum
        new_values = carry_here[1] + value_sum
        window_sum = (
            jnp.einsum("hqk,khd->qhd", score_grads, key_heads, preferred_element_type=jnp.float32)
            .reshape(block_size, feature_width)
            .astype(jnp.bfloat16)
        )
        return (
            new_keys,
            new_values,
            lax.dynamic_update_slice_in_dim(carry_here[2], window_sum, first_row, 0),
        )

    start_carry = (zero_rows, zero_rows, jnp.zeros((group_rows, feature_width), jnp.bfloat16))
    shard_piece = (
        lax.all_gather(queries, "ctx", axis=0, tiled=True),
        lax.all_gather(out_grads, "ctx", axis=0, tiled=True),
        lax.all_gather(arrived_users, "ctx", axis=0, tiled=True),
    )
    block_rows = block_length(shard_piece[0].shape[0], slot_rows)
    key_results = run_blocks(start_carry, shard_piece, block_rows, backward_step)
    key_grads = key_results[0]
    value_grads = key_results[1]
    query_grads = lax.psum_scatter(key_results[2], "ctx", scatter_dimension=0, tiled=True).astype(
        jnp.float32
    )
    grads_owned = jnp.concatenate(
        [
            unit_grads,
            query_grads.astype(jnp.bfloat16),
            key_grads.astype(jnp.bfloat16),
            value_grads.astype(jnp.bfloat16),
        ],
        axis=1,
    )
    returned = lax.all_to_all(grads_owned, "dp", split_axis=0, concat_axis=0, tiled=True)
    back_rows = jnp.take(returned, jnp.maximum(send_slot, 0), axis=0)
    grad_read = jnp.where(is_live[:, None], back_rows, jnp.zeros((), jnp.bfloat16))
    return (layer_out, grad_read)


def solution(mesh):
    in_specs = (P(("dp", "ctx"), None), P(), P(), P(("dp", "ctx")), P(("dp", "ctx"), None))
    out_specs = (P(("dp", "ctx"), None), P(("dp", "ctx"), None))
    return jax.shard_map(local, mesh=mesh, in_specs=in_specs, out_specs=out_specs, check_vma=False)
```

profile of v0, /device:TPU:1, one launch (start us, length us, event | category | flops | bytes accessed | tf_op | source)
XLA Modules:
  0.0 141.5 jit_solution(17670771440552236641)
XLA Ops:
  7.2 0.7 broadcast_compare_fusion.3
  8.8 0.9 gather_fusion.1
  9.7 0.9 select_select_fusion.1
  10.6 6.4 %all-to-all-start = ((bf16[8,16,2048]{2,1,0:T(8,128)(2,1)}), bf16[8,16,2048]{2,1,0:T(8,128)(2,1)S(1)}, u32[]{:S(2)}, u32[]{:S(2)}) async-start(bf16[8,16,2048]{2,1,0:T(8,128)(2,1)} %bitcast), calls=%async_computation | async-start | bytes 1048576 | tf_op jit(solution)/shard_map/all_to_all | solution.py:75
  17.2 1.2 gather_fusion
  18.5 0.6 select_select_fusion.2
  19.1 12.4 %all-to-all-done = bf16[8,16,2048]{2,1,0:T(8,128)(2,1)S(1)} async-done(((bf16[8,16,2048]{2,1,0:T(8,128)(2,1)}), bf16[8,16,2048]{2,1,0:T(8,128)(2,1)S(1)}, u32[]{:S(2)}, u32[]{:S(2)}) %all-to-all-start) | async-done | bytes 524320 | tf_op jit(solution)/shard_map/all_to_all | solution.py:75
  31.5 4.1 %all-to-all-start.1 = ((s32[8,16,1]{1,2,0:T(1,128)}), s32[8,16,1]{1,2,0:T(1,128)S(1)}, u32[]{:S(2)}, u32[]{:S(2)}) async-start(s32[8,16,1]{1,2,0:T(1,128)} %bitcast.5), calls=%async_computation.1 | async-start | bytes 8192 | tf_op jit(solution)/shard_map/all_to_all | solution.py:76
  35.6 0.7 slice.38
  36.4 4.0 %all-to-all-done.1 = s32[8,16,1]{1,2,0:T(1,128)S(1)} async-done(((s32[8,16,1]{1,2,0:T(1,128)}), s32[8,16,1]{1,2,0:T(1,128)S(1)}, u32[]{:S(2)}, u32[]{:S(2)}) %all-to-all-start.1) | async-done | bytes 544 | tf_op jit(solution)/shard_map/all_to_all | solution.py:76
  41.0 0.7 reduce.8
  41.7 5.9 %all-gather = s32[4,1,128]{2,1,0:T(1,128)S(1)} all-gather(s32[1,1,128]{2,1,0:T(1,128)S(1)} %reshape.337), channel_id=1, replica_groups=mesh['dp'=8,'ctx'=4] {'ctx'}, dimensions={0}, use_global_device_ids=true | all-gather | bytes 2560 | tf_op jit(solution)/shard_map/all_gather | solution.py:111
  47.7 0.8 fusion.12
  48.4 0.8 fusion.13
  49.4 8.7 %all_gather.16 = bf16[512,512]{1,0:T(8,128)(2,1)S(1)} all-gather(bf16[128,512]{1,0:T(8,128)(2,1)S(1)} %get-tuple-element.63), channel_id=1, replica_groups=mesh['dp'=8,'ctx'=4] {'ctx'}, dimensions={0}, use_global_device_ids=true | all-gather | bytes 655360 | tf_op jit(solution)/shard_map/all_gather | solution.py:173
  58.6 1.4 convolution_multiply_fusion
  60.0 7.8 %all-gather.3.cloned.1.call-done = bf16[512,1024]{1,0:T(8,128)(2,1)} async-done(((bf16[128,1024]{1,0:T(8,128)(2,1)}), bf16[512,1024]{1,0:T(8,128)(2,1)}) %all-gather.3.cloned.1.call-update) | async-done | bytes 1048592 | tf_op jit(solution)/shard_map/all_gather | solution.py:110
  67.8 1.3 fusion.24
  69.5 1.6 %fusion.26 = (f32[128]{0:T(128)S(1)}, f32[4,128,128]{2,1,0:T(8,128)S(1)}) fusion(bf16[512,4,128]{0,2,1:T(8,128)(2,1)S(1)} %bitcast.62, bf16[128,4,128]{0,2,1:T(8,128)(2,1)S(1)} %bitcast.65, bf16[512,4,128]{0,2,1:T(8,128)(2,1)S(1)} %bitcast.63, pred[128,512]{1,0:T(8,128)(4,1)} %fusion.12), kind=kOutput, calls=%fused_computation.76 | convolution fusion | flops 136118144 | bytes 1507840 | tf_op jit(solution)/shard_map/while/body/eval_jaxpr/hqk,khd->qhd/dot_general | solution.py:103
  71.3 0.8 copy-done.5
  72.3 0.9 multiply_convert_fusion
  73.2 7.7 %all_gather.15 = bf16[512,512]{1,0:T(8,128)(2,1)S(1)} all-gather(bf16[128,512]{1,0:T(8,128)(2,1)S(1)} %get-tuple-element.59), channel_id=1, replica_groups=mesh['dp'=8,'ctx'=4] {'ctx'}, dimensions={0}, use_global_device_ids=true | all-gather | bytes 655360 | tf_op jit(solution)/shard_map/all_gather | solution.py:174
  81.1 0.8 copy-done.3
  81.9 1.5 %fusion.2 = bf16[4,512,128]{2,1,0:T(8,128)(2,1)S(1)} fusion(bf16[512,4,128]{0,2,1:T(8,128)(2,1)S(1)} %bitcast.60, bf16[128,4,128]{0,2,1:T(8,128)(2,1)S(1)} %bitcast.64, f32[4,512,128]{2,1,0:T(8,128)S(1)} %copy-done.2, pred[512,128]{1,0:T(8,128)(4,1)} %fusion.13), kind=kOutput, calls=%fused_computation.9 | convolution fusion | flops 69992448 | bytes 2293760 | tf_op jit(solution)/shard_map/while/body/eval_jaxpr/qhd,khd->hqk/dot_general | solution.py:146
  83.7 1.0 copy.75
  84.8 1.0 copy-done.4
  86.8 24.4 %reduce-scatter.2.cloned.1.call-done = bf16[128,512]{1,0:T(8,128)(2,1)} async-done(((bf16[512,512]{1,0:T(8,128)(2,1)}), bf16[128,512]{1,0:T(8,128)(2,1)}) %reduce-scatter.2.cloned.1.call-update) | async-done | bytes 131088 | tf_op jit(solution)/shard_map/reduce_scatter | solution.py:181
  111.2 1.7 %pad_maximum_fusion = bf16[128,2048]{1,0:T(8,128)(2,1)} fusion(bf16[128,512]{1,0:T(8,128)(2,1)S(1)} %copy.77, bf16[128,512]{1,0:T(8,128)(2,1)S(1)} %copy.76, bf16[128,512]{1,0:T(8,128)(2,1)} %reduce-scatter.2.cloned.1.call-done, bf16[128,512]{1,0:T(8,128)(2,1)S(1)} %get-tuple-element.64), kind=kLoop, calls=%fused_computation.16 | loop fusion | flops 2097152 | bytes 1048576 | tf_op jit(solution)/shard_map/concatenate | solution.py:184
  112.9 5.4 %all-to-all-start.2 = ((bf16[8,16,2048]{2,1,0:T(8,128)(2,1)}), bf16[8,16,2048]{2,1,0:T(8,128)(2,1)S(1)}, u32[]{:S(2)}, u32[]{:S(2)}) async-start(bf16[8,16,2048]{2,1,0:T(8,128)(2,1)} %bitcast.21), calls=%async_computation.3 | async-start | bytes 1048576 | tf_op jit(solution)/shard_map/all_to_all | solution.py:193
  118.3 14.5 %all-to-all-done.2 = bf16[8,16,2048]{2,1,0:T(8,128)(2,1)S(1)} async-done(((bf16[8,16,2048]{2,1,0:T(8,128)(2,1)}), bf16[8,16,2048]{2,1,0:T(8,128)(2,1)S(1)}, u32[]{:S(2)}, u32[]{:S(2)}) %all-to-all-start.2) | async-done | bytes 524320 | tf_op jit(solution)/shard_map/all_to_all | solution.py:193
  132.8 0.9 gather_fusion.2
  133.8 0.9 select_select_fusion
  (61 shorter events, 4.8 us)
Async XLA Ops:
  7.2 1.6 %copy-start = (bf16[128,2048]{1,0:T(8,128)(2,1)S(1)}, bf16[128,2048]{1,0:T(8,128)(2,1)}, u32[]{:S(2)}) copy-start(bf16[128,2048]{1,0:T(8,128)(2,1)} %param.7) | copy-start | bytes 1572868
  7.2 0.7 copy-start.1
  7.2 0.7 copy-start.8
  10.6 20.9 %all-to-all-start = ((bf16[8,16,2048]{2,1,0:T(8,128)(2,1)}), bf16[8,16,2048]{2,1,0:T(8,128)(2,1)S(1)}, u32[]{:S(2)}, u32[]{:S(2)}) async-start(bf16[8,16,2048]{2,1,0:T(8,128)(2,1)} %bitcast), calls=%async_computation | async-start | bytes 1048576 | tf_op jit(solution)/shard_map/all_to_all | solution.py:75
  31.5 8.9 %all-to-all-start.1 = ((s32[8,16,1]{1,2,0:T(1,128)}), s32[8,16,1]{1,2,0:T(1,128)S(1)}, u32[]{:S(2)}, u32[]{:S(2)}) async-start(s32[8,16,1]{1,2,0:T(1,128)} %bitcast.5), calls=%async_computation.1 | async-start | bytes 8192 | tf_op jit(solution)/shard_map/all_to_all | solution.py:76
  35.6 32.2 %all-gather.3.cloned.1.call-start = ((), (), s32[]{:S(2)}) async-start(), calls=%async_computation.4 | async-start | bytes 1310720 | tf_op jit(solution)/shard_map/all_gather | solution.py:110
  36.3 74.8 %reduce-scatter.2.cloned.1.call-start = ((), (), s32[]{:S(2)}) async-start(), calls=%async_computation.5 | async-start | bytes 655360 | tf_op jit(solution)/shard_map/reduce_scatter | solution.py:181
  71.2 0.9 copy-start.5
  71.2 0.9 copy-start.7
  73.2 8.8 %copy-start.2 = (f32[4,512,128]{2,1,0:T(8,128)S(1)}, f32[4,512,128]{2,1,0:T(8,128)}, u32[]{:S(2)}) copy-start(f32[4,512,128]{2,1,0:T(8,128)} %convolution_multiply_fusion) | copy-start | bytes 3145732
  81.1 0.8 copy-start.3
  83.7 1.0 copy-start.6
  84.7 1.0 copy-start.4
  112.9 19.9 %all-to-all-start.2 = ((bf16[8,16,2048]{2,1,0:T(8,128)(2,1)}), bf16[8,16,2048]{2,1,0:T(8,128)(2,1)S(1)}, u32[]{:S(2)}, u32[]{:S(2)}) async-start(bf16[8,16,2048]{2,1,0:T(8,128)(2,1)} %bitcast.21), calls=%async_computation.3 | async-start | bytes 1048576 | tf_op jit(solution)/shard_map/all_to_all | solution.py:193
Sparse Core Ops, SparseCore 0:
  38.8 28.8 all-gather.2
  84.9 26.2 reduce-scatter.1
where the time goes:
time: 143 us; the launch traced here: 142 us
  waiting for transfers between devices  63.1 us (44%)
  blocking collectives  22.4 us (16%)
  starting transfers between devices  15.9 us (11%)
  between operations  14.3 us (10%)
  local copies, waits for them, and re-layouts  11.2 us (8%)
  other arithmetic  9.16 us (6%)
  matrix products  5.53 us (4%)
    reduce_scatter x1, waiting for transfers between devices, local(): lax.psum_scatter(key_results[2], 'ctx', scatter_dimension=0, tiled=True)  24.4 us
    all_to_all x1, waiting for transfers between devices, local(): lax.all_to_all(grads_owned, 'dp', split_axis=0, concat_axis=0, tiled=True)  14.5 us
    all_to_all x1, waiting for transfers between devices, local(): lax.all_to_all(outgoing, 'dp', split_axis=0, concat_axis=0, tiled=True)  12.4 us
    all_gather x1, blocking collectives, local(): lax.all_gather(queries, 'ctx', axis=0, tiled=True)  8.71 us
    all_gather x1, waiting for transfers between devices, local(): lax.all_gather(key_values, 'ctx', axis=0, tiled=True)  7.78 us
    all_gather x1, blocking collectives, local(): lax.all_gather(out_grads, 'ctx', axis=0, tiled=True)  7.75 us
    all_to_all x1, starting transfers between devices, local(): lax.all_to_all(outgoing, 'dp', split_axis=0, concat_axis=0, tiled=True)  6.38 us
    all_gather x1, blocking collectives, local(): lax.all_gather(arrived_users, 'ctx', axis=0, tiled=True)  5.9 us
  transfers between devices with their start and end apart: 5, of which 5 were waited for; matrix products, arithmetic and copies ran while one was open for 6% of the time, Pallas kernels for 0%

commit v1 on v0

--- a/solution.py
+++ b/solution.py
@@ -1,6 +1,10 @@
+import functools
+
 import jax
 import jax.numpy as jnp
 from jax import lax
+from jax.experimental import pallas as pl
+from jax.experimental.pallas import tpu as pltpu
 from jax.sharding import PartitionSpec as P
 
 HEADS = 4
@@ -45,7 +49,7 @@
     return lax.fori_loop(0, total_rows // block_rows, one_block, carry_now)
 
 
-def local(proj_read, norm_gain, owner_of, user_of, grad_output):
+def windowed(proj_read, norm_gain, owner_of, user_of, grad_output):
     slot_rows = proj_read.shape[0]
     reader_peers = lax.axis_size("dp")
     per_pair = slot_rows // reader_peers
@@ -196,7 +200,295 @@
     return (layer_out, grad_read)
 
 
+def vmem(count):
+    return [pl.BlockSpec(memory_space=pltpu.VMEM)] * count
+
+
+def smem():
+    return pl.BlockSpec(memory_space=pltpu.SMEM)
+
+
+def dot(left, right, left_dim, right_dim):
+    return lax.dot_general(
+        left, right, (((left_dim,), (right_dim,)), ((), ())), preferred_element_type=jnp.float32
+    )
+
+
+def slot_kernel(owner_ref, user_ref, proj_ref, send_ref, users_ref, slot_ref, *, per_pair):
+    slots = user_ref.shape[1]
+    users = user_ref[...]
+    owners = jnp.zeros_like(users)
+    for user in range(owner_ref.shape[0]):
+        owners = jnp.where(users == user, owner_ref[user], owners)
+    is_live = users >= 0
+    owner_range = lax.broadcasted_iota(jnp.int32, (slots // per_pair, slots), 0)
+    hits = (owner_range == owners) & is_live
+    earlier = lax.broadcasted_iota(jnp.int32, (slots, slots), 0)
+    later = lax.broadcasted_iota(jnp.int32, (slots, slots), 1)
+    upto = (earlier <= later).astype(jnp.bfloat16)
+    hits_f = hits.astype(jnp.float32)
+    running = dot(hits_f.astype(jnp.bfloat16), upto, 1, 0)
+    ranks = jnp.sum(hits_f * running, axis=0, keepdims=True).astype(jnp.int32) - 1
+    slot = jnp.where(is_live, owners * per_pair + ranks, -1)
+    slot_ref[...] = slot
+    placed = (earlier == slot).astype(jnp.bfloat16)
+    tagged = (users + 1).astype(jnp.float32).astype(jnp.bfloat16)
+    tagged = jnp.broadcast_to(tagged, (16, slots))
+    users_ref[...] = dot(tagged, placed, 1, 1)[:1]
+    for part in range(4):
+        width = HEADS * HD
+        rows = dot(placed, proj_ref[:, part * width : (part + 1) * width], 1, 0)
+        rows = rows.astype(jnp.bfloat16)
+        for head in range(HEADS):
+            send_ref[head * slots : (head + 1) * slots, part * HD : (part + 1) * HD] = rows[
+                :, head * HD : (head + 1) * HD
+            ]
+
+
+def columns_kernel(place_ref, grad_ref, *piece_refs):
+    me = place_ref[0]
+    for step, piece_ref in enumerate(piece_refs):
+        start = pl.multiple_of((me ^ step) * HD, HD)
+        piece_ref[...] = grad_ref[:, pl.ds(start, HD)]
+
+
+def group_kernel(place_ref, users_ref, *refs, per_pair):
+    piece_refs, (group_users_ref, grads_ref) = refs[:HEADS], refs[HEADS:]
+    me, owner = place_ref[0], place_ref[1]
+    readers = users_ref.shape[0] // HEADS
+    slots = users_ref.shape[1]
+    source = lax.broadcasted_iota(jnp.int32, (slots, slots), 0)
+    target = lax.broadcasted_iota(jnp.int32, (slots, slots), 1)
+    same_rank = lax.rem(source, per_pair) == lax.rem(target, per_pair)
+    spread = (same_rank & (lax.div(source, per_pair) == owner)).astype(jnp.bfloat16)
+    mine = dot(users_ref[...].astype(jnp.bfloat16), spread, 1, 0)
+    distance = lax.broadcasted_iota(jnp.int32, (readers, slots), 0)
+    reader = lax.div(lax.broadcasted_iota(jnp.int32, (readers, slots), 1), per_pair)
+    from_reader = reader == (distance ^ owner)
+    for step in range(HEADS):
+        window = me ^ step
+        rows = mine[step * readers : (step + 1) * readers]
+        group_users_ref[pl.ds(window, 1), :] = (
+            jnp.sum(jnp.where(from_reader, rows, 0.0), axis=0, keepdims=True) - 1.0
+        )
+        grads_ref[pl.ds(pl.multiple_of(window * slots, slots), slots), :] = piece_refs[step][...]
+
+
+def visible_block(users_ref, query_window, key_windows):
+    size = users_ref.shape[1]
+    query_users = jnp.broadcast_to(users_ref[query_window : query_window + 1], (size, size)).T
+    blocks = []
+    for window in range(key_windows):
+        block = (query_users == users_ref[window : window + 1]) & (query_users >= 0.0)
+        if window == query_window:
+            rows = lax.broadcasted_iota(jnp.int32, (size, size), 0)
+            columns = lax.broadcasted_iota(jnp.int32, (size, size), 1)
+            block = block & (columns <= rows)
+        blocks.append(block)
+    return jnp.concatenate(blocks, axis=1)
+
+
+def forward_kernel(users_ref, rows_ref, grads_ref, gain_ref, attended_ref, stats_ref):
+    size = users_ref.shape[1]
+    scale = HD ** (-0.5)
+    lane = lax.broadcasted_iota(jnp.int32, (size, HD), 1)
+    for window in range(users_ref.shape[0]):
+        here = slice(window * size, (window + 1) * size)
+        upto = slice(0, (window + 1) * size)
+        queries = rows_ref[here, HD : 2 * HD]
+        scores = dot(queries, rows_ref[upto, 2 * HD : 3 * HD], 1, 1) * scale
+        visible = visible_block(users_ref, window, window + 1)
+        weights = jnp.where(visible, scores * jax.nn.sigmoid(scores), 0.0).astype(jnp.bfloat16)
+        attended = dot(weights, rows_ref[upto, 3 * HD :], 1, 0)
+        attended_ref[here] = attended
+        grad_normed = (
+            grads_ref[here].astype(jnp.float32)
+            * gain_ref[...]
+            * rows_ref[here, :HD].astype(jnp.float32)
+        )
+        mean = jnp.mean(attended, axis=1, keepdims=True)
+        centered = attended - mean
+        spread = jnp.sum(centered * centered, axis=1, keepdims=True)
+        grad_sum = jnp.sum(grad_normed, axis=1, keepdims=True)
+        cross = jnp.sum(grad_normed * centered, axis=1, keepdims=True)
+        packed = jnp.where(
+            lane == 0, mean, jnp.where(lane == 1, spread, jnp.where(lane == 2, grad_sum, cross))
+        )
+        stats_ref[:, here] = packed.T[:8]
+
+
+def backward_kernel(
+    place_ref, users_ref, rows_ref, grads_ref, gain_ref, attended_ref, *refs
+):
+    stats_refs = refs[:HEADS]
+    out_ref = refs[HEADS]
+    layer_refs = refs[HEADS + 1 : 2 * HEADS + 1]
+    layer_all, out_grads_all, key_sum, value_sum = refs[2 * HEADS + 1 :]
+    me = place_ref[0]
+    size = users_ref.shape[1]
+    windows = users_ref.shape[0]
+    scale = HD ** (-0.5)
+    width = float(HEADS * HD)
+    stats = [stat_ref[...] for stat_ref in stats_refs]
+    mean = sum(stat[0:1] for stat in stats) * (1.0 / HEADS)
+    spread = sum(stat[1:2] + HD * (stat[0:1] - mean) * (stat[0:1] - mean) for stat in stats)
+    inv_std = lax.rsqrt(spread / width + epsilon)
+    mean_grad = sum(stat[2:3] for stat in stats) / width
+    cross = sum(stat[3:4] + (stat[0:1] - mean) * stat[2:3] for stat in stats)
+    mean_cross = cross * inv_std / width
+    key_sum[...] = jnp.zeros_like(key_sum)
+    value_sum[...] = jnp.zeros_like(value_sum)
+    row = lax.broadcasted_iota(jnp.int32, (size, size), 0)
+    for window in range(windows):
+        here = slice(window * size, (window + 1) * size)
+        upto = slice(0, (window + 1) * size)
+        packed = jnp.where(
+            row == 0,
+            mean[:, here],
+            jnp.where(
+                row == 1,
+                inv_std[:, here],
+                jnp.where(row == 2, mean_grad[:, here], mean_cross[:, here]),
+            ),
+        ).T
+        unit = rows_ref[here, :HD].astype(jnp.float32)
+        grad_gain = grads_ref[here].astype(jnp.float32) * gain_ref[...]
+        normed = (attended_ref[here] - packed[:, 0:1]) * packed[:, 1:2]
+        layer_all[here] = (normed * gain_ref[...] * unit).astype(jnp.bfloat16)
+        out_ref[here, :HD] = (grad_gain * normed).astype(jnp.bfloat16)
+        out_grads = (
+            packed[:, 1:2] * (grad_gain * unit - packed[:, 2:3] - normed * packed[:, 3:4])
+        ).astype(jnp.bfloat16)
+        queries = rows_ref[here, HD : 2 * HD]
+        keys = rows_ref[upto, 2 * HD : 3 * HD]
+        scores = dot(queries, keys, 1, 1) * scale
+        visible = visible_block(users_ref, window, window + 1)
+        sigmoid = jax.nn.sigmoid(scores)
+        weights = jnp.where(visible, scores * sigmoid, 0.0).astype(jnp.bfloat16)
+        slope = jnp.where(visible, sigmoid * (1.0 + scores * (1.0 - sigmoid)) * scale, 0.0)
+        score_grads = (dot(out_grads, rows_ref[upto, 3 * HD :], 1, 1) * slope).astype(jnp.bfloat16)
+        out_ref[here, HD : 2 * HD] = dot(score_grads, keys, 1, 0).astype(jnp.bfloat16)
+        key_sum[upto] += dot(score_grads, queries, 0, 0)
+        value_sum[upto] += dot(weights, out_grads, 0, 0)
+    out_ref[:, 2 * HD : 3 * HD] = key_sum[...].astype(jnp.bfloat16)
+    out_ref[:, 3 * HD :] = value_sum[...].astype(jnp.bfloat16)
+    for step, layer_ref in enumerate(layer_refs):
+        start = pl.multiple_of((me ^ step) * size, size)
+        layer_ref[...] = layer_all[pl.ds(start, size), :]
+
+
+def unslot_kernel(place_ref, slot_ref, returned_ref, *refs):
+    piece_refs, (layer_ref, grad_ref) = refs[:HEADS], refs[HEADS:]
+    me = place_ref[0]
+    slots = slot_ref.shape[1]
+    width = HEADS * HD
+    placed = (
+        lax.broadcasted_iota(jnp.int32, (slots, slots), 0) == slot_ref[...]
+    ).astype(jnp.bfloat16)
+    for head in range(HEADS):
+        rows = dot(placed, returned_ref[head * slots : (head + 1) * slots], 0, 0)
+        rows = rows.astype(jnp.bfloat16)
+        for part in range(4):
+            start = part * width + head * HD
+            grad_ref[:, start : start + HD] = rows[:, part * HD : (part + 1) * HD]
+    for step, piece_ref in enumerate(piece_refs):
+        start = pl.multiple_of((me ^ step) * HD, HD)
+        layer_ref[:, pl.ds(start, HD)] = piece_ref[...]
+
+
+def swap(value, axis, distance):
+    pairs = [(index, index ^ distance) for index in range(lax.axis_size(axis))]
+    return lax.ppermute(value, axis, pairs)
+
+
+def by_heads(proj_read, norm_gain, owner_of, user_of, grad_output):
+    slots = proj_read.shape[0]
+    readers = lax.axis_size("dp")
+    per_pair = slots // readers
+    group_rows = slots * HEADS
+    width = 4 * HD
+    me = lax.axis_index("ctx")
+    place = jnp.stack([me, lax.axis_index("dp")]).astype(jnp.int32)
+    gain = lax.dynamic_slice_in_dim(norm_gain, me * HD, HD, 0).reshape(1, HD)
+    rows_shape = jax.ShapeDtypeStruct((group_rows, width), jnp.bfloat16)
+    piece_shape = jax.ShapeDtypeStruct((slots, HD), jnp.bfloat16)
+    outgoing, slot_users, slot = pl.pallas_call(
+        functools.partial(slot_kernel, per_pair=per_pair),
+        out_shape=(
+            rows_shape,
+            jax.ShapeDtypeStruct((1, slots), jnp.float32),
+            jax.ShapeDtypeStruct((1, slots), jnp.int32),
+        ),
+        in_specs=[smem()] + vmem(2),
+        out_specs=tuple(vmem(3)),
+        name="slot_rows",
+    )(owner_of, user_of.reshape(1, slots), proj_read)
+    rows = lax.all_to_all(outgoing, ("ctx", "dp"), split_axis=0, concat_axis=0, tiled=True)
+    pieces = pl.pallas_call(
+        columns_kernel,
+        out_shape=(piece_shape,) * HEADS,
+        in_specs=[smem()] + vmem(1),
+        out_specs=tuple(vmem(HEADS)),
+        name="cut_columns",
+    )(place, grad_output)
+    users = slot_users
+    for axis in ("dp", "ctx"):
+        distance = 1
+        while distance < lax.axis_size(axis):
+            users = jnp.concatenate([users, swap(users, axis, distance)], axis=0)
+            distance *= 2
+    pieces = (pieces[0],) + tuple(swap(pieces[step], "ctx", step) for step in range(1, HEADS))
+    group_users, grads = pl.pallas_call(
+        functools.partial(group_kernel, per_pair=per_pair),
+        out_shape=(
+            jax.ShapeDtypeStruct((HEADS, slots), jnp.float32),
+            jax.ShapeDtypeStruct((group_rows, HD), jnp.bfloat16),
+        ),
+        in_specs=[smem()] + vmem(1 + HEADS),
+        out_specs=tuple(vmem(2)),
+        name="lay_group",
+    )(place, users, *pieces)
+    attended, stats = pl.pallas_call(
+        forward_kernel,
+        out_shape=(
+            jax.ShapeDtypeStruct((group_rows, HD), jnp.float32),
+            jax.ShapeDtypeStruct((8, group_rows), jnp.float32),
+        ),
+        in_specs=vmem(4),
+        out_specs=tuple(vmem(2)),
+        name="forward",
+    )(group_users, rows, grads, gain)
+    all_stats = (stats,) + tuple(swap(stats, "ctx", step) for step in range(1, HEADS))
+    results = pl.pallas_call(
+        backward_kernel,
+        out_shape=(rows_shape,) + (piece_shape,) * HEADS,
+        in_specs=[smem()] + vmem(5 + HEADS),
+        out_specs=tuple(vmem(1 + HEADS)),
+        scratch_shapes=[
+            pltpu.VMEM((group_rows, HD), jnp.bfloat16),
+            pltpu.VMEM((group_rows, HD), jnp.bfloat16),
+            pltpu.VMEM((group_rows, HD), jnp.float32),
+            pltpu.VMEM((group_rows, HD), jnp.float32),
+        ],
+        name="backward",
+    )(place, group_users, rows, grads, gain, attended, *all_stats)
+    grads_owned, layers = results[0], results[1:]
+    returned = lax.all_to_all(grads_owned, ("ctx", "dp"), split_axis=0, concat_axis=0, tiled=True)
+    layers = (layers[0],) + tuple(swap(layers[step], "ctx", step) for step in range(1, HEADS))
+    return pl.pallas_call(
+        unslot_kernel,
+        out_shape=(
+            jax.ShapeDtypeStruct((slots, HEADS * HD), jnp.bfloat16),
+            jax.ShapeDtypeStruct((slots, 4 * HEADS * HD), jnp.bfloat16),
+        ),
+        in_specs=[smem()] + vmem(2 + HEADS),
+        out_specs=tuple(vmem(2)),
+        name="unslot_rows",
+    )(place, slot, returned, *layers)
+
+
 def solution(mesh):
     in_specs = (P(("dp", "ctx"), None), P(), P(), P(("dp", "ctx")), P(("dp", "ctx"), None))
     out_specs = (P(("dp", "ctx"), None), P(("dp", "ctx"), None))
+    local = by_heads if mesh.shape["ctx"] == HEADS else windowed
     return jax.shard_map(local, mesh=mesh, in_specs=in_specs, out_specs=out_specs, check_vma=False)

time: 143 us -> 79.3 us (0.55)
  waiting for transfers between devices: 63.1 us -> 23.7 us
  blocking collectives: 22.4 us -> 0 us
  starting transfers between devices: 15.9 us -> 33.4 us
  Pallas kernels: 0 us -> 13.9 us
  between operations: 14.3 us -> 0.76 us
  other arithmetic: 9.16 us -> 0.69 us
  matrix products: 5.53 us -> 0 us
  local copies, waits for them, and re-layouts: 11.2 us -> 5.86 us
    reduce_scatter x1 -> x0, waiting for transfers between devices: 24.4 us -> none  [local(): lax.psum_scatter(key_results[2], 'ctx', scatter_dimension=0, tiled=True)]
    all_gather x3 -> x0, blocking collectives: 22.4 us -> none  [the longest x1 8.71 us: local(): lax.all_gather(queries, 'ctx', axis=0, tiled=True)]
    all_to_all x3 -> x2, waiting for transfers between devices: 30.9 us -> 8.6 us  [the longest x1 8.6 us: by_heads(): lax.all_to_all(grads_owned, ('ctx', 'dp'), split_axis=0, concat_axis=0, t...]
    ppermute x0 -> x14, starting transfers between devices: none -> 16.6 us  [swap(): return lax.ppermute(value, axis, pairs)]
    ppermute x0 -> x14, waiting for transfers between devices: none -> 15.1 us  [swap(): return lax.ppermute(value, axis, pairs)]
    pallas_call x0 -> x6, Pallas kernels: none -> 13.9 us  [the longest x1 3.66 us: by_heads(): pl.pallas_call(backward_kernel, out_shape=(rows_shape,) + (piece_shape,)...]
    all_gather x1 -> x0, waiting for transfers between devices: 7.78 us -> none  [local(): lax.all_gather(key_values, 'ctx', axis=0, tiled=True)]
    dot_general x6 -> x0, matrix products: 5.53 us -> none  [the longest x1 1.56 us: forward_step(): jnp.einsum('hqk,khd->qhd', weights, remote_values, preferred_element_type...]
  transfers between devices with their start and end apart: 5 -> 16, of which waited for: 5 -> 10; matrix products, arithmetic and copies ran while one was open for 6% -> 4% of each run, Pallas kernels for 0% -> 4%
where the time goes in v1:
time: 79.3 us; the launch traced here: 78.4 us
  starting transfers between devices  33.4 us (42%)
  waiting for transfers between devices  23.7 us (30%)
  Pallas kernels  13.9 us (18%)
  local copies, waits for them, and re-layouts  5.86 us (7%)
    ppermute x14, starting transfers between devices, swap(): return lax.ppermute(value, axis, pairs)  16.6 us
    ppermute x14, waiting for transfers between devices, swap(): return lax.ppermute(value, axis, pairs)  15.1 us
    all_to_all x1, starting transfers between devices, by_heads(): lax.all_to_all(grads_owned, ('ctx', 'dp'), split_axis=0, concat_axis=0, t...  9.68 us
    all_to_all x1, waiting for transfers between devices, by_heads(): lax.all_to_all(grads_owned, ('ctx', 'dp'), split_axis=0, concat_axis=0, t...  8.6 us
    all_to_all x1, starting transfers between devices, by_heads(): lax.all_to_all(outgoing, ('ctx', 'dp'), split_axis=0, concat_axis=0, tile...  7.1 us
    pallas_call x1, Pallas kernels, by_heads(): pl.pallas_call(backward_kernel, out_shape=(rows_shape,) + (piece_shape,)...  3.66 us
    unnamed x32, local copies, waits for them, and re-layouts  3.47 us
    pallas_call x1, Pallas kernels, by_heads(): pl.pallas_call(forward_kernel, out_shape=(jax.ShapeDtypeStruct((group_row...  2.68 us
  transfers between devices with their start and end apart: 16, of which 10 were waited for; matrix products, arithmetic and copies ran while one was open for 4% of the time, Pallas kernels for 4%

profile of v1, /device:TPU:1, one launch (start us, length us, event | category | flops | bytes accessed | tf_op | source)
XLA Modules:
  0.0 78.4 jit_solution(4739834818684506402)
XLA Ops:
  0.6 2.3 %slot_rows.1 = (bf16[512,512]{1,0:T(8,128)(2,1)}, f32[1,128]{1,0:T(1,128)}, s32[1,128]{1,0:T(1,128)}) custom-call(s32[16]{0:T(128)} %owner_ref.1, s32[1,128]{1,0:T(1,128)} %bitcast.14, bf16[128,2048]{1,0:T(8,128)(2,1)} %proj_ref.1), custom_call_target="tpu_custom_call" | custom-call | tf_op jit(solution)/shard_map/slot_rows/pallas_call | solution.py:415
  3.0 7.1 %all-to-all-start = ((bf16[32,16,512]{2,1,0:T(8,128)(2,1)}), bf16[32,16,512]{2,1,0:T(8,128)(2,1)S(1)}, u32[]{:S(2)}, u32[]{:S(2)}) async-start(bf16[32,16,512]{2,1,0:T(8,128)(2,1)} %bitcast.12), calls=%async_computation | async-start | bytes 1048576 | tf_op jit(solution)/shard_map/all_to_all | solution.py:426
  10.1 0.6 copy-done.12
  11.0 0.9 %collective-permute-done = f32[1,128]{1,0:T(1,128)S(1)} collective-permute-done((f32[1,128]{1,0:T(1,128)S(1)}, f32[1,128]{1,0:T(1,128)S(1)}, u32[]{:S(2)}, u32[]{:S(2)}) %collective-permute-start) | collective-permute-done | bytes 544 | tf_op jit(solution)/shard_map/ppermute | solution.py:401
  11.8 1.4 %collective-permute-start.1 = (f32[2,128]{1,0:T(2,128)S(1)}, f32[2,128]{1,0:T(2,128)S(1)}, u32[]{:S(2)}, u32[]{:S(2)}) collective-permute-start(f32[2,128]{1,0:T(2,128)S(1)} %pad_maximum_fusion.2), channel_id=1, source_target_pairs={{0,8},{4,12},{8,0},{12,4},{16,24},{20,28},{24,16},{28,20},{1,9},{5... | collective-permute-start | bytes 3080 | tf_op jit(solution)/shard_map/ppermute | solution.py:401
  13.3 5.5 %collective-permute-done.1 = f32[2,128]{1,0:T(2,128)S(1)} collective-permute-done((f32[2,128]{1,0:T(2,128)S(1)}, f32[2,128]{1,0:T(2,128)S(1)}, u32[]{:S(2)}, u32[]{:S(2)}) %collective-permute-start.1) | collective-permute-done | bytes 1056 | tf_op jit(solution)/shard_map/ppermute | solution.py:401
  18.8 4.2 %collective-permute-start.2 = (f32[4,128]{1,0:T(4,128)S(1)}, f32[4,128]{1,0:T(4,128)S(1)}, u32[]{:S(2)}, u32[]{:S(2)}) collective-permute-start(f32[4,128]{1,0:T(4,128)S(1)} %pad_maximum_fusion.1), channel_id=1, source_target_pairs={{0,16},{4,20},{8,24},{12,28},{16,0},{20,4},{24,8},{28,12},{1,17},{... | collective-permute-start | bytes 6152 | tf_op jit(solution)/shard_map/ppermute | solution.py:401
  23.0 1.2 %collective-permute-done.2 = f32[4,128]{1,0:T(4,128)S(1)} collective-permute-done((f32[4,128]{1,0:T(4,128)S(1)}, f32[4,128]{1,0:T(4,128)S(1)}, u32[]{:S(2)}, u32[]{:S(2)}) %collective-permute-start.2) | collective-permute-done | bytes 2080 | tf_op jit(solution)/shard_map/ppermute | solution.py:401
  24.2 1.5 %collective-permute-start.3 = (f32[8,128]{1,0:T(8,128)S(1)}, f32[8,128]{1,0:T(8,128)S(1)}, u32[]{:S(2)}, u32[]{:S(2)}) collective-permute-start(f32[8,128]{1,0:T(8,128)S(1)} %pad_maximum_fusion), channel_id=1, source_target_pairs={{0,1},{1,0},{2,3},{3,2},{4,5},{5,4},{6,7},{7,6},{8,9},{9,8},{10,11... | collective-permute-start | bytes 12296 | tf_op jit(solution)/shard_map/ppermute | solution.py:401
  25.7 0.7 pad_add_fusion.place_ref
  26.4 1.6 %cut_columns.1 = (bf16[128,128]{1,0:T(8,128)(2,1)}, bf16[128,128]{1,0:T(8,128)(2,1)}, bf16[128,128]{1,0:T(8,128)(2,1)}, bf16[128,128]{1,0:T(8,128)(2,1)}) custom-call(s32[2]{0:T(128)} %pad_add_fusion.place_ref, bf16[128,512]{1,0:T(8,128)(2,1)} %grad_ref.1), custom_call_target="tpu_custom_call" | custom-call | tf_op jit(solution)/shard_map/cut_columns/pallas_call | solution.py:427
  28.0 1.5 %collective-permute-start.6 = (bf16[128,128]{1,0:T(8,128)(2,1)}, bf16[128,128]{1,0:T(8,128)(2,1)S(1)}, u32[]{:S(2)}, u32[]{:S(2)}) collective-permute-start(bf16[128,128]{1,0:T(8,128)(2,1)} %get-tuple-element.22), channel_id=1, source_target_pairs={{0,2},{1,3},{2,0},{3,1},{4,6},{5,7},{6,4},{7,5},{8,10},{9,11},{10,... | collective-permute-start | bytes 98312 | tf_op jit(solution)/shard_map/ppermute | solution.py:401
  29.5 1.1 %collective-permute-start.7 = (bf16[128,128]{1,0:T(8,128)(2,1)}, bf16[128,128]{1,0:T(8,128)(2,1)S(1)}, u32[]{:S(2)}, u32[]{:S(2)}) collective-permute-start(bf16[128,128]{1,0:T(8,128)(2,1)} %get-tuple-element.23), channel_id=1, source_target_pairs={{0,3},{1,2},{2,1},{3,0},{4,7},{5,6},{6,5},{7,4},{8,11},{9,10},{10,... | collective-permute-start | bytes 98312 | tf_op jit(solution)/shard_map/ppermute | solution.py:401
  30.6 1.3 %collective-permute-start.4 = (f32[16,128]{1,0:T(8,128)S(1)}, f32[16,128]{1,0:T(8,128)S(1)}, u32[]{:S(2)}, u32[]{:S(2)}) collective-permute-start(f32[16,128]{1,0:T(8,128)S(1)} %concatenate.22), channel_id=1, source_target_pairs={{0,2},{1,3},{2,0},{3,1},{4,6},{5,7},{6,4},{7,5},{8,10},{9,11},{10,... | collective-permute-start | bytes 24584 | tf_op jit(solution)/shard_map/ppermute | solution.py:401
  32.5 1.3 %collective-permute-done.4 = f32[16,128]{1,0:T(8,128)S(1)} collective-permute-done((f32[16,128]{1,0:T(8,128)S(1)}, f32[16,128]{1,0:T(8,128)S(1)}, u32[]{:S(2)}, u32[]{:S(2)}) %collective-permute-start.4) | collective-permute-done | bytes 8224 | tf_op jit(solution)/shard_map/ppermute | solution.py:401
  33.8 1.8 %concatenate.23.users_ref = f32[32,128]{1,0:T(8,128)} concatenate(f32[1,128]{1,0:T(1,128)S(1)} %copy-done.12, f32[1,128]{1,0:T(1,128)S(1)} %collective-permute-done, f32[2,128]{1,0:T(2,128)S(1)} %collective-permute-done.1, f32[4,128]{1,0:T(4,128)S(1)} %collective-permute-done.2, f32[8,128]{1,0:T(8,128)S(1)} %collective-permute-done.3, f32[16,128]{1,0:T(8,128)S(1)} %collective-permute-done.4), dimensions={0} | concatenate | bytes 32768 | tf_op jit(solution)/shard_map/concatenate | solution.py:438
  36.3 1.6 %lay_group.1 = (f32[4,128]{1,0:T(4,128)}, bf16[512,128]{1,0:T(8,128)(2,1)}) custom-call(s32[2]{0:T(128)} %pad_add_fusion.place_ref, f32[32,128]{1,0:T(8,128)} %concatenate.23.users_ref, bf16[128,128]{1,0:T(8,128)(2,1)} %get-tuple-element.20.refs_0_, bf16[128,128]{1,0:T(8,128)(2,1)} %copy-done.6, bf16[128,128]{1,0:T(8,128)(2,1)} %copy-done.7, ...), custom_call_target="tpu_custom_call" | custom-call | tf_op jit(solution)/shard_map/lay_group/pallas_call | solution.py:441
  37.8 0.8 %copy-done.1 = bf16[32,16,512]{2,1,0:T(8,128)(2,1)} copy-done((bf16[32,16,512]{2,1,0:T(8,128)(2,1)}, bf16[32,16,512]{2,1,0:T(8,128)(2,1)S(1)}, u32[]{:S(2)}) %copy-start.1) | copy-done | bytes 524312
  38.6 2.7 %forward.1 = (f32[512,128]{1,0:T(8,128)}, f32[8,512]{1,0:T(8,128)}) custom-call(f32[4,128]{1,0:T(4,128)} %get-tuple-element.24.users_ref, bf16[512,512]{1,0:T(8,128)(2,1)} %bitcast.9, bf16[512,128]{1,0:T(8,128)(2,1)} %get-tuple-element.26.grads_ref, f32[1,128]{1,0:T(1,128)} %dynamic-slice_bitcast_fusion.gain_ref), custom_call_target="tpu_custom_call" | custom-call | tf_op jit(solution)/shard_map/forward/pallas_call | solution.py:451
  41.3 0.7 collective-permute-start.10
  42.2 1.7 %collective-permute-start.8 = (f32[8,512]{1,0:T(8,128)}, f32[8,512]{1,0:T(8,128)S(1)}, u32[]{:S(2)}, u32[]{:S(2)}) collective-permute-start(f32[8,512]{1,0:T(8,128)} %get-tuple-element.28.refs_0_), channel_id=1, source_target_pairs={{0,1},{1,0},{2,3},{3,2},{4,5},{5,4},{6,7},{7,6},{8,9},{9,8},{10,11... | collective-permute-start | bytes 49160 | tf_op jit(solution)/shard_map/ppermute | solution.py:401
  43.9 1.1 %collective-permute-done.10.refs_3_ = f32[8,512]{1,0:T(8,128)S(1)} collective-permute-done((f32[8,512]{1,0:T(8,128)}, f32[8,512]{1,0:T(8,128)S(1)}, u32[]{:S(2)}, u32[]{:S(2)}) %collective-permute-start.10) | collective-permute-done | bytes 16416 | tf_op jit(solution)/shard_map/ppermute | solution.py:401
  45.9 3.7 %backward.1 = (bf16[512,512]{1,0:T(8,128)(2,1)}, bf16[128,128]{1,0:T(8,128)(2,1)}, bf16[128,128]{1,0:T(8,128)(2,1)}, bf16[128,128]{1,0:T(8,128)(2,1)}, bf16[128,128]{1,0:T(8,128)(2,1)}) custom-call(s32[2]{0:T(128)} %pad_add_fusion.place_ref, f32[4,128]{1,0:T(4,128)} %get-tuple-element.24.users_ref, bf16[512,512]{1,0:T(8,128)(2,1)} %bitcast.10, ...), custom_call_target="tpu_custom_call" | custom-call | tf_op jit(solution)/shard_map/backward/pallas_call | solution.py:462
  49.6 9.7 %all-to-all-start.1 = ((bf16[32,16,512]{2,1,0:T(8,128)(2,1)}), bf16[32,16,512]{2,1,0:T(8,128)(2,1)S(1)}, u32[]{:S(2)}, u32[]{:S(2)}) async-start(bf16[32,16,512]{2,1,0:T(8,128)(2,1)} %bitcast.13), calls=%async_computation.1 | async-start | bytes 1048576 | tf_op jit(solution)/shard_map/all_to_all | solution.py:476
  59.3 1.5 %collective-permute-start.11 = (bf16[128,128]{1,0:T(8,128)(2,1)S(1)}, bf16[128,128]{1,0:T(8,128)(2,1)S(1)}, u32[]{:S(2)}, u32[]{:S(2)}) collective-permute-start(bf16[128,128]{1,0:T(8,128)(2,1)S(1)} %copy-done.15), channel_id=1, source_target_pairs={{0,1},{1,0},{2,3},{3,2},{4,5},{5,4},{6,7},{7,6},{8,9},{9,8},{10,11... | collective-permute-start | bytes 98312 | tf_op jit(solution)/shard_map/ppermute | solution.py:401
  60.8 1.2 %collective-permute-start.12 = (bf16[128,128]{1,0:T(8,128)(2,1)S(1)}, bf16[128,128]{1,0:T(8,128)(2,1)S(1)}, u32[]{:S(2)}, u32[]{:S(2)}) collective-permute-start(bf16[128,128]{1,0:T(8,128)(2,1)S(1)} %copy-done.14), channel_id=1, source_target_pairs={{0,2},{1,3},{2,0},{3,1},{4,6},{5,7},{6,4},{7,5},{8,10},{9,11},{10,... | collective-permute-start | bytes 98312 | tf_op jit(solution)/shard_map/ppermute | solution.py:401
  62.0 2.1 %collective-permute-done.11.refs_1_ = bf16[128,128]{1,0:T(8,128)(2,1)S(1)} collective-permute-done((bf16[128,128]{1,0:T(8,128)(2,1)S(1)}, bf16[128,128]{1,0:T(8,128)(2,1)S(1)}, u32[]{:S(2)}, u32[]{:S(2)}) %collective-permute-start.11) | collective-permute-done | bytes 32800 | tf_op jit(solution)/shard_map/ppermute | solution.py:401
  64.2 0.8 collective-permute-done.12.refs_2_
  64.9 1.9 %collective-permute-done.13.refs_3_ = bf16[128,128]{1,0:T(8,128)(2,1)S(1)} collective-permute-done((bf16[128,128]{1,0:T(8,128)(2,1)S(1)}, bf16[128,128]{1,0:T(8,128)(2,1)S(1)}, u32[]{:S(2)}, u32[]{:S(2)}) %collective-permute-start.13) | collective-permute-done | bytes 32800 | tf_op jit(solution)/shard_map/ppermute | solution.py:401
  66.8 8.6 %all-to-all-done.1 = bf16[32,16,512]{2,1,0:T(8,128)(2,1)S(1)} async-done(((bf16[32,16,512]{2,1,0:T(8,128)(2,1)}), bf16[32,16,512]{2,1,0:T(8,128)(2,1)S(1)}, u32[]{:S(2)}, u32[]{:S(2)}) %all-to-all-start.1) | async-done | bytes 524320 | tf_op jit(solution)/shard_map/all_to_all | solution.py:476
  75.4 0.8 copy-done.2
  76.2 2.2 %unslot_rows.1 = (bf16[128,512]{1,0:T(8,128)(2,1)}, bf16[128,2048]{1,0:T(8,128)(2,1)}) custom-call(s32[2]{0:T(128)} %pad_add_fusion.place_ref, s32[1,128]{1,0:T(1,128)} %get-tuple-element.18.slot_ref, bf16[512,512]{1,0:T(8,128)(2,1)} %bitcast.11, bf16[128,128]{1,0:T(8,128)(2,1)} %get-tuple-element.30.refs_0_, bf16[128,128]{1,0:T(8,128)(2,1)} %copy-done.3, ...), custom_call_target="tpu_custom_call" | custom-call | tf_op jit(solution)/shard_map/unslot_rows/pallas_call | solution.py:478
  (45 shorter events, 2.8 us)
Async XLA Ops:
  0.6 31.3 %copy-start = (f32[512]{0:T(512)S(1)}, f32[512]{0:T(512)}, u32[]{:S(2)}) copy-start(f32[512]{0:T(512)} %param.6) | copy-start | bytes 6148
  3.0 34.9 %all-to-all-start = ((bf16[32,16,512]{2,1,0:T(8,128)(2,1)}), bf16[32,16,512]{2,1,0:T(8,128)(2,1)S(1)}, u32[]{:S(2)}, u32[]{:S(2)}) async-start(bf16[32,16,512]{2,1,0:T(8,128)(2,1)} %bitcast.12), calls=%async_computation | async-start | bytes 1048576 | tf_op jit(solution)/shard_map/all_to_all | solution.py:426
  10.1 0.7 copy-start.12
  10.7 1.1 %collective-permute-start = (f32[1,128]{1,0:T(1,128)S(1)}, f32[1,128]{1,0:T(1,128)S(1)}, u32[]{:S(2)}, u32[]{:S(2)}) collective-permute-start(f32[1,128]{1,0:T(1,128)S(1)} %copy-done.12), channel_id=1, source_target_pairs={{0,4},{4,0},{8,12},{12,8},{16,20},{20,16},{24,28},{28,24},{1,5},{5... | collective-permute-start | bytes 1544 | tf_op jit(solution)/shard_map/ppermute | solution.py:401
  11.8 7.0 %collective-permute-start.1 = (f32[2,128]{1,0:T(2,128)S(1)}, f32[2,128]{1,0:T(2,128)S(1)}, u32[]{:S(2)}, u32[]{:S(2)}) collective-permute-start(f32[2,128]{1,0:T(2,128)S(1)} %pad_maximum_fusion.2), channel_id=1, source_target_pairs={{0,8},{4,12},{8,0},{12,4},{16,24},{20,28},{24,16},{28,20},{1,9},{5... | collective-permute-start | bytes 3080 | tf_op jit(solution)/shard_map/ppermute | solution.py:401
  18.8 5.4 %collective-permute-start.2 = (f32[4,128]{1,0:T(4,128)S(1)}, f32[4,128]{1,0:T(4,128)S(1)}, u32[]{:S(2)}, u32[]{:S(2)}) collective-permute-start(f32[4,128]{1,0:T(4,128)S(1)} %pad_maximum_fusion.1), channel_id=1, source_target_pairs={{0,16},{4,20},{8,24},{12,28},{16,0},{20,4},{24,8},{28,12},{1,17},{... | collective-permute-start | bytes 6152 | tf_op jit(solution)/shard_map/ppermute | solution.py:401
  24.2 6.4 %collective-permute-start.3 = (f32[8,128]{1,0:T(8,128)S(1)}, f32[8,128]{1,0:T(8,128)S(1)}, u32[]{:S(2)}, u32[]{:S(2)}) collective-permute-start(f32[8,128]{1,0:T(8,128)S(1)} %pad_maximum_fusion), channel_id=1, source_target_pairs={{0,1},{1,0},{2,3},{3,2},{4,5},{5,4},{6,7},{7,6},{8,9},{9,8},{10,11... | collective-permute-start | bytes 12296 | tf_op jit(solution)/shard_map/ppermute | solution.py:401
  28.0 7.7 %collective-permute-start.5 = (bf16[128,128]{1,0:T(8,128)(2,1)}, bf16[128,128]{1,0:T(8,128)(2,1)S(1)}, u32[]{:S(2)}, u32[]{:S(2)}) collective-permute-start(bf16[128,128]{1,0:T(8,128)(2,1)} %get-tuple-element.21), channel_id=1, source_target_pairs={{0,1},{1,0},{2,3},{3,2},{4,5},{5,4},{6,7},{7,6},{8,9},{9,8},{10,11... | collective-permute-start | bytes 98312 | tf_op jit(solution)/shard_map/ppermute | solution.py:401
  28.0 7.6 %collective-permute-start.6 = (bf16[128,128]{1,0:T(8,128)(2,1)}, bf16[128,128]{1,0:T(8,128)(2,1)S(1)}, u32[]{:S(2)}, u32[]{:S(2)}) collective-permute-start(bf16[128,128]{1,0:T(8,128)(2,1)} %get-tuple-element.22), channel_id=1, source_target_pairs={{0,2},{1,3},{2,0},{3,1},{4,6},{5,7},{6,4},{7,5},{8,10},{9,11},{10,... | collective-permute-start | bytes 98312 | tf_op jit(solution)/shard_map/ppermute | solution.py:401
  29.5 6.1 %collective-permute-start.7 = (bf16[128,128]{1,0:T(8,128)(2,1)}, bf16[128,128]{1,0:T(8,128)(2,1)S(1)}, u32[]{:S(2)}, u32[]{:S(2)}) collective-permute-start(bf16[128,128]{1,0:T(8,128)(2,1)} %get-tuple-element.23), channel_id=1, source_target_pairs={{0,3},{1,2},{2,1},{3,0},{4,7},{5,6},{6,5},{7,4},{8,11},{9,10},{10,... | collective-permute-start | bytes 98312 | tf_op jit(solution)/shard_map/ppermute | solution.py:401
  30.6 3.2 %collective-permute-start.4 = (f32[16,128]{1,0:T(8,128)S(1)}, f32[16,128]{1,0:T(8,128)S(1)}, u32[]{:S(2)}, u32[]{:S(2)}) collective-permute-start(f32[16,128]{1,0:T(8,128)S(1)} %concatenate.22), channel_id=1, source_target_pairs={{0,2},{1,3},{2,0},{3,1},{4,6},{5,7},{6,4},{7,5},{8,10},{9,11},{10,... | collective-permute-start | bytes 24584 | tf_op jit(solution)/shard_map/ppermute | solution.py:401
  35.6 0.6 copy-start.6
  35.6 0.6 copy-start.7
  35.6 0.6 copy-start.8
  37.8 0.8 %copy-start.1 = (bf16[32,16,512]{2,1,0:T(8,128)(2,1)}, bf16[32,16,512]{2,1,0:T(8,128)(2,1)S(1)}, u32[]{:S(2)}) copy-start(bf16[32,16,512]{2,1,0:T(8,128)(2,1)S(1)} %all-to-all-done) | copy-start | bytes 1572868
  41.3 3.7 %collective-permute-start.10 = (f32[8,512]{1,0:T(8,128)}, f32[8,512]{1,0:T(8,128)S(1)}, u32[]{:S(2)}, u32[]{:S(2)}) collective-permute-start(f32[8,512]{1,0:T(8,128)} %get-tuple-element.28.refs_0_), channel_id=1, source_target_pairs={{0,3},{1,2},{2,1},{3,0},{4,7},{5,6},{6,5},{7,4},{8,11},{9,10},{10,... | collective-permute-start | bytes 49160 | tf_op jit(solution)/shard_map/ppermute | solution.py:401
  42.0 3.0 %collective-permute-start.9 = (f32[8,512]{1,0:T(8,128)}, f32[8,512]{1,0:T(8,128)S(1)}, u32[]{:S(2)}, u32[]{:S(2)}) collective-permute-start(f32[8,512]{1,0:T(8,128)} %get-tuple-element.28.refs_0_), channel_id=1, source_target_pairs={{0,2},{1,3},{2,0},{3,1},{4,6},{5,7},{6,4},{7,5},{8,10},{9,11},{10,... | collective-permute-start | bytes 49160 | tf_op jit(solution)/shard_map/ppermute | solution.py:401
  42.2 3.1 %collective-permute-start.8 = (f32[8,512]{1,0:T(8,128)}, f32[8,512]{1,0:T(8,128)S(1)}, u32[]{:S(2)}, u32[]{:S(2)}) collective-permute-start(f32[8,512]{1,0:T(8,128)} %get-tuple-element.28.refs_0_), channel_id=1, source_target_pairs={{0,1},{1,0},{2,3},{3,2},{4,5},{5,4},{6,7},{7,6},{8,9},{9,8},{10,11... | collective-permute-start | bytes 49160 | tf_op jit(solution)/shard_map/ppermute | solution.py:401
  45.0 0.6 copy-start.9
  45.0 0.6 copy-start.10
  45.3 0.6 copy-start.11
  49.6 9.7 %copy-start.15 = (bf16[128,128]{1,0:T(8,128)(2,1)S(1)}, bf16[128,128]{1,0:T(8,128)(2,1)}, u32[]{:S(2)}) copy-start(bf16[128,128]{1,0:T(8,128)(2,1)} %get-tuple-element.31) | copy-start | bytes 98308
  49.6 11.2 %copy-start.14 = (bf16[128,128]{1,0:T(8,128)(2,1)S(1)}, bf16[128,128]{1,0:T(8,128)(2,1)}, u32[]{:S(2)}) copy-start(bf16[128,128]{1,0:T(8,128)(2,1)} %get-tuple-element.32) | copy-start | bytes 98308
  49.6 12.3 %copy-start.13 = (bf16[128,128]{1,0:T(8,128)(2,1)S(1)}, bf16[128,128]{1,0:T(8,128)(2,1)}, u32[]{:S(2)}) copy-start(bf16[128,128]{1,0:T(8,128)(2,1)} %get-tuple-element.33) | copy-start | bytes 98308
  49.6 25.8 %all-to-all-start.1 = ((bf16[32,16,512]{2,1,0:T(8,128)(2,1)}), bf16[32,16,512]{2,1,0:T(8,128)(2,1)S(1)}, u32[]{:S(2)}, u32[]{:S(2)}) async-start(bf16[32,16,512]{2,1,0:T(8,128)(2,1)} %bitcast.13), calls=%async_computation.1 | async-start | bytes 1048576 | tf_op jit(solution)/shard_map/all_to_all | solution.py:476
  59.3 4.9 %collective-permute-start.11 = (bf16[128,128]{1,0:T(8,128)(2,1)S(1)}, bf16[128,128]{1,0:T(8,128)(2,1)S(1)}, u32[]{:S(2)}, u32[]{:S(2)}) collective-permute-start(bf16[128,128]{1,0:T(8,128)(2,1)S(1)} %copy-done.15), channel_id=1, source_target_pairs={{0,1},{1,0},{2,3},{3,2},{4,5},{5,4},{6,7},{7,6},{8,9},{9,8},{10,11... | collective-permute-start | bytes 98312 | tf_op jit(solution)/shard_map/ppermute | solution.py:401
  60.8 4.2 %collective-permute-start.12 = (bf16[128,128]{1,0:T(8,128)(2,1)S(1)}, bf16[128,128]{1,0:T(8,128)(2,1)S(1)}, u32[]{:S(2)}, u32[]{:S(2)}) collective-permute-start(bf16[128,128]{1,0:T(8,128)(2,1)S(1)} %copy-done.14), channel_id=1, source_target_pairs={{0,2},{1,3},{2,0},{3,1},{4,6},{5,7},{6,4},{7,5},{8,10},{9,11},{10,... | collective-permute-start | bytes 98312 | tf_op jit(solution)/shard_map/ppermute | solution.py:401
  61.9 4.9 %collective-permute-start.13 = (bf16[128,128]{1,0:T(8,128)(2,1)S(1)}, bf16[128,128]{1,0:T(8,128)(2,1)S(1)}, u32[]{:S(2)}, u32[]{:S(2)}) collective-permute-start(bf16[128,128]{1,0:T(8,128)(2,1)S(1)} %copy-done.13), channel_id=1, source_target_pairs={{0,3},{1,2},{2,1},{3,0},{4,7},{5,6},{6,5},{7,4},{8,11},{9,10},{10,... | collective-permute-start | bytes 98312 | tf_op jit(solution)/shard_map/ppermute | solution.py:401
  64.2 11.2 %copy-start.3 = (bf16[128,128]{1,0:T(8,128)(2,1)}, bf16[128,128]{1,0:T(8,128)(2,1)S(1)}, u32[]{:S(2)}) copy-start(bf16[128,128]{1,0:T(8,128)(2,1)S(1)} %collective-permute-done.11.refs_1_) | copy-start | bytes 98308
  64.9 10.5 %copy-start.4 = (bf16[128,128]{1,0:T(8,128)(2,1)}, bf16[128,128]{1,0:T(8,128)(2,1)S(1)}, u32[]{:S(2)}) copy-start(bf16[128,128]{1,0:T(8,128)(2,1)S(1)} %collective-permute-done.12.refs_2_) | copy-start | bytes 98308
  66.8 8.6 %copy-start.5 = (bf16[128,128]{1,0:T(8,128)(2,1)}, bf16[128,128]{1,0:T(8,128)(2,1)S(1)}, u32[]{:S(2)}) copy-start(bf16[128,128]{1,0:T(8,128)(2,1)S(1)} %collective-permute-done.13.refs_3_) | copy-start | bytes 98308
  75.4 0.8 %copy-start.2 = (bf16[32,16,512]{2,1,0:T(8,128)(2,1)}, bf16[32,16,512]{2,1,0:T(8,128)(2,1)S(1)}, u32[]{:S(2)}) copy-start(bf16[32,16,512]{2,1,0:T(8,128)(2,1)S(1)} %all-to-all-done.1) | copy-start | bytes 1572868

commit v2 on v1

--- a/solution.py
+++ b/solution.py
@@ -200,6 +200,17 @@
     return (layer_out, grad_read)
 
 
+LIMIT = pltpu.CompilerParams(vmem_limit_bytes=16 * 2**20)
+
+
+def device_of(owner, head):
+    return (owner & ~1) | (head & 1), ((owner & 1) << 1) | (head >> 1)
+
+
+def turned(index):
+    return ((index & 1) << 1) | (index >> 1)
+
+
 def vmem(count):
     return [pl.BlockSpec(memory_space=pltpu.VMEM)] * count
 
@@ -214,63 +225,77 @@
     )
 
 
-def slot_kernel(owner_ref, user_ref, proj_ref, send_ref, users_ref, slot_ref, *, per_pair):
-    slots = user_ref.shape[1]
-    users = user_ref[...]
+def owners_of(users, owner_ref):
     owners = jnp.zeros_like(users)
     for user in range(owner_ref.shape[0]):
         owners = jnp.where(users == user, owner_ref[user], owners)
+    return owners
+
+
+def lower_ones(size):
+    earlier = lax.broadcasted_iota(jnp.int32, (size, size), 0)
+    later = lax.broadcasted_iota(jnp.int32, (size, size), 1)
+    return (earlier <= later).astype(jnp.bfloat16)
+
+
+def slot_kernel(owner_ref, user_ref, proj_ref, send_ref, slot_ref, *, per_pair):
+    slots = user_ref.shape[1]
+    readers = slots // per_pair
+    users = user_ref[...]
+    owners = owners_of(users, owner_ref)
     is_live = users >= 0
-    owner_range = lax.broadcasted_iota(jnp.int32, (slots // per_pair, slots), 0)
-    hits = (owner_range == owners) & is_live
-    earlier = lax.broadcasted_iota(jnp.int32, (slots, slots), 0)
-    later = lax.broadcasted_iota(jnp.int32, (slots, slots), 1)
-    upto = (earlier <= later).astype(jnp.bfloat16)
-    hits_f = hits.astype(jnp.float32)
-    running = dot(hits_f.astype(jnp.bfloat16), upto, 1, 0)
-    ranks = jnp.sum(hits_f * running, axis=0, keepdims=True).astype(jnp.int32) - 1
+    owner_range = lax.broadcasted_iota(jnp.int32, (readers, slots), 0)
+    hits = ((owner_range == owners) & is_live).astype(jnp.float32)
+    running = dot(hits.astype(jnp.bfloat16), lower_ones(slots), 1, 0)
+    ranks = jnp.sum(hits * running, axis=0, keepdims=True).astype(jnp.int32) - 1
     slot = jnp.where(is_live, owners * per_pair + ranks, -1)
     slot_ref[...] = slot
-    placed = (earlier == slot).astype(jnp.bfloat16)
-    tagged = (users + 1).astype(jnp.float32).astype(jnp.bfloat16)
-    tagged = jnp.broadcast_to(tagged, (16, slots))
-    users_ref[...] = dot(tagged, placed, 1, 1)[:1]
+    placed = (lax.broadcasted_iota(jnp.int32, (slots, slots), 0) == slot).astype(jnp.bfloat16)
     for part in range(4):
         width = HEADS * HD
         rows = dot(placed, proj_ref[:, part * width : (part + 1) * width], 1, 0)
         rows = rows.astype(jnp.bfloat16)
-        for head in range(HEADS):
-            send_ref[head * slots : (head + 1) * slots, part * HD : (part + 1) * HD] = rows[
-                :, head * HD : (head + 1) * HD
-            ]
+        for owner in range(readers):
+            for head in range(HEADS):
+                dp_index, ctx_index = device_of(owner, head)
+                start = (ctx_index * readers + dp_index) * per_pair
+                send_ref[start : start + per_pair, part * HD : (part + 1) * HD] = rows[
+                    owner * per_pair : (owner + 1) * per_pair, head * HD : (head + 1) * HD
+                ]
 
 
 def columns_kernel(place_ref, grad_ref, *piece_refs):
-    me = place_ref[0]
+    first = turned(place_ref[3])
     for step, piece_ref in enumerate(piece_refs):
-        start = pl.multiple_of((me ^ step) * HD, HD)
+        start = pl.multiple_of((first ^ step) * HD, HD)
         piece_ref[...] = grad_ref[:, pl.ds(start, HD)]
 
 
-def group_kernel(place_ref, users_ref, *refs, per_pair):
+def group_kernel(place_ref, owner_ref, users_ref, *refs, per_pair):
     piece_refs, (group_users_ref, grads_ref) = refs[:HEADS], refs[HEADS:]
-    me, owner = place_ref[0], place_ref[1]
-    readers = users_ref.shape[0] // HEADS
-    slots = users_ref.shape[1]
-    source = lax.broadcasted_iota(jnp.int32, (slots, slots), 0)
-    target = lax.broadcasted_iota(jnp.int32, (slots, slots), 1)
-    same_rank = lax.rem(source, per_pair) == lax.rem(target, per_pair)
-    spread = (same_rank & (lax.div(source, per_pair) == owner)).astype(jnp.bfloat16)
-    mine = dot(users_ref[...].astype(jnp.bfloat16), spread, 1, 0)
-    distance = lax.broadcasted_iota(jnp.int32, (readers, slots), 0)
-    reader = lax.div(lax.broadcasted_iota(jnp.int32, (readers, slots), 1), per_pair)
-    from_reader = reader == (distance ^ owner)
+    head, owner, my_dp, my_ctx = [place_ref[index] for index in range(4)]
+    count, slots = users_ref.shape
+    readers = count // HEADS
+    users = users_ref[...]
+    hits = (owners_of(users, owner_ref) == owner) & (users >= 0)
+    running = dot(hits.astype(jnp.float32).astype(jnp.bfloat16), lower_ones(slots), 1, 0)
+    ranks = jnp.where(hits, running - 1.0, -1.0)
+    tagged = (users + 1).astype(jnp.float32)
+    lane = lax.broadcasted_iota(jnp.int32, (count, slots), 1)
+    rank_here = lax.rem(lane, per_pair)
+    spread = jnp.zeros((count, slots), jnp.float32)
+    for rank in range(per_pair):
+        user = jnp.sum(jnp.where(ranks == float(rank), tagged, 0.0), axis=1, keepdims=True)
+        spread = jnp.where(rank_here == rank, user, spread)
+    order = lax.rem(lax.broadcasted_iota(jnp.int32, (count, slots), 0), readers)
+    half = readers // 2
+    distance = 2 * lax.rem(order, half) + lax.div(order, half)
+    spread = jnp.where(lax.div(lane, per_pair) == (distance ^ my_dp), spread, 0.0)
     for step in range(HEADS):
-        window = me ^ step
-        rows = mine[step * readers : (step + 1) * readers]
-        group_users_ref[pl.ds(window, 1), :] = (
-            jnp.sum(jnp.where(from_reader, rows, 0.0), axis=0, keepdims=True) - 1.0
-        )
+        group_users_ref[pl.ds(my_ctx ^ step, 1), :] = (
+            jnp.sum(spread[step * readers : (step + 1) * readers], axis=0, keepdims=True) - 1.0
+        )
+        window = turned(head ^ step)
         grads_ref[pl.ds(pl.multiple_of(window * slots, slots), slots), :] = piece_refs[step][...]
 
 
@@ -323,8 +348,8 @@
     stats_refs = refs[:HEADS]
     out_ref = refs[HEADS]
     layer_refs = refs[HEADS + 1 : 2 * HEADS + 1]
-    layer_all, out_grads_all, key_sum, value_sum = refs[2 * HEADS + 1 :]
-    me = place_ref[0]
+    layer_all, key_sum, value_sum = refs[2 * HEADS + 1 :]
+    head = place_ref[0]
     size = users_ref.shape[1]
     windows = users_ref.shape[0]
     scale = HD ** (-0.5)
@@ -373,32 +398,58 @@
     out_ref[:, 2 * HD : 3 * HD] = key_sum[...].astype(jnp.bfloat16)
     out_ref[:, 3 * HD :] = value_sum[...].astype(jnp.bfloat16)
     for step, layer_ref in enumerate(layer_refs):
-        start = pl.multiple_of((me ^ step) * size, size)
+        start = pl.multiple_of(turned(head ^ step) * size, size)
         layer_ref[...] = layer_all[pl.ds(start, size), :]
 
 
-def unslot_kernel(place_ref, slot_ref, returned_ref, *refs):
+def unslot_kernel(place_ref, slot_ref, returned_ref, *refs, per_pair):
     piece_refs, (layer_ref, grad_ref) = refs[:HEADS], refs[HEADS:]
-    me = place_ref[0]
     slots = slot_ref.shape[1]
+    readers = slots // per_pair
     width = HEADS * HD
     placed = (
         lax.broadcasted_iota(jnp.int32, (slots, slots), 0) == slot_ref[...]
     ).astype(jnp.bfloat16)
     for head in range(HEADS):
-        rows = dot(placed, returned_ref[head * slots : (head + 1) * slots], 0, 0)
-        rows = rows.astype(jnp.bfloat16)
+        chunks = []
+        for owner in range(readers):
+            dp_index, ctx_index = device_of(owner, head)
+            start = (ctx_index * readers + dp_index) * per_pair
+            chunks.append(returned_ref[start : start + per_pair])
+        rows = dot(placed, jnp.concatenate(chunks, axis=0), 0, 0).astype(jnp.bfloat16)
         for part in range(4):
             start = part * width + head * HD
             grad_ref[:, start : start + HD] = rows[:, part * HD : (part + 1) * HD]
+    first = turned(place_ref[3])
     for step, piece_ref in enumerate(piece_refs):
-        start = pl.multiple_of((me ^ step) * HD, HD)
+        start = pl.multiple_of((first ^ step) * HD, HD)
         layer_ref[:, pl.ds(start, HD)] = piece_ref[...]
 
 
-def swap(value, axis, distance):
-    pairs = [(index, index ^ distance) for index in range(lax.axis_size(axis))]
-    return lax.ppermute(value, axis, pairs)
+def send(value, target, back=False):
+    width = lax.axis_size("ctx")
+    pairs = []
+    for dp_index in range(lax.axis_size("dp")):
+        for ctx_index in range(width):
+            to_dp, to_ctx = target(dp_index, ctx_index)
+            pair = (dp_index * width + ctx_index, to_dp * width + to_ctx)
+            pairs.append(pair[::-1] if back else pair)
+    return lax.ppermute(value, ("dp", "ctx"), pairs)
+
+
+def swap(value, dp_bits, ctx_bits):
+    return send(value, lambda dp_index, ctx_index: (dp_index ^ dp_bits, ctx_index ^ ctx_bits))
+
+
+def regroup(pieces, back=False):
+    moved = []
+    for step, piece in enumerate(pieces):
+
+        def target(dp_index, ctx_index, step=step):
+            return device_of(dp_index, turned(ctx_index) ^ step)
+
+        moved.append(send(piece, target, back))
+    return moved
 
 
 def by_heads(proj_read, norm_gain, owner_of, user_of, grad_output):
@@ -407,47 +458,52 @@
     per_pair = slots // readers
     group_rows = slots * HEADS
     width = 4 * HD
-    me = lax.axis_index("ctx")
-    place = jnp.stack([me, lax.axis_index("dp")]).astype(jnp.int32)
-    gain = lax.dynamic_slice_in_dim(norm_gain, me * HD, HD, 0).reshape(1, HD)
+    my_dp, my_ctx = lax.axis_index("dp"), lax.axis_index("ctx")
+    head = ((my_ctx & 1) << 1) | (my_dp & 1)
+    owner = (my_dp & ~1) | (my_ctx >> 1)
+    place = jnp.stack([head, owner, my_dp, my_ctx]).astype(jnp.int32)
+    gain = lax.dynamic_slice_in_dim(norm_gain, head * HD, HD, 0).reshape(1, HD)
     rows_shape = jax.ShapeDtypeStruct((group_rows, width), jnp.bfloat16)
     piece_shape = jax.ShapeDtypeStruct((slots, HD), jnp.bfloat16)
-    outgoing, slot_users, slot = pl.pallas_call(
+    user_row = user_of.reshape(1, slots)
+    users = [user_row] + [swap(user_row, bits, 0) for bits in range(2, readers, 2)]
+    users = jnp.concatenate(users, axis=0)
+    outgoing, slot = pl.pallas_call(
         functools.partial(slot_kernel, per_pair=per_pair),
         out_shape=(
             rows_shape,
-            jax.ShapeDtypeStruct((1, slots), jnp.float32),
             jax.ShapeDtypeStruct((1, slots), jnp.int32),
         ),
         in_specs=[smem()] + vmem(2),
-        out_specs=tuple(vmem(3)),
+        out_specs=tuple(vmem(2)),
+        compiler_params=LIMIT,
         name="slot_rows",
-    )(owner_of, user_of.reshape(1, slots), proj_read)
+    )(owner_of, user_row, proj_read)
+    outgoing, users = lax.optimization_barrier((outgoing, users))
     rows = lax.all_to_all(outgoing, ("ctx", "dp"), split_axis=0, concat_axis=0, tiled=True)
+    users = jnp.concatenate([users, swap(users, 1, 0)], axis=0)
+    users = jnp.concatenate(
+        [users] + [swap(users, 0, bits) for bits in range(1, HEADS)], axis=0
+    )
     pieces = pl.pallas_call(
         columns_kernel,
         out_shape=(piece_shape,) * HEADS,
         in_specs=[smem()] + vmem(1),
         out_specs=tuple(vmem(HEADS)),
+        compiler_params=LIMIT,
         name="cut_columns",
     )(place, grad_output)
-    users = slot_users
-    for axis in ("dp", "ctx"):
-        distance = 1
-        while distance < lax.axis_size(axis):
-            users = jnp.concatenate([users, swap(users, axis, distance)], axis=0)
-            distance *= 2
-    pieces = (pieces[0],) + tuple(swap(pieces[step], "ctx", step) for step in range(1, HEADS))
     group_users, grads = pl.pallas_call(
         functools.partial(group_kernel, per_pair=per_pair),
         out_shape=(
             jax.ShapeDtypeStruct((HEADS, slots), jnp.float32),
             jax.ShapeDtypeStruct((group_rows, HD), jnp.bfloat16),
         ),
-        in_specs=[smem()] + vmem(1 + HEADS),
+        in_specs=[smem(), smem()] + vmem(1 + HEADS),
         out_specs=tuple(vmem(2)),
+        compiler_params=LIMIT,
         name="lay_group",
-    )(place, users, *pieces)
+    )(place, owner_of, users, *regroup(pieces))
     attended, stats = pl.pallas_call(
         forward_kernel,
         out_shape=(
@@ -456,9 +512,10 @@
         ),
         in_specs=vmem(4),
         out_specs=tuple(vmem(2)),
+        compiler_params=LIMIT,
         name="forward",
     )(group_users, rows, grads, gain)
-    all_stats = (stats,) + tuple(swap(stats, "ctx", step) for step in range(1, HEADS))
+    all_stats = [stats, swap(stats, 1, 0), swap(stats, 0, 1), swap(stats, 1, 1)]
     results = pl.pallas_call(
         backward_kernel,
         out_shape=(rows_shape,) + (piece_shape,) * HEADS,
@@ -466,25 +523,24 @@
         out_specs=tuple(vmem(1 + HEADS)),
         scratch_shapes=[
             pltpu.VMEM((group_rows, HD), jnp.bfloat16),
-            pltpu.VMEM((group_rows, HD), jnp.bfloat16),
             pltpu.VMEM((group_rows, HD), jnp.float32),
             pltpu.VMEM((group_rows, HD), jnp.float32),
         ],
+        compiler_params=LIMIT,
         name="backward",
     )(place, group_users, rows, grads, gain, attended, *all_stats)
-    grads_owned, layers = results[0], results[1:]
-    returned = lax.all_to_all(grads_owned, ("ctx", "dp"), split_axis=0, concat_axis=0, tiled=True)
-    layers = (layers[0],) + tuple(swap(layers[step], "ctx", step) for step in range(1, HEADS))
+    returned = lax.all_to_all(results[0], ("ctx", "dp"), split_axis=0, concat_axis=0, tiled=True)
     return pl.pallas_call(
-        unslot_kernel,
+        functools.partial(unslot_kernel, per_pair=per_pair),
         out_shape=(
             jax.ShapeDtypeStruct((slots, HEADS * HD), jnp.bfloat16),
             jax.ShapeDtypeStruct((slots, 4 * HEADS * HD), jnp.bfloat16),
         ),
         in_specs=[smem()] + vmem(2 + HEADS),
         out_specs=tuple(vmem(2)),
+        compiler_params=LIMIT,
         name="unslot_rows",
-    )(place, slot, returned, *layers)
+    )(place, slot, returned, *regroup(results[1:], back=True))
 
 
 def solution(mesh):

time: 79.3 us -> 61.9 us (0.78)
  waiting for transfers between devices: 23.7 us -> 17.9 us
  Pallas kernels: 13.9 us -> 8.83 us
  local copies, waits for them, and re-layouts: 5.86 us -> 1.8 us
  starting transfers between devices: 33.4 us -> 31.7 us
    ppermute x14 -> x18, waiting for transfers between devices: 15.1 us -> 9.44 us  [send(): return lax.ppermute(value, ('dp', 'ctx'), pairs)]
    all_to_all x1, starting transfers between devices: 9.68 us -> 4.19 us  [by_heads(): lax.all_to_all(results[0], ('ctx', 'dp'), split_axis=0, concat_axis=0, ti...]
    ppermute x14 -> x18, starting transfers between devices: 16.6 us -> 20.7 us  [send(): return lax.ppermute(value, ('dp', 'ctx'), pairs)]
    concatenate x2 -> x1, local copies, waits for them, and re-layouts: 1.8 us -> 0.02 us  [by_heads(): jnp.concatenate([users] + [swap(users, 0, bits) for bits in range(1, HEAD...]
    unnamed x32 -> x10, local copies, waits for them, and re-layouts: 3.47 us -> 1.71 us
    all_to_all x1, waiting for transfers between devices: 8.6 us -> 6.87 us  [by_heads(): lax.all_to_all(results[0], ('ctx', 'dp'), split_axis=0, concat_axis=0, ti...]
    pallas_call x1, Pallas kernels: 2.68 us -> 1.02 us  [by_heads(): pl.pallas_call(forward_kernel, out_shape=(jax.ShapeDtypeStruct((group_row...]
    all_to_all x1, waiting for transfers between devices: 0.01 us -> 1.58 us  [by_heads(): lax.all_to_all(outgoing, ('ctx', 'dp'), split_axis=0, concat_axis=0, tile...]
  transfers between devices with their start and end apart: 16 -> 20, of which waited for: 10 -> 11; matrix products, arithmetic and copies ran while one was open for 4% -> 0% of each run, Pallas kernels for 4% -> 5%
where the time goes in v2:
time: 61.9 us; the launch traced here: 61.1 us
  starting transfers between devices  31.7 us (51%)
  waiting for transfers between devices  17.9 us (29%)
  Pallas kernels  8.83 us (14%)
  local copies, waits for them, and re-layouts  1.8 us (3%)
  between operations  0.77 us (1%)
    ppermute x18, starting transfers between devices, send(): return lax.ppermute(value, ('dp', 'ctx'), pairs)  20.7 us
    ppermute x18, waiting for transfers between devices, send(): return lax.ppermute(value, ('dp', 'ctx'), pairs)  9.44 us
    all_to_all x1, waiting for transfers between devices, by_heads(): lax.all_to_all(results[0], ('ctx', 'dp'), split_axis=0, concat_axis=0, ti...  6.87 us
    all_to_all x1, starting transfers between devices, by_heads(): lax.all_to_all(outgoing, ('ctx', 'dp'), split_axis=0, concat_axis=0, tile...  6.86 us
    all_to_all x1, starting transfers between devices, by_heads(): lax.all_to_all(results[0], ('ctx', 'dp'), split_axis=0, concat_axis=0, ti...  4.19 us
    pallas_call x1, Pallas kernels, by_heads(): pl.pallas_call(backward_kernel, out_shape=(rows_shape,) + (piece_shape,)...  3 us
    pallas_call x1, Pallas kernels, by_heads(): pl.pallas_call(functools.partial(slot_kernel, per_pair=per_pair), out_sha...  1.76 us
    unnamed x10, local copies, waits for them, and re-layouts  1.71 us
  transfers between devices with their start and end apart: 20, of which 11 were waited for; matrix products, arithmetic and copies ran while one was open for 0% of the time, Pallas kernels for 5%

profile of v2, /device:TPU:1, one launch (start us, length us, event | category | flops | bytes accessed | tf_op | source)
XLA Modules:
  0.0 61.1 jit_solution(15381546610606107230)
XLA Ops:
  0.7 0.6 %copy-done.4 = s32[128]{0:T(128)S(1)} copy-done((s32[128]{0:T(128)S(1)}, s32[128]{0:T(128)}, u32[]{:S(2)}) %copy-start.4) | copy-done | bytes 536
  1.3 4.2 %collective-permute-start.2 = (s32[1,128]{1,0:T(1,128)S(1)}, s32[1,128]{1,0:T(1,128)S(1)}, u32[]{:S(2)}, u32[]{:S(2)}) collective-permute-start(s32[1,128]{1,0:T(1,128)S(1)} %bitcast.14), channel_id=1, source_target_pairs={{0,24},{1,25},{2,26},{3,27},{4,28},{5,29},{6,30},{7,31},{8,16},{9,... | collective-permute-start | bytes 1544 | tf_op jit(solution)/shard_map/ppermute | solution.py:437
  5.5 0.3 collective-permute-start
  5.8 1.0 %copy-done.1 = bf16[128,2048]{1,0:T(8,128)(2,1)S(1)} copy-done((bf16[128,2048]{1,0:T(8,128)(2,1)S(1)}, bf16[128,2048]{1,0:T(8,128)(2,1)}, u32[]{:S(2)}) %copy-start.1) | copy-done | bytes 524312
  6.8 1.8 %slot_rows.1 = (bf16[512,512]{1,0:T(8,128)(2,1)}, s32[1,128]{1,0:T(1,128)S(1)}) custom-call(s32[16]{0:T(128)S(1)} %copy-done.3, s32[1,128]{1,0:T(1,128)S(1)} %bitcast.17, bf16[128,2048]{1,0:T(8,128)(2,1)S(1)} %copy-done.1), custom_call_target="tpu_custom_call" | custom-call | tf_op jit(solution)/shard_map/slot_rows/pallas_call | solution.py:471
  8.8 6.9 %all-to-all-start = ((bf16[32,16,512]{2,1,0:T(8,128)(2,1)}), bf16[32,16,512]{2,1,0:T(8,128)(2,1)S(1)}, u32[]{:S(2)}, u32[]{:S(2)}) async-start(bf16[32,16,512]{2,1,0:T(8,128)(2,1)} %bitcast.5), calls=%async_computation | async-start | bytes 1048576 | tf_op jit(solution)/shard_map/all_to_all | solution.py:483
  15.6 0.3 collective-permute-start.3
  16.0 0.9 %collective-permute-done.3 = s32[4,128]{1,0:T(4,128)S(1)} collective-permute-done((s32[4,128]{1,0:T(4,128)S(1)}, s32[4,128]{1,0:T(4,128)S(1)}, u32[]{:S(2)}, u32[]{:S(2)}) %collective-permute-start.3) | collective-permute-done | bytes 2080 | tf_op jit(solution)/shard_map/ppermute | solution.py:437
  16.9 2.3 %collective-permute-start.6 = (s32[8,128]{1,0:T(8,128)S(1)}, s32[8,128]{1,0:T(8,128)S(1)}, u32[]{:S(2)}, u32[]{:S(2)}) collective-permute-start(s32[8,128]{1,0:T(8,128)S(1)} %pad_add_fusion), channel_id=1, source_target_pairs={{0,3},{1,2},{2,1},{3,0},{4,7},{5,6},{6,5},{7,4},{8,11},{9,10},{10,... | collective-permute-start | bytes 12296 | tf_op jit(solution)/shard_map/ppermute | solution.py:437
  19.6 0.6 cut_columns.1
  20.1 3.9 %collective-permute-start.7 = (bf16[128,128]{1,0:T(8,128)(2,1)S(1)}, bf16[128,128]{1,0:T(8,128)(2,1)S(1)}, u32[]{:S(2)}, u32[]{:S(2)}) collective-permute-start(bf16[128,128]{1,0:T(8,128)(2,1)S(1)} %get-tuple-element.22), channel_id=1, source_target_pairs={{0,0},{1,1},{2,4},{3,5},{4,2},{5,3},{6,6},{7,7},{8,8},{9,9},{10,12... | collective-permute-start | bytes 98312 | tf_op jit(solution)/shard_map/ppermute | solution.py:437
  24.1 1.2 %collective-permute-start.10 = (bf16[128,128]{1,0:T(8,128)(2,1)S(1)}, bf16[128,128]{1,0:T(8,128)(2,1)S(1)}, u32[]{:S(2)}, u32[]{:S(2)}) collective-permute-start(bf16[128,128]{1,0:T(8,128)(2,1)S(1)} %get-tuple-element.25), channel_id=1, source_target_pairs={{0,5},{1,4},{2,1},{3,0},{4,7},{5,6},{6,3},{7,2},{8,13},{9,12},{10,... | collective-permute-start | bytes 98312 | tf_op jit(solution)/shard_map/ppermute | solution.py:437
  25.7 2.6 %collective-permute-done.4 = s32[8,128]{1,0:T(8,128)S(1)} collective-permute-done((s32[8,128]{1,0:T(8,128)S(1)}, s32[8,128]{1,0:T(8,128)S(1)}, u32[]{:S(2)}, u32[]{:S(2)}) %collective-permute-start.4) | collective-permute-done | bytes 4128 | tf_op jit(solution)/shard_map/ppermute | solution.py:437
  28.4 1.0 %collective-permute-done.9.refs_2_ = bf16[128,128]{1,0:T(8,128)(2,1)S(1)} collective-permute-done((bf16[128,128]{1,0:T(8,128)(2,1)S(1)}, bf16[128,128]{1,0:T(8,128)(2,1)S(1)}, u32[]{:S(2)}, u32[]{:S(2)}) %collective-permute-start.9) | collective-permute-done | bytes 32800 | tf_op jit(solution)/shard_map/ppermute | solution.py:437
  29.3 0.8 %lay_group.1 = (f32[4,128]{1,0:T(4,128)S(1)}, bf16[512,128]{1,0:T(8,128)(2,1)S(1)}) custom-call(s32[4]{0:T(128)S(1)} %pad_add_fusion.2.place_ref, s32[16]{0:T(128)S(1)} %copy-done.3, s32[32,128]{1,0:T(8,128)S(1)} %concatenate.12.users_ref, bf16[128,128]{1,0:T(8,128)(2,1)S(1)} %collective-permute-done.7.refs_0_, ...), custom_call_target="tpu_custom_call" | custom-call | tf_op jit(solution)/shard_map/lay_group/pallas_call | solution.py:496
  30.2 1.6 %all-to-all-done = bf16[32,16,512]{2,1,0:T(8,128)(2,1)S(1)} async-done(((bf16[32,16,512]{2,1,0:T(8,128)(2,1)}), bf16[32,16,512]{2,1,0:T(8,128)(2,1)S(1)}, u32[]{:S(2)}, u32[]{:S(2)}) %all-to-all-start) | async-done | bytes 524320 | tf_op jit(solution)/shard_map/all_to_all | solution.py:483
  31.8 1.0 %forward.1 = (f32[512,128]{1,0:T(8,128)S(1)}, f32[8,512]{1,0:T(8,128)S(1)}) custom-call(f32[4,128]{1,0:T(4,128)S(1)} %get-tuple-element.26.users_ref, bf16[512,512]{1,0:T(8,128)(2,1)S(1)} %bitcast.11, bf16[512,128]{1,0:T(8,128)(2,1)S(1)} %get-tuple-element.28.grads_ref, f32[1,128]{1,0:T(1,128)S(1)} %dynamic-slice_bitcast_fusion.gain_ref), custom_call_target="tpu_custom_call" | custom-call | tf_op jit(solution)/shard_map/forward/pallas_call | solution.py:507
  32.8 0.3 collective-permute-start.13
  33.1 1.6 %collective-permute-start.12 = (f32[8,512]{1,0:T(8,128)S(1)}, f32[8,512]{1,0:T(8,128)S(1)}, u32[]{:S(2)}, u32[]{:S(2)}) collective-permute-start(f32[8,512]{1,0:T(8,128)S(1)} %get-tuple-element.30.refs_0_), channel_id=1, source_target_pairs={{0,1},{1,0},{2,3},{3,2},{4,5},{5,4},{6,7},{7,6},{8,9},{9,8},{10,11... | collective-permute-start | bytes 49160 | tf_op jit(solution)/shard_map/ppermute | solution.py:437
  34.7 0.3 collective-permute-start.11
  35.0 1.2 %collective-permute-done.13.refs_3_ = f32[8,512]{1,0:T(8,128)S(1)} collective-permute-done((f32[8,512]{1,0:T(8,128)S(1)}, f32[8,512]{1,0:T(8,128)S(1)}, u32[]{:S(2)}, u32[]{:S(2)}) %collective-permute-start.13) | collective-permute-done | bytes 16416 | tf_op jit(solution)/shard_map/ppermute | solution.py:437
  36.1 3.0 %backward.1 = (bf16[512,512]{1,0:T(8,128)(2,1)}, bf16[128,128]{1,0:T(8,128)(2,1)S(1)}, bf16[128,128]{1,0:T(8,128)(2,1)S(1)}, bf16[128,128]{1,0:T(8,128)(2,1)S(1)}, bf16[128,128]{1,0:T(8,128)(2,1)S(1)}) custom-call(s32[4]{0:T(128)S(1)} %pad_add_fusion.2.place_ref, f32[4,128]{1,0:T(4,128)S(1)} %get-tuple-element.26.users_ref, bf16[512,512]{1,0:T(8,128)(2,1)S(1)} %bitcast.12, ...), custom_call_target="tpu_custom_call" | custom-call | tf_op jit(solution)/shard_map/backward/pallas_call | solution.py:519
  39.1 4.2 %all-to-all-start.1 = ((bf16[32,16,512]{2,1,0:T(8,128)(2,1)}), bf16[32,16,512]{2,1,0:T(8,128)(2,1)S(1)}, u32[]{:S(2)}, u32[]{:S(2)}) async-start(bf16[32,16,512]{2,1,0:T(8,128)(2,1)} %bitcast.8), calls=%async_computation.1 | async-start | bytes 1048576 | tf_op jit(solution)/shard_map/all_to_all | solution.py:532
  43.3 3.5 %collective-permute-start.14 = (bf16[128,128]{1,0:T(8,128)(2,1)S(1)}, bf16[128,128]{1,0:T(8,128)(2,1)S(1)}, u32[]{:S(2)}, u32[]{:S(2)}) collective-permute-start(bf16[128,128]{1,0:T(8,128)(2,1)S(1)} %get-tuple-element.32), channel_id=1, source_target_pairs={{0,0},{1,1},{4,2},{5,3},{2,4},{3,5},{6,6},{7,7},{8,8},{9,9},{12,10... | collective-permute-start | bytes 98312 | tf_op jit(solution)/shard_map/ppermute | solution.py:437
  46.9 1.3 %collective-permute-start.16 = (bf16[128,128]{1,0:T(8,128)(2,1)S(1)}, bf16[128,128]{1,0:T(8,128)(2,1)S(1)}, u32[]{:S(2)}, u32[]{:S(2)}) collective-permute-start(bf16[128,128]{1,0:T(8,128)(2,1)S(1)} %get-tuple-element.34), channel_id=1, source_target_pairs={{1,0},{0,1},{5,2},{4,3},{3,4},{2,5},{7,6},{6,7},{9,8},{8,9},{13,10... | collective-permute-start | bytes 98312 | tf_op jit(solution)/shard_map/ppermute | solution.py:437
  48.2 0.8 %collective-permute-start.17 = (bf16[128,128]{1,0:T(8,128)(2,1)S(1)}, bf16[128,128]{1,0:T(8,128)(2,1)S(1)}, u32[]{:S(2)}, u32[]{:S(2)}) collective-permute-start(bf16[128,128]{1,0:T(8,128)(2,1)S(1)} %get-tuple-element.35), channel_id=1, source_target_pairs={{5,0},{4,1},{1,2},{0,3},{7,4},{6,5},{3,6},{2,7},{13,8},{12,9},{9,1... | collective-permute-start | bytes 98312 | tf_op jit(solution)/shard_map/ppermute | solution.py:437
  49.0 0.3 collective-permute-done.14.refs_0_
  49.4 1.3 %collective-permute-done.15.refs_1_ = bf16[128,128]{1,0:T(8,128)(2,1)S(1)} collective-permute-done((bf16[128,128]{1,0:T(8,128)(2,1)S(1)}, bf16[128,128]{1,0:T(8,128)(2,1)S(1)}, u32[]{:S(2)}, u32[]{:S(2)}) %collective-permute-start.15) | collective-permute-done | bytes 32800 | tf_op jit(solution)/shard_map/ppermute | solution.py:437
  50.7 1.6 %collective-permute-done.16.refs_2_ = bf16[128,128]{1,0:T(8,128)(2,1)S(1)} collective-permute-done((bf16[128,128]{1,0:T(8,128)(2,1)S(1)}, bf16[128,128]{1,0:T(8,128)(2,1)S(1)}, u32[]{:S(2)}, u32[]{:S(2)}) %collective-permute-start.16) | collective-permute-done | bytes 32800 | tf_op jit(solution)/shard_map/ppermute | solution.py:437
  52.2 0.4 collective-permute-done.17.refs_3_
  52.6 6.9 %all-to-all-done.1 = bf16[32,16,512]{2,1,0:T(8,128)(2,1)S(1)} async-done(((bf16[32,16,512]{2,1,0:T(8,128)(2,1)}), bf16[32,16,512]{2,1,0:T(8,128)(2,1)S(1)}, u32[]{:S(2)}, u32[]{:S(2)}) %all-to-all-start.1) | async-done | bytes 524320 | tf_op jit(solution)/shard_map/all_to_all | solution.py:532
  59.4 1.7 %unslot_rows.1 = (bf16[128,512]{1,0:T(8,128)(2,1)}, bf16[128,2048]{1,0:T(8,128)(2,1)}) custom-call(s32[4]{0:T(128)S(1)} %pad_add_fusion.2.place_ref, s32[1,128]{1,0:T(1,128)S(1)} %get-tuple-element.19.slot_ref, bf16[512,512]{1,0:T(8,128)(2,1)S(1)} %bitcast.13, bf16[128,128]{1,0:T(8,128)(2,1)S(1)} %collective-permute-done.14.refs_0_, ...), custom_call_target="tpu_custom_call" | custom-call | tf_op jit(solution)/shard_map/unslot_rows/pallas_call | solution.py:533
  (29 shorter events, 1.1 us)
Async XLA Ops:
  0.6 25.0 %copy-start = (f32[512]{0:T(512)S(1)}, f32[512]{0:T(512)}, u32[]{:S(2)}) copy-start(f32[512]{0:T(512)} %param.6) | copy-start | bytes 6148
  0.6 0.7 %copy-start.4 = (s32[128]{0:T(128)S(1)}, s32[128]{0:T(128)}, u32[]{:S(2)}) copy-start(s32[128]{0:T(128)} %param.8) | copy-start | bytes 1540
  0.7 5.1 %copy-start.3 = (s32[16]{0:T(128)S(1)}, s32[16]{0:T(128)}, u32[]{:S(2)}) copy-start(s32[16]{0:T(128)} %owner_ref.3) | copy-start | bytes 196
  1.3 7.2 %collective-permute-start.2 = (s32[1,128]{1,0:T(1,128)S(1)}, s32[1,128]{1,0:T(1,128)S(1)}, u32[]{:S(2)}, u32[]{:S(2)}) collective-permute-start(s32[1,128]{1,0:T(1,128)S(1)} %bitcast.14), channel_id=1, source_target_pairs={{0,24},{1,25},{2,26},{3,27},{4,28},{5,29},{6,30},{7,31},{8,16},{9,... | collective-permute-start | bytes 1544 | tf_op jit(solution)/shard_map/ppermute | solution.py:437
  5.5 3.3 %collective-permute-start.1 = (s32[1,128]{1,0:T(1,128)S(1)}, s32[1,128]{1,0:T(1,128)S(1)}, u32[]{:S(2)}, u32[]{:S(2)}) collective-permute-start(s32[1,128]{1,0:T(1,128)S(1)} %bitcast.15), channel_id=1, source_target_pairs={{0,16},{1,17},{2,18},{3,19},{4,20},{5,21},{6,22},{7,23},{8,24},{9,... | collective-permute-start | bytes 1544 | tf_op jit(solution)/shard_map/ppermute | solution.py:437
  5.5 3.3 %collective-permute-start = (s32[1,128]{1,0:T(1,128)S(1)}, s32[1,128]{1,0:T(1,128)S(1)}, u32[]{:S(2)}, u32[]{:S(2)}) collective-permute-start(s32[1,128]{1,0:T(1,128)S(1)} %bitcast.16), channel_id=1, source_target_pairs={{0,8},{1,9},{2,10},{3,11},{4,12},{5,13},{6,14},{7,15},{8,0},{9,1},... | collective-permute-start | bytes 1544 | tf_op jit(solution)/shard_map/ppermute | solution.py:437
  5.7 1.0 %copy-start.1 = (bf16[128,2048]{1,0:T(8,128)(2,1)S(1)}, bf16[128,2048]{1,0:T(8,128)(2,1)}, u32[]{:S(2)}) copy-start(bf16[128,2048]{1,0:T(8,128)(2,1)} %proj_ref.1) | copy-start | bytes 1572868
  8.8 10.8 %copy-start.2 = (bf16[128,512]{1,0:T(8,128)(2,1)S(1)}, bf16[128,512]{1,0:T(8,128)(2,1)}, u32[]{:S(2)}) copy-start(bf16[128,512]{1,0:T(8,128)(2,1)} %grad_ref.1) | copy-start | bytes 393220
  8.8 23.0 %all-to-all-start = ((bf16[32,16,512]{2,1,0:T(8,128)(2,1)}), bf16[32,16,512]{2,1,0:T(8,128)(2,1)S(1)}, u32[]{:S(2)}, u32[]{:S(2)}) async-start(bf16[32,16,512]{2,1,0:T(8,128)(2,1)} %bitcast.5), calls=%async_computation | async-start | bytes 1048576 | tf_op jit(solution)/shard_map/all_to_all | solution.py:483
  15.6 1.2 %collective-permute-start.3 = (s32[4,128]{1,0:T(4,128)S(1)}, s32[4,128]{1,0:T(4,128)S(1)}, u32[]{:S(2)}, u32[]{:S(2)}) collective-permute-start(s32[4,128]{1,0:T(4,128)S(1)} %pad_add_fusion.1), channel_id=1, source_target_pairs={{0,4},{1,5},{2,6},{3,7},{4,0},{5,1},{6,2},{7,3},{8,12},{9,13},{10,... | collective-permute-start | bytes 6152 | tf_op jit(solution)/shard_map/ppermute | solution.py:437
  16.9 7.3 %collective-permute-start.6 = (s32[8,128]{1,0:T(8,128)S(1)}, s32[8,128]{1,0:T(8,128)S(1)}, u32[]{:S(2)}, u32[]{:S(2)}) collective-permute-start(s32[8,128]{1,0:T(8,128)S(1)} %pad_add_fusion), channel_id=1, source_target_pairs={{0,3},{1,2},{2,1},{3,0},{4,7},{5,6},{6,5},{7,4},{8,11},{9,10},{10,... | collective-permute-start | bytes 12296 | tf_op jit(solution)/shard_map/ppermute | solution.py:437
  19.2 6.2 %collective-permute-start.5 = (s32[8,128]{1,0:T(8,128)S(1)}, s32[8,128]{1,0:T(8,128)S(1)}, u32[]{:S(2)}, u32[]{:S(2)}) collective-permute-start(s32[8,128]{1,0:T(8,128)S(1)} %pad_add_fusion), channel_id=1, source_target_pairs={{0,2},{1,3},{2,0},{3,1},{4,6},{5,7},{6,4},{7,5},{8,10},{9,11},{10,... | collective-permute-start | bytes 12296 | tf_op jit(solution)/shard_map/ppermute | solution.py:437
  20.1 8.2 %collective-permute-start.7 = (bf16[128,128]{1,0:T(8,128)(2,1)S(1)}, bf16[128,128]{1,0:T(8,128)(2,1)S(1)}, u32[]{:S(2)}, u32[]{:S(2)}) collective-permute-start(bf16[128,128]{1,0:T(8,128)(2,1)S(1)} %get-tuple-element.22), channel_id=1, source_target_pairs={{0,0},{1,1},{2,4},{3,5},{4,2},{5,3},{6,6},{7,7},{8,8},{9,9},{10,12... | collective-permute-start | bytes 98312 | tf_op jit(solution)/shard_map/ppermute | solution.py:437
  24.0 4.4 %collective-permute-start.8 = (bf16[128,128]{1,0:T(8,128)(2,1)S(1)}, bf16[128,128]{1,0:T(8,128)(2,1)S(1)}, u32[]{:S(2)}, u32[]{:S(2)}) collective-permute-start(bf16[128,128]{1,0:T(8,128)(2,1)S(1)} %get-tuple-element.23), channel_id=1, source_target_pairs={{0,4},{1,5},{2,0},{3,1},{4,6},{5,7},{6,2},{7,3},{8,12},{9,13},{10,... | collective-permute-start | bytes 98312 | tf_op jit(solution)/shard_map/ppermute | solution.py:437
  24.0 5.3 %collective-permute-start.9 = (bf16[128,128]{1,0:T(8,128)(2,1)S(1)}, bf16[128,128]{1,0:T(8,128)(2,1)S(1)}, u32[]{:S(2)}, u32[]{:S(2)}) collective-permute-start(bf16[128,128]{1,0:T(8,128)(2,1)S(1)} %get-tuple-element.24), channel_id=1, source_target_pairs={{0,1},{1,0},{2,5},{3,4},{4,3},{5,2},{6,7},{7,6},{8,9},{9,8},{10,13... | collective-permute-start | bytes 98312 | tf_op jit(solution)/shard_map/ppermute | solution.py:437
  24.1 5.2 %collective-permute-start.10 = (bf16[128,128]{1,0:T(8,128)(2,1)S(1)}, bf16[128,128]{1,0:T(8,128)(2,1)S(1)}, u32[]{:S(2)}, u32[]{:S(2)}) collective-permute-start(bf16[128,128]{1,0:T(8,128)(2,1)S(1)} %get-tuple-element.25), channel_id=1, source_target_pairs={{0,5},{1,4},{2,1},{3,0},{4,7},{5,6},{6,3},{7,2},{8,13},{9,12},{10,... | collective-permute-start | bytes 98312 | tf_op jit(solution)/shard_map/ppermute | solution.py:437
  25.3 3.0 %collective-permute-start.4 = (s32[8,128]{1,0:T(8,128)S(1)}, s32[8,128]{1,0:T(8,128)S(1)}, u32[]{:S(2)}, u32[]{:S(2)}) collective-permute-start(s32[8,128]{1,0:T(8,128)S(1)} %pad_add_fusion), channel_id=1, source_target_pairs={{0,1},{1,0},{2,3},{3,2},{4,5},{5,4},{6,7},{7,6},{8,9},{9,8},{10,11... | collective-permute-start | bytes 12296 | tf_op jit(solution)/shard_map/ppermute | solution.py:437
  32.8 3.4 %collective-permute-start.13 = (f32[8,512]{1,0:T(8,128)S(1)}, f32[8,512]{1,0:T(8,128)S(1)}, u32[]{:S(2)}, u32[]{:S(2)}) collective-permute-start(f32[8,512]{1,0:T(8,128)S(1)} %get-tuple-element.30.refs_0_), channel_id=1, source_target_pairs={{0,5},{1,4},{2,7},{3,6},{4,1},{5,0},{6,3},{7,2},{8,13},{9,12},{10,... | collective-permute-start | bytes 49160 | tf_op jit(solution)/shard_map/ppermute | solution.py:437
  33.1 3.1 %collective-permute-start.12 = (f32[8,512]{1,0:T(8,128)S(1)}, f32[8,512]{1,0:T(8,128)S(1)}, u32[]{:S(2)}, u32[]{:S(2)}) collective-permute-start(f32[8,512]{1,0:T(8,128)S(1)} %get-tuple-element.30.refs_0_), channel_id=1, source_target_pairs={{0,1},{1,0},{2,3},{3,2},{4,5},{5,4},{6,7},{7,6},{8,9},{9,8},{10,11... | collective-permute-start | bytes 49160 | tf_op jit(solution)/shard_map/ppermute | solution.py:437
  34.7 1.5 %collective-permute-start.11 = (f32[8,512]{1,0:T(8,128)S(1)}, f32[8,512]{1,0:T(8,128)S(1)}, u32[]{:S(2)}, u32[]{:S(2)}) collective-permute-start(f32[8,512]{1,0:T(8,128)S(1)} %get-tuple-element.30.refs_0_), channel_id=1, source_target_pairs={{0,4},{1,5},{2,6},{3,7},{4,0},{5,1},{6,2},{7,3},{8,12},{9,13},{10,... | collective-permute-start | bytes 49160 | tf_op jit(solution)/shard_map/ppermute | solution.py:437
  39.1 20.3 %all-to-all-start.1 = ((bf16[32,16,512]{2,1,0:T(8,128)(2,1)}), bf16[32,16,512]{2,1,0:T(8,128)(2,1)S(1)}, u32[]{:S(2)}, u32[]{:S(2)}) async-start(bf16[32,16,512]{2,1,0:T(8,128)(2,1)} %bitcast.8), calls=%async_computation.1 | async-start | bytes 1048576 | tf_op jit(solution)/shard_map/all_to_all | solution.py:532
  43.3 6.0 %collective-permute-start.14 = (bf16[128,128]{1,0:T(8,128)(2,1)S(1)}, bf16[128,128]{1,0:T(8,128)(2,1)S(1)}, u32[]{:S(2)}, u32[]{:S(2)}) collective-permute-start(bf16[128,128]{1,0:T(8,128)(2,1)S(1)} %get-tuple-element.32), channel_id=1, source_target_pairs={{0,0},{1,1},{4,2},{5,3},{2,4},{3,5},{6,6},{7,7},{8,8},{9,9},{12,10... | collective-permute-start | bytes 98312 | tf_op jit(solution)/shard_map/ppermute | solution.py:437
  46.9 3.8 %collective-permute-start.15 = (bf16[128,128]{1,0:T(8,128)(2,1)S(1)}, bf16[128,128]{1,0:T(8,128)(2,1)S(1)}, u32[]{:S(2)}, u32[]{:S(2)}) collective-permute-start(bf16[128,128]{1,0:T(8,128)(2,1)S(1)} %get-tuple-element.33), channel_id=1, source_target_pairs={{4,0},{5,1},{0,2},{1,3},{6,4},{7,5},{2,6},{3,7},{12,8},{13,9},{8,1... | collective-permute-start | bytes 98312 | tf_op jit(solution)/shard_map/ppermute | solution.py:437
  46.9 5.3 %collective-permute-start.16 = (bf16[128,128]{1,0:T(8,128)(2,1)S(1)}, bf16[128,128]{1,0:T(8,128)(2,1)S(1)}, u32[]{:S(2)}, u32[]{:S(2)}) collective-permute-start(bf16[128,128]{1,0:T(8,128)(2,1)S(1)} %get-tuple-element.34), channel_id=1, source_target_pairs={{1,0},{0,1},{5,2},{4,3},{3,4},{2,5},{7,6},{6,7},{9,8},{8,9},{13,10... | collective-permute-start | bytes 98312 | tf_op jit(solution)/shard_map/ppermute | solution.py:437
  48.2 4.4 %collective-permute-start.17 = (bf16[128,128]{1,0:T(8,128)(2,1)S(1)}, bf16[128,128]{1,0:T(8,128)(2,1)S(1)}, u32[]{:S(2)}, u32[]{:S(2)}) collective-permute-start(bf16[128,128]{1,0:T(8,128)(2,1)S(1)} %get-tuple-element.35), channel_id=1, source_target_pairs={{5,0},{4,1},{1,2},{0,3},{7,4},{6,5},{3,6},{2,7},{13,8},{12,9},{9,1... | collective-permute-start | bytes 98312 | tf_op jit(solution)/shard_map/ppermute | solution.py:437

commit v3 on v2

--- a/solution.py
+++ b/solution.py
@@ -215,8 +215,8 @@
     return [pl.BlockSpec(memory_space=pltpu.VMEM)] * count
 
 
-def smem():
-    return pl.BlockSpec(memory_space=pltpu.SMEM)
+def hbm(count):
+    return [pl.BlockSpec(memory_space=pltpu.HBM)] * count
 
 
 def dot(left, right, left_dim, right_dim):
@@ -238,73 +238,135 @@
     return (earlier <= later).astype(jnp.bfloat16)
 
 
-def slot_kernel(owner_ref, user_ref, proj_ref, send_ref, slot_ref, *, per_pair):
+def my_place():
+    my_dp, my_ctx = lax.axis_index("dp"), lax.axis_index("ctx")
+    return ((my_ctx & 1) << 1) | (my_dp & 1), (my_dp & ~1) | (my_ctx >> 1), my_dp, my_ctx
+
+
+def slot_kernel(
+    owner_hbm,
+    user_hbm,
+    proj_hbm,
+    send_hbm,
+    slot_hbm,
+    owner_ref,
+    user_ref,
+    slot_ref,
+    proj_ref,
+    send_ref,
+    load_sems,
+    store_sems,
+    *,
+    per_pair,
+):
     slots = user_ref.shape[1]
     readers = slots // per_pair
+    width = HEADS * HD
+    loads = [
+        pltpu.make_async_copy(source, target, load_sems.at[index])
+        for index, (source, target) in enumerate(
+            ((user_hbm, user_ref), (owner_hbm, owner_ref), (proj_hbm, proj_ref))
+        )
+    ]
+    for copy in loads:
+        copy.start()
+    my_dp = lax.axis_index("dp")
+    source = lax.broadcasted_iota(jnp.int32, (slots, slots), 0)
+    target = lax.broadcasted_iota(jnp.int32, (slots, slots), 1)
+    owner_range = lax.broadcasted_iota(jnp.int32, (readers, slots), 0)
+    by_owner = lax.div(lax.broadcasted_iota(jnp.int32, (readers, slots), 1), per_pair)
+    to_lane = (lax.div(target, per_pair) == my_dp) & (
+        lax.rem(target, per_pair) == lax.rem(source, per_pair)
+    )
+    loads[0].wait()
+    loads[1].wait()
     users = user_ref[...]
     owners = owners_of(users, owner_ref)
     is_live = users >= 0
-    owner_range = lax.broadcasted_iota(jnp.int32, (readers, slots), 0)
     hits = ((owner_range == owners) & is_live).astype(jnp.float32)
     running = dot(hits.astype(jnp.bfloat16), lower_ones(slots), 1, 0)
     ranks = jnp.sum(hits * running, axis=0, keepdims=True).astype(jnp.int32) - 1
     slot = jnp.where(is_live, owners * per_pair + ranks, -1)
     slot_ref[...] = slot
-    placed = (lax.broadcasted_iota(jnp.int32, (slots, slots), 0) == slot).astype(jnp.bfloat16)
-    for part in range(4):
-        width = HEADS * HD
-        rows = dot(placed, proj_ref[:, part * width : (part + 1) * width], 1, 0)
-        rows = rows.astype(jnp.bfloat16)
-        for owner in range(readers):
-            for head in range(HEADS):
-                dp_index, ctx_index = device_of(owner, head)
-                start = (ctx_index * readers + dp_index) * per_pair
-                send_ref[start : start + per_pair, part * HD : (part + 1) * HD] = rows[
-                    owner * per_pair : (owner + 1) * per_pair, head * HD : (head + 1) * HD
-                ]
-
-
-def columns_kernel(place_ref, grad_ref, *piece_refs):
-    first = turned(place_ref[3])
+    stores = [pltpu.make_async_copy(slot_ref, slot_hbm, store_sems.at[HEADS])]
+    stores[0].start()
+    placed = (source == slot).astype(jnp.bfloat16)
+    tagged = jnp.broadcast_to((users + 1).astype(jnp.float32), (readers, slots))
+    tagged = dot(tagged.astype(jnp.bfloat16), placed, 1, 1)
+    tagged = jnp.where(by_owner == owner_range, tagged, 0.0).astype(jnp.bfloat16)
+    tagged = dot(tagged, to_lane.astype(jnp.bfloat16), 1, 0).astype(jnp.bfloat16)
+    extra = send_ref.shape[1] - 4 * per_pair
+    for owner in range(readers):
+        for head in range(HEADS):
+            dp_index, ctx_index = device_of(owner, head)
+            send_ref[ctx_index * readers + dp_index, 4 * per_pair :, :] = jnp.broadcast_to(
+                tagged[owner : owner + 1], (extra, slots)
+            )
+    loads[2].wait()
+    for half in range(2):
+        for part in range(4):
+            start = part * width + half * 2 * HD
+            rows = dot(placed, proj_ref[:, start : start + 2 * HD], 1, 0).astype(jnp.bfloat16)
+            for owner in range(readers):
+                for side in range(2):
+                    dp_index, ctx_index = device_of(owner, 2 * half + side)
+                    chunk = ctx_index * readers + dp_index
+                    send_ref[chunk, part * per_pair : (part + 1) * per_pair, :] = rows[
+                        owner * per_pair : (owner + 1) * per_pair, side * HD : (side + 1) * HD
+                    ]
+        for ctx_index in (half, 2 + half):
+            span = pl.ds(ctx_index * readers, readers)
+            stores.append(
+                pltpu.make_async_copy(
+                    send_ref.at[span], send_hbm.at[span], store_sems.at[ctx_index]
+                )
+            )
+            stores[-1].start()
+    for copy in stores:
+        copy.wait()
+
+
+def columns_kernel(slot_ref, grad_ref, *refs):
+    piece_refs, back_ref = refs[:HEADS], refs[HEADS]
+    slots = slot_ref.shape[1]
+    slot = jnp.broadcast_to(slot_ref[...].astype(jnp.float32), (slots, slots)).T
+    lane = lax.broadcasted_iota(jnp.int32, (slots, slots), 1).astype(jnp.float32)
+    back_ref[...] = (slot == lane).astype(jnp.bfloat16)
+    first = turned(lax.axis_index("ctx"))
     for step, piece_ref in enumerate(piece_refs):
         start = pl.multiple_of((first ^ step) * HD, HD)
         piece_ref[...] = grad_ref[:, pl.ds(start, HD)]
 
 
-def group_kernel(place_ref, owner_ref, users_ref, *refs, per_pair):
-    piece_refs, (group_users_ref, grads_ref) = refs[:HEADS], refs[HEADS:]
-    head, owner, my_dp, my_ctx = [place_ref[index] for index in range(4)]
-    count, slots = users_ref.shape
-    readers = count // HEADS
-    users = users_ref[...]
-    hits = (owners_of(users, owner_ref) == owner) & (users >= 0)
-    running = dot(hits.astype(jnp.float32).astype(jnp.bfloat16), lower_ones(slots), 1, 0)
-    ranks = jnp.where(hits, running - 1.0, -1.0)
-    tagged = (users + 1).astype(jnp.float32)
-    lane = lax.broadcasted_iota(jnp.int32, (count, slots), 1)
-    rank_here = lax.rem(lane, per_pair)
-    spread = jnp.zeros((count, slots), jnp.float32)
-    for rank in range(per_pair):
-        user = jnp.sum(jnp.where(ranks == float(rank), tagged, 0.0), axis=1, keepdims=True)
-        spread = jnp.where(rank_here == rank, user, spread)
-    order = lax.rem(lax.broadcasted_iota(jnp.int32, (count, slots), 0), readers)
-    half = readers // 2
-    distance = 2 * lax.rem(order, half) + lax.div(order, half)
-    spread = jnp.where(lax.div(lane, per_pair) == (distance ^ my_dp), spread, 0.0)
-    for step in range(HEADS):
-        group_users_ref[pl.ds(my_ctx ^ step, 1), :] = (
-            jnp.sum(spread[step * readers : (step + 1) * readers], axis=0, keepdims=True) - 1.0
-        )
-        window = turned(head ^ step)
-        grads_ref[pl.ds(pl.multiple_of(window * slots, slots), slots), :] = piece_refs[step][...]
-
-
-def visible_block(users_ref, query_window, key_windows):
-    size = users_ref.shape[1]
-    query_users = jnp.broadcast_to(users_ref[query_window : query_window + 1], (size, size)).T
+def group_kernel(*refs):
+    piece_refs, grads_ref = refs[:HEADS], refs[HEADS]
+    head = my_place()[0]
+    for step, piece_ref in enumerate(piece_refs):
+        slots = piece_ref.shape[0]
+        start = pl.multiple_of(turned(head ^ step) * slots, slots)
+        grads_ref[pl.ds(start, slots), :] = piece_ref[...]
+
+
+def part_rows(rows_ref, part, first, last):
+    per_pair = HD // (rows_ref.shape[0] // HEADS)
+    readers = rows_ref.shape[0] // HEADS
+    rows = rows_ref[first * readers : last * readers, part * per_pair : (part + 1) * per_pair, :]
+    return rows.reshape((last - first) * readers * per_pair, HD)
+
+
+def window_users(rows_ref, window):
+    readers = rows_ref.shape[0] // HEADS
+    per_pair = HD // readers
+    tags = rows_ref[window * readers : (window + 1) * readers, 4 * per_pair :, :]
+    return jnp.sum(tags.astype(jnp.float32), axis=0)[:1]
+
+
+def visible_block(users, query_window):
+    size = users[0].shape[1]
+    query_users = jnp.broadcast_to(users[query_window], (size, size)).T
     blocks = []
-    for window in range(key_windows):
-        block = (query_users == users_ref[window : window + 1]) & (query_users >= 0.0)
+    for window in range(query_window + 1):
+        block = (query_users == users[window]) & (query_users > 0.0)
         if window == query_window:
             rows = lax.broadcasted_iota(jnp.int32, (size, size), 0)
             columns = lax.broadcasted_iota(jnp.int32, (size, size), 1)
@@ -313,23 +375,23 @@
     return jnp.concatenate(blocks, axis=1)
 
 
-def forward_kernel(users_ref, rows_ref, grads_ref, gain_ref, attended_ref, stats_ref):
-    size = users_ref.shape[1]
+def forward_kernel(rows_ref, grads_ref, gain_ref, attended_ref, stats_ref):
+    size = HD
     scale = HD ** (-0.5)
     lane = lax.broadcasted_iota(jnp.int32, (size, HD), 1)
-    for window in range(users_ref.shape[0]):
+    users = [window_users(rows_ref, window) for window in range(HEADS)]
+    for window in range(HEADS):
         here = slice(window * size, (window + 1) * size)
-        upto = slice(0, (window + 1) * size)
-        queries = rows_ref[here, HD : 2 * HD]
-        scores = dot(queries, rows_ref[upto, 2 * HD : 3 * HD], 1, 1) * scale
-        visible = visible_block(users_ref, window, window + 1)
+        queries = part_rows(rows_ref, 1, window, window + 1)
+        scores = dot(queries, part_rows(rows_ref, 2, 0, window + 1), 1, 1) * scale
+        visible = visible_block(users, window)
         weights = jnp.where(visible, scores * jax.nn.sigmoid(scores), 0.0).astype(jnp.bfloat16)
-        attended = dot(weights, rows_ref[upto, 3 * HD :], 1, 0)
+        attended = dot(weights, part_rows(rows_ref, 3, 0, window + 1), 1, 0)
         attended_ref[here] = attended
         grad_normed = (
             grads_ref[here].astype(jnp.float32)
             * gain_ref[...]
-            * rows_ref[here, :HD].astype(jnp.float32)
+            * part_rows(rows_ref, 0, window, window + 1).astype(jnp.float32)
         )
         mean = jnp.mean(attended, axis=1, keepdims=True)
         centered = attended - mean
@@ -342,17 +404,43 @@
         stats_ref[:, here] = packed.T[:8]
 
 
+def slope_kernel(rows_ref, slopes_ref, turned_slopes_ref, turned_weights_ref):
+    size = HD
+    scale = HD ** (-0.5)
+    users = [window_users(rows_ref, window) for window in range(HEADS)]
+    for window in range(HEADS):
+        here = slice(window * size, (window + 1) * size)
+        upto = slice(0, (window + 1) * size)
+        queries = part_rows(rows_ref, 1, window, window + 1)
+        scores = dot(queries, part_rows(rows_ref, 2, 0, window + 1), 1, 1) * scale
+        sigmoid = jax.nn.sigmoid(scores)
+        slopes = sigmoid * (1.0 + scores * (1.0 - sigmoid)) * scale
+        visible = visible_block(users, window)
+        slopes = jnp.where(visible, slopes, 0.0)
+        weights = jnp.where(visible, scores * sigmoid, 0.0)
+        slopes_ref[here, upto] = slopes
+        for key_window in range(window + 1):
+            there = slice(key_window * size, (key_window + 1) * size)
+            turned_slopes_ref[there, here] = slopes[:, there].T
+            turned_weights_ref[there, here] = weights[:, there].T.astype(jnp.bfloat16)
+
+
 def backward_kernel(
-    place_ref, users_ref, rows_ref, grads_ref, gain_ref, attended_ref, *refs
+    rows_ref,
+    grads_ref,
+    gain_ref,
+    attended_ref,
+    slopes_ref,
+    turned_slopes_ref,
+    turned_weights_ref,
+    *refs,
 ):
     stats_refs = refs[:HEADS]
-    out_ref = refs[HEADS]
+    out_hbm = refs[HEADS]
     layer_refs = refs[HEADS + 1 : 2 * HEADS + 1]
-    layer_all, key_sum, value_sum = refs[2 * HEADS + 1 :]
-    head = place_ref[0]
-    size = users_ref.shape[1]
-    windows = users_ref.shape[0]
-    scale = HD ** (-0.5)
+    layer_all, out_ref, out_grads, store_sems = refs[2 * HEADS + 1 :]
+    head = my_place()[0]
+    size = HD
     width = float(HEADS * HD)
     stats = [stat_ref[...] for stat_ref in stats_refs]
     mean = sum(stat[0:1] for stat in stats) * (1.0 / HEADS)
@@ -361,12 +449,9 @@
     mean_grad = sum(stat[2:3] for stat in stats) / width
     cross = sum(stat[3:4] + (stat[0:1] - mean) * stat[2:3] for stat in stats)
     mean_cross = cross * inv_std / width
-    key_sum[...] = jnp.zeros_like(key_sum)
-    value_sum[...] = jnp.zeros_like(value_sum)
     row = lax.broadcasted_iota(jnp.int32, (size, size), 0)
-    for window in range(windows):
+    for window in range(HEADS):
         here = slice(window * size, (window + 1) * size)
-        upto = slice(0, (window + 1) * size)
         packed = jnp.where(
             row == 0,
             mean[:, here],
@@ -376,54 +461,83 @@
                 jnp.where(row == 2, mean_grad[:, here], mean_cross[:, here]),
             ),
         ).T
-        unit = rows_ref[here, :HD].astype(jnp.float32)
+        unit = part_rows(rows_ref, 0, window, window + 1).astype(jnp.float32)
         grad_gain = grads_ref[here].astype(jnp.float32) * gain_ref[...]
         normed = (attended_ref[here] - packed[:, 0:1]) * packed[:, 1:2]
         layer_all[here] = (normed * gain_ref[...] * unit).astype(jnp.bfloat16)
         out_ref[here, :HD] = (grad_gain * normed).astype(jnp.bfloat16)
-        out_grads = (
+        out_grads[here] = (
             packed[:, 1:2] * (grad_gain * unit - packed[:, 2:3] - normed * packed[:, 3:4])
         ).astype(jnp.bfloat16)
-        queries = rows_ref[here, HD : 2 * HD]
-        keys = rows_ref[upto, 2 * HD : 3 * HD]
-        scores = dot(queries, keys, 1, 1) * scale
-        visible = visible_block(users_ref, window, window + 1)
-        sigmoid = jax.nn.sigmoid(scores)
-        weights = jnp.where(visible, scores * sigmoid, 0.0).astype(jnp.bfloat16)
-        slope = jnp.where(visible, sigmoid * (1.0 + scores * (1.0 - sigmoid)) * scale, 0.0)
-        score_grads = (dot(out_grads, rows_ref[upto, 3 * HD :], 1, 1) * slope).astype(jnp.bfloat16)
-        out_ref[here, HD : 2 * HD] = dot(score_grads, keys, 1, 0).astype(jnp.bfloat16)
-        key_sum[upto] += dot(score_grads, queries, 0, 0)
-        value_sum[upto] += dot(weights, out_grads, 0, 0)
-    out_ref[:, 2 * HD : 3 * HD] = key_sum[...].astype(jnp.bfloat16)
-    out_ref[:, 3 * HD :] = value_sum[...].astype(jnp.bfloat16)
+    stores = []
+    for window in range(HEADS):
+        here = slice(window * size, (window + 1) * size)
+        upto = slice(0, (window + 1) * size)
+        after = slice(window * size, HEADS * size)
+        score_grads = (
+            dot(out_grads[here], part_rows(rows_ref, 3, 0, window + 1), 1, 1)
+            * slopes_ref[here, upto]
+        ).astype(jnp.bfloat16)
+        out_ref[here, HD : 2 * HD] = dot(
+            score_grads, part_rows(rows_ref, 2, 0, window + 1), 1, 0
+        ).astype(jnp.bfloat16)
+        turned_grads = (
+            dot(part_rows(rows_ref, 3, window, window + 1), out_grads[after], 1, 1)
+            * turned_slopes_ref[here, after]
+        ).astype(jnp.bfloat16)
+        out_ref[here, 2 * HD : 3 * HD] = dot(
+            turned_grads, part_rows(rows_ref, 1, window, HEADS), 1, 0
+        ).astype(jnp.bfloat16)
+        out_ref[here, 3 * HD :] = dot(
+            turned_weights_ref[here, after], out_grads[after], 1, 0
+        ).astype(jnp.bfloat16)
+        span = pl.ds(window * size, size)
+        stores.append(
+            pltpu.make_async_copy(out_ref.at[span], out_hbm.at[span], store_sems.at[window])
+        )
+        stores[-1].start()
     for step, layer_ref in enumerate(layer_refs):
         start = pl.multiple_of(turned(head ^ step) * size, size)
         layer_ref[...] = layer_all[pl.ds(start, size), :]
-
-
-def unslot_kernel(place_ref, slot_ref, returned_ref, *refs, per_pair):
-    piece_refs, (layer_ref, grad_ref) = refs[:HEADS], refs[HEADS:]
-    slots = slot_ref.shape[1]
+    for copy in stores:
+        copy.wait()
+
+
+def unslot_kernel(back_ref, returned_ref, *refs, per_pair):
+    piece_refs = refs[:HEADS]
+    layer_hbm, grad_hbm, layer_ref, grad_ref, store_sems = refs[HEADS:]
+    slots = back_ref.shape[0]
     readers = slots // per_pair
     width = HEADS * HD
-    placed = (
-        lax.broadcasted_iota(jnp.int32, (slots, slots), 0) == slot_ref[...]
-    ).astype(jnp.bfloat16)
+    first = turned(lax.axis_index("ctx"))
+    for step, piece_ref in enumerate(piece_refs):
+        start = pl.multiple_of((first ^ step) * HD, HD)
+        layer_ref[:, pl.ds(start, HD)] = piece_ref[...]
+    stores = [pltpu.make_async_copy(layer_ref, layer_hbm, store_sems.at[2])]
+    stores[0].start()
+    heads = []
     for head in range(HEADS):
         chunks = []
         for owner in range(readers):
             dp_index, ctx_index = device_of(owner, head)
             start = (ctx_index * readers + dp_index) * per_pair
             chunks.append(returned_ref[start : start + per_pair])
-        rows = dot(placed, jnp.concatenate(chunks, axis=0), 0, 0).astype(jnp.bfloat16)
-        for part in range(4):
-            start = part * width + head * HD
-            grad_ref[:, start : start + HD] = rows[:, part * HD : (part + 1) * HD]
-    first = turned(place_ref[3])
-    for step, piece_ref in enumerate(piece_refs):
-        start = pl.multiple_of((first ^ step) * HD, HD)
-        layer_ref[:, pl.ds(start, HD)] = piece_ref[...]
+        heads.append(jnp.concatenate(chunks, axis=0))
+    half = slots // 2
+    for side in range(2):
+        span = pl.ds(side * half, half)
+        here = slice(side * half, (side + 1) * half)
+        for head in range(HEADS):
+            rows = dot(back_ref[here], heads[head], 1, 0).astype(jnp.bfloat16)
+            for part in range(4):
+                start = part * width + head * HD
+                grad_ref[here, start : start + HD] = rows[:, part * HD : (part + 1) * HD]
+        stores.append(
+            pltpu.make_async_copy(grad_ref.at[span], grad_hbm.at[span], store_sems.at[side])
+        )
+        stores[-1].start()
+    for copy in stores:
+        copy.wait()
 
 
 def send(value, target, back=False):
@@ -458,89 +572,103 @@
     per_pair = slots // readers
     group_rows = slots * HEADS
     width = 4 * HD
-    my_dp, my_ctx = lax.axis_index("dp"), lax.axis_index("ctx")
-    head = ((my_ctx & 1) << 1) | (my_dp & 1)
-    owner = (my_dp & ~1) | (my_ctx >> 1)
-    place = jnp.stack([head, owner, my_dp, my_ctx]).astype(jnp.int32)
-    gain = lax.dynamic_slice_in_dim(norm_gain, head * HD, HD, 0).reshape(1, HD)
-    rows_shape = jax.ShapeDtypeStruct((group_rows, width), jnp.bfloat16)
+    gain = lax.dynamic_slice_in_dim(norm_gain, my_place()[0] * HD, HD, 0).reshape(1, HD)
     piece_shape = jax.ShapeDtypeStruct((slots, HD), jnp.bfloat16)
-    user_row = user_of.reshape(1, slots)
-    users = [user_row] + [swap(user_row, bits, 0) for bits in range(2, readers, 2)]
-    users = jnp.concatenate(users, axis=0)
+    chunk_shape = (HEADS * readers, 4 * per_pair + 8, HD)
     outgoing, slot = pl.pallas_call(
         functools.partial(slot_kernel, per_pair=per_pair),
         out_shape=(
-            rows_shape,
+            jax.ShapeDtypeStruct(chunk_shape, jnp.bfloat16),
             jax.ShapeDtypeStruct((1, slots), jnp.int32),
         ),
-        in_specs=[smem()] + vmem(2),
-        out_specs=tuple(vmem(2)),
-        compiler_params=LIMIT,
+        in_specs=hbm(3),
+        out_specs=tuple(hbm(2)),
+        scratch_shapes=[
+            pltpu.SMEM(owner_of.shape, jnp.int32),
+            pltpu.VMEM((1, slots), jnp.int32),
+            pltpu.VMEM((1, slots), jnp.int32),
+            pltpu.VMEM(proj_read.shape, jnp.bfloat16),
+            pltpu.VMEM(chunk_shape, jnp.bfloat16),
+            pltpu.SemaphoreType.DMA((3,)),
+            pltpu.SemaphoreType.DMA((HEADS + 1,)),
+        ],
         name="slot_rows",
-    )(owner_of, user_row, proj_read)
-    outgoing, users = lax.optimization_barrier((outgoing, users))
+    )(owner_of, user_of.reshape(1, slots), proj_read)
     rows = lax.all_to_all(outgoing, ("ctx", "dp"), split_axis=0, concat_axis=0, tiled=True)
-    users = jnp.concatenate([users, swap(users, 1, 0)], axis=0)
-    users = jnp.concatenate(
-        [users] + [swap(users, 0, bits) for bits in range(1, HEADS)], axis=0
-    )
-    pieces = pl.pallas_call(
+    *pieces, back = pl.pallas_call(
         columns_kernel,
-        out_shape=(piece_shape,) * HEADS,
-        in_specs=[smem()] + vmem(1),
-        out_specs=tuple(vmem(HEADS)),
+        out_shape=(piece_shape,) * HEADS + (jax.ShapeDtypeStruct((slots, slots), jnp.bfloat16),),
+        in_specs=vmem(2),
+        out_specs=tuple(vmem(HEADS + 1)),
         compiler_params=LIMIT,
         name="cut_columns",
-    )(place, grad_output)
-    group_users, grads = pl.pallas_call(
-        functools.partial(group_kernel, per_pair=per_pair),
-        out_shape=(
-            jax.ShapeDtypeStruct((HEADS, slots), jnp.float32),
-            jax.ShapeDtypeStruct((group_rows, HD), jnp.bfloat16),
-        ),
-        in_specs=[smem(), smem()] + vmem(1 + HEADS),
-        out_specs=tuple(vmem(2)),
+    )(slot, grad_output)
+    grads = pl.pallas_call(
+        group_kernel,
+        out_shape=jax.ShapeDtypeStruct((group_rows, HD), jnp.bfloat16),
+        in_specs=vmem(HEADS),
+        out_specs=vmem(1)[0],
         compiler_params=LIMIT,
         name="lay_group",
-    )(place, owner_of, users, *regroup(pieces))
+    )(*regroup(pieces))
     attended, stats = pl.pallas_call(
         forward_kernel,
         out_shape=(
             jax.ShapeDtypeStruct((group_rows, HD), jnp.float32),
             jax.ShapeDtypeStruct((8, group_rows), jnp.float32),
         ),
-        in_specs=vmem(4),
+        in_specs=vmem(3),
         out_specs=tuple(vmem(2)),
         compiler_params=LIMIT,
         name="forward",
-    )(group_users, rows, grads, gain)
+    )(rows, grads, gain)
+    late_rows, stats = lax.optimization_barrier((rows, stats))
+    slopes = pl.pallas_call(
+        slope_kernel,
+        out_shape=(
+            jax.ShapeDtypeStruct((group_rows, group_rows), jnp.float32),
+            jax.ShapeDtypeStruct((group_rows, group_rows), jnp.float32),
+            jax.ShapeDtypeStruct((group_rows, group_rows), jnp.bfloat16),
+        ),
+        in_specs=vmem(1),
+        out_specs=tuple(vmem(3)),
+        compiler_params=LIMIT,
+        name="slopes",
+    )(late_rows)
     all_stats = [stats, swap(stats, 1, 0), swap(stats, 0, 1), swap(stats, 1, 1)]
     results = pl.pallas_call(
         backward_kernel,
-        out_shape=(rows_shape,) + (piece_shape,) * HEADS,
-        in_specs=[smem()] + vmem(5 + HEADS),
-        out_specs=tuple(vmem(1 + HEADS)),
+        out_shape=(jax.ShapeDtypeStruct((group_rows, width), jnp.bfloat16),)
+        + (piece_shape,) * HEADS,
+        in_specs=vmem(7 + HEADS),
+        out_specs=tuple(hbm(1) + vmem(HEADS)),
         scratch_shapes=[
             pltpu.VMEM((group_rows, HD), jnp.bfloat16),
-            pltpu.VMEM((group_rows, HD), jnp.float32),
-            pltpu.VMEM((group_rows, HD), jnp.float32),
+            pltpu.VMEM((group_rows, width), jnp.bfloat16),
+            pltpu.VMEM((group_rows, HD), jnp.bfloat16),
+            pltpu.SemaphoreType.DMA((HEADS,)),
         ],
         compiler_params=LIMIT,
         name="backward",
-    )(place, group_users, rows, grads, gain, attended, *all_stats)
+    )(rows, grads, gain, attended, *slopes, *all_stats)
     returned = lax.all_to_all(results[0], ("ctx", "dp"), split_axis=0, concat_axis=0, tiled=True)
+    layer_shape, grad_shape = (slots, HEADS * HD), (slots, 4 * HEADS * HD)
     return pl.pallas_call(
         functools.partial(unslot_kernel, per_pair=per_pair),
         out_shape=(
-            jax.ShapeDtypeStruct((slots, HEADS * HD), jnp.bfloat16),
-            jax.ShapeDtypeStruct((slots, 4 * HEADS * HD), jnp.bfloat16),
+            jax.ShapeDtypeStruct(layer_shape, jnp.bfloat16),
+            jax.ShapeDtypeStruct(grad_shape, jnp.bfloat16),
         ),
-        in_specs=[smem()] + vmem(2 + HEADS),
-        out_specs=tuple(vmem(2)),
+        in_specs=vmem(2 + HEADS),
+        out_specs=tuple(hbm(2)),
+        scratch_shapes=[
+            pltpu.VMEM(layer_shape, jnp.bfloat16),
+            pltpu.VMEM(grad_shape, jnp.bfloat16),
+            pltpu.SemaphoreType.DMA((3,)),
+        ],
         compiler_params=LIMIT,
         name="unslot_rows",
-    )(place, slot, returned, *regroup(results[1:], back=True))
+    )(back, returned, *regroup(results[1:], back=True))
 
 
 def solution(mesh):

time: 61.9 us -> 56.1 us (0.906)
  starting transfers between devices: 31.7 us -> 23.5 us
  waiting for transfers between devices: 17.9 us -> 22.7 us
  Pallas kernels: 8.83 us -> 7.64 us
  local copies, waits for them, and re-layouts: 1.8 us -> 0.73 us
    ppermute x18 -> x11, starting transfers between devices: 20.7 us -> 12.8 us  [send(): return lax.ppermute(value, ('dp', 'ctx'), pairs)]
    all_to_all x1, waiting for transfers between devices: 1.58 us -> 7.61 us  [by_heads(): lax.all_to_all(outgoing, ('ctx', 'dp'), split_axis=0, concat_axis=0, tile...]
    ppermute x18 -> x11, waiting for transfers between devices: 9.44 us -> 7.99 us  [send(): return lax.ppermute(value, ('dp', 'ctx'), pairs)]
    pallas_call x3 -> x4, Pallas kernels: 4.4 us -> 3.3 us  [the longest x1 2.43 us: by_heads(): pl.pallas_call(backward_kernel, out_shape=(jax.ShapeDtypeStruct((group_ro...]
    unnamed x10 -> x6, local copies, waits for them, and re-layouts: 1.71 us -> 0.66 us
    all_to_all x1, starting transfers between devices: 4.19 us -> 3.54 us  [by_heads(): lax.all_to_all(results[0], ('ctx', 'dp'), split_axis=0, concat_axis=0, ti...]
    pallas_call x1, Pallas kernels: 1.66 us -> 1.04 us  [by_heads(): pl.pallas_call(functools.partial(unslot_kernel, per_pair=per_pair), out_s...]
  transfers between devices with their start and end apart: 20 -> 13, of which waited for: 11 -> 11; matrix products, arithmetic and copies ran while one was open for 0% -> 0% of each run, Pallas kernels for 5% -> 2%
where the time goes in v3:
time: 56.1 us; the launch traced here: 55.3 us
  starting transfers between devices  23.5 us (42%)
  waiting for transfers between devices  22.7 us (40%)
  Pallas kernels  7.64 us (14%)
  between operations  0.76 us (1%)
  local copies, waits for them, and re-layouts  0.73 us (1%)
    ppermute x11, starting transfers between devices, send(): return lax.ppermute(value, ('dp', 'ctx'), pairs)  12.8 us
    ppermute x11, waiting for transfers between devices, send(): return lax.ppermute(value, ('dp', 'ctx'), pairs)  7.99 us
    all_to_all x1, waiting for transfers between devices, by_heads(): lax.all_to_all(outgoing, ('ctx', 'dp'), split_axis=0, concat_axis=0, tile...  7.61 us
    all_to_all x1, waiting for transfers between devices, by_heads(): lax.all_to_all(results[0], ('ctx', 'dp'), split_axis=0, concat_axis=0, ti...  7.11 us
    all_to_all x1, starting transfers between devices, by_heads(): lax.all_to_all(outgoing, ('ctx', 'dp'), split_axis=0, concat_axis=0, tile...  7.11 us
    all_to_all x1, starting transfers between devices, by_heads(): lax.all_to_all(results[0], ('ctx', 'dp'), split_axis=0, concat_axis=0, ti...  3.54 us
    pallas_call x1, Pallas kernels, by_heads(): pl.pallas_call(backward_kernel, out_shape=(jax.ShapeDtypeStruct((group_ro...  2.43 us
    pallas_call x1, Pallas kernels, by_heads(): pl.pallas_call(functools.partial(slot_kernel, per_pair=per_pair), out_sha...  2.29 us
  transfers between devices with their start and end apart: 13, of which 11 were waited for; matrix products, arithmetic and copies ran while one was open for 0% of the time, Pallas kernels for 2%

profile of v3, /device:TPU:1, one launch (start us, length us, event | category | flops | bytes accessed | tf_op | source)
XLA Modules:
  0.0 55.3 jit_solution(14346775127827582996)
XLA Ops:
  0.6 2.3 %slot_rows.1 = (bf16[32,72,128]{2,1,0:T(8,128)(2,1)}, s32[1,128]{1,0:T(1,128)}) custom-call(s32[16]{0:T(128)} %owner_hbm.1, s32[1,128]{1,0:T(1,128)} %bitcast.6, bf16[128,2048]{1,0:T(8,128)(2,1)} %proj_hbm.1), custom_call_target="tpu_custom_call" | custom-call | tf_op jit(solution)/shard_map/slot_rows/pallas_call | solution.py:578
  3.0 7.1 %all-to-all-start = ((bf16[32,72,128]{2,1,0:T(8,128)(2,1)}), bf16[32,72,128]{2,1,0:T(8,128)(2,1)S(1)}, u32[]{:S(2)}, u32[]{:S(2)}) async-start(bf16[32,72,128]{2,1,0:T(8,128)(2,1)} %get-tuple-element.23), calls=%async_computation | async-start | bytes 1179648 | tf_op jit(solution)/shard_map/all_to_all | solution.py:597
  10.1 0.6 %copy-done.2 = s32[1,128]{1,0:T(1,128)S(1)} copy-done((s32[1,128]{1,0:T(1,128)S(1)}, s32[1,128]{1,0:T(1,128)}, u32[]{:S(2)}) %copy-start.2) | copy-done | bytes 536
  10.7 0.1 cut_columns.1
  10.8 3.5 %collective-permute-start = (bf16[128,128]{1,0:T(8,128)(2,1)S(1)}, bf16[128,128]{1,0:T(8,128)(2,1)S(1)}, u32[]{:S(2)}, u32[]{:S(2)}) collective-permute-start(bf16[128,128]{1,0:T(8,128)(2,1)S(1)} %get-tuple-element.24), channel_id=1, source_target_pairs={{0,0},{1,1},{2,4},{3,5},{4,2},{5,3},{6,6},{7,7},{8,8},{9,9},{10,12... | collective-permute-start | bytes 98312 | tf_op jit(solution)/shard_map/ppermute | solution.py:551
  14.4 0.0 collective-permute-start.1
  14.4 1.3 %collective-permute-start.2 = (bf16[128,128]{1,0:T(8,128)(2,1)S(1)}, bf16[128,128]{1,0:T(8,128)(2,1)S(1)}, u32[]{:S(2)}, u32[]{:S(2)}) collective-permute-start(bf16[128,128]{1,0:T(8,128)(2,1)S(1)} %get-tuple-element.26), channel_id=1, source_target_pairs={{0,1},{1,0},{2,5},{3,4},{4,3},{5,2},{6,7},{7,6},{8,9},{9,8},{10,13... | collective-permute-start | bytes 98312 | tf_op jit(solution)/shard_map/ppermute | solution.py:551
  15.7 0.1 collective-permute-start.3
  15.8 0.1 dynamic-slice_bitcast_fusion.gain_ref
  15.9 0.6 %collective-permute-done.refs_0_ = bf16[128,128]{1,0:T(8,128)(2,1)S(1)} collective-permute-done((bf16[128,128]{1,0:T(8,128)(2,1)S(1)}, bf16[128,128]{1,0:T(8,128)(2,1)S(1)}, u32[]{:S(2)}, u32[]{:S(2)}) %collective-permute-start) | collective-permute-done | bytes 32800 | tf_op jit(solution)/shard_map/ppermute | solution.py:551
  16.5 0.3 collective-permute-done.1.refs_1_
  16.8 2.3 %collective-permute-done.2.refs_2_ = bf16[128,128]{1,0:T(8,128)(2,1)S(1)} collective-permute-done((bf16[128,128]{1,0:T(8,128)(2,1)S(1)}, bf16[128,128]{1,0:T(8,128)(2,1)S(1)}, u32[]{:S(2)}, u32[]{:S(2)}) %collective-permute-start.2) | collective-permute-done | bytes 32800 | tf_op jit(solution)/shard_map/ppermute | solution.py:551
  19.1 0.7 %collective-permute-done.3.refs_3_ = bf16[128,128]{1,0:T(8,128)(2,1)S(1)} collective-permute-done((bf16[128,128]{1,0:T(8,128)(2,1)S(1)}, bf16[128,128]{1,0:T(8,128)(2,1)S(1)}, u32[]{:S(2)}, u32[]{:S(2)}) %collective-permute-start.3) | collective-permute-done | bytes 32800 | tf_op jit(solution)/shard_map/ppermute | solution.py:551
  19.9 7.6 %all-to-all-done.rows_ref = bf16[32,72,128]{2,1,0:T(8,128)(2,1)S(1)} async-done(((bf16[32,72,128]{2,1,0:T(8,128)(2,1)}), bf16[32,72,128]{2,1,0:T(8,128)(2,1)S(1)}, u32[]{:S(2)}, u32[]{:S(2)}) %all-to-all-start) | async-done | bytes 589856 | tf_op jit(solution)/shard_map/all_to_all | solution.py:597
  27.5 1.0 %forward.1 = (f32[512,128]{1,0:T(8,128)S(1)}, f32[8,512]{1,0:T(8,128)S(1)}) custom-call(bf16[32,72,128]{2,1,0:T(8,128)(2,1)S(1)} %all-to-all-done.rows_ref, bf16[512,128]{1,0:T(8,128)(2,1)S(1)} %lay_group.1.grads_ref, f32[1,128]{1,0:T(1,128)S(1)} %dynamic-slice_bitcast_fusion.gain_ref), custom_call_target="tpu_custom_call" | custom-call | tf_op jit(solution)/shard_map/forward/pallas_call | solution.py:614
  28.5 0.0 collective-permute-start.6
  28.5 2.0 %collective-permute-start.5 = (f32[8,512]{1,0:T(8,128)S(1)}, f32[8,512]{1,0:T(8,128)S(1)}, u32[]{:S(2)}, u32[]{:S(2)}) collective-permute-start(f32[8,512]{1,0:T(8,128)S(1)} %get-tuple-element.34.refs_0_), channel_id=1, source_target_pairs={{0,1},{1,0},{2,3},{3,2},{4,5},{5,4},{6,7},{7,6},{8,9},{9,8},{10,11... | collective-permute-start | bytes 49160 | tf_op jit(solution)/shard_map/ppermute | solution.py:551
  30.5 0.2 collective-permute-start.4
  30.7 0.8 %slopes.1 = (f32[512,512]{1,0:T(8,128)S(1)}, f32[512,512]{1,0:T(8,128)S(1)}, bf16[512,512]{1,0:T(8,128)(2,1)S(1)}) custom-call(bf16[32,72,128]{2,1,0:T(8,128)(2,1)S(1)} %all-to-all-done.rows_ref), custom_call_target="tpu_custom_call" | custom-call | tf_op jit(solution)/shard_map/slopes/pallas_call | solution.py:626
  31.4 0.6 %collective-permute-done.6.refs_3_ = f32[8,512]{1,0:T(8,128)S(1)} collective-permute-done((f32[8,512]{1,0:T(8,128)S(1)}, f32[8,512]{1,0:T(8,128)S(1)}, u32[]{:S(2)}, u32[]{:S(2)}) %collective-permute-start.6) | collective-permute-done | bytes 16416 | tf_op jit(solution)/shard_map/ppermute | solution.py:551
  32.0 2.4 %backward.1 = (bf16[512,512]{1,0:T(8,128)(2,1)}, bf16[128,128]{1,0:T(8,128)(2,1)S(1)}, bf16[128,128]{1,0:T(8,128)(2,1)S(1)}, bf16[128,128]{1,0:T(8,128)(2,1)S(1)}, bf16[128,128]{1,0:T(8,128)(2,1)S(1)}) custom-call(bf16[32,72,128]{2,1,0:T(8,128)(2,1)S(1)} %all-to-all-done.rows_ref, bf16[512,128]{1,0:T(8,128)(2,1)S(1)} %lay_group.1.grads_ref, ...), custom_call_target="tpu_custom_call" | custom-call | tf_op jit(solution)/shard_map/backward/pallas_call | solution.py:639
  34.5 3.5 %all-to-all-start.1 = ((bf16[32,16,512]{2,1,0:T(8,128)(2,1)}), bf16[32,16,512]{2,1,0:T(8,128)(2,1)S(1)}, u32[]{:S(2)}, u32[]{:S(2)}) async-start(bf16[32,16,512]{2,1,0:T(8,128)(2,1)} %bitcast.2), calls=%async_computation.1 | async-start | bytes 1048576 | tf_op jit(solution)/shard_map/all_to_all | solution.py:654
  38.0 3.6 %collective-permute-start.7 = (bf16[128,128]{1,0:T(8,128)(2,1)S(1)}, bf16[128,128]{1,0:T(8,128)(2,1)S(1)}, u32[]{:S(2)}, u32[]{:S(2)}) collective-permute-start(bf16[128,128]{1,0:T(8,128)(2,1)S(1)} %get-tuple-element.36), channel_id=1, source_target_pairs={{0,0},{1,1},{4,2},{5,3},{2,4},{3,5},{6,6},{7,7},{8,8},{9,9},{12,10... | collective-permute-start | bytes 98312 | tf_op jit(solution)/shard_map/ppermute | solution.py:551
  41.6 0.0 collective-permute-start.8
  41.6 1.3 %collective-permute-start.9 = (bf16[128,128]{1,0:T(8,128)(2,1)S(1)}, bf16[128,128]{1,0:T(8,128)(2,1)S(1)}, u32[]{:S(2)}, u32[]{:S(2)}) collective-permute-start(bf16[128,128]{1,0:T(8,128)(2,1)S(1)} %get-tuple-element.38), channel_id=1, source_target_pairs={{1,0},{0,1},{5,2},{4,3},{3,4},{2,5},{7,6},{6,7},{9,8},{8,9},{13,10... | collective-permute-start | bytes 98312 | tf_op jit(solution)/shard_map/ppermute | solution.py:551
  42.9 0.8 %collective-permute-start.10 = (bf16[128,128]{1,0:T(8,128)(2,1)S(1)}, bf16[128,128]{1,0:T(8,128)(2,1)S(1)}, u32[]{:S(2)}, u32[]{:S(2)}) collective-permute-start(bf16[128,128]{1,0:T(8,128)(2,1)S(1)} %get-tuple-element.39), channel_id=1, source_target_pairs={{5,0},{4,1},{1,2},{0,3},{7,4},{6,5},{3,6},{2,7},{13,8},{12,9},{9,1... | collective-permute-start | bytes 98312 | tf_op jit(solution)/shard_map/ppermute | solution.py:551
  43.7 0.3 collective-permute-done.7.refs_0_
  44.0 1.1 %collective-permute-done.8.refs_1_ = bf16[128,128]{1,0:T(8,128)(2,1)S(1)} collective-permute-done((bf16[128,128]{1,0:T(8,128)(2,1)S(1)}, bf16[128,128]{1,0:T(8,128)(2,1)S(1)}, u32[]{:S(2)}, u32[]{:S(2)}) %collective-permute-start.8) | collective-permute-done | bytes 32800 | tf_op jit(solution)/shard_map/ppermute | solution.py:551
  45.1 1.9 %collective-permute-done.9.refs_2_ = bf16[128,128]{1,0:T(8,128)(2,1)S(1)} collective-permute-done((bf16[128,128]{1,0:T(8,128)(2,1)S(1)}, bf16[128,128]{1,0:T(8,128)(2,1)S(1)}, u32[]{:S(2)}, u32[]{:S(2)}) %collective-permute-start.9) | collective-permute-done | bytes 32800 | tf_op jit(solution)/shard_map/ppermute | solution.py:551
  47.0 0.2 collective-permute-done.10.refs_3_
  47.2 7.1 %all-to-all-done.1 = bf16[32,16,512]{2,1,0:T(8,128)(2,1)S(1)} async-done(((bf16[32,16,512]{2,1,0:T(8,128)(2,1)}), bf16[32,16,512]{2,1,0:T(8,128)(2,1)S(1)}, u32[]{:S(2)}, u32[]{:S(2)}) %all-to-all-start.1) | async-done | bytes 524320 | tf_op jit(solution)/shard_map/all_to_all | solution.py:654
  54.3 1.0 %unslot_rows.1 = (bf16[128,512]{1,0:T(8,128)(2,1)}, bf16[128,2048]{1,0:T(8,128)(2,1)}) custom-call(bf16[128,128]{1,0:T(8,128)(2,1)S(1)} %get-tuple-element.22.back_ref, bf16[512,512]{1,0:T(8,128)(2,1)S(1)} %bitcast.5, bf16[128,128]{1,0:T(8,128)(2,1)S(1)} %collective-permute-done.7.refs_0_, bf16[128,128]{1,0:T(8,128)(2,1)S(1)} %collective-permute-done.8.refs_1_, ...), custom_call_target="tpu_custom_call" | custom-call | tf_op jit(solution)/shard_map/unslot_rows/pallas_call | solution.py:656
  (8 shorter events, 0.0 us)
Async XLA Ops:
  0.6 15.2 %copy-start = (f32[512]{0:T(512)S(1)}, f32[512]{0:T(512)}, u32[]{:S(2)}) copy-start(f32[512]{0:T(512)} %param.6) | copy-start | bytes 6148
  2.9 7.1 %copy-start.1 = (bf16[128,512]{1,0:T(8,128)(2,1)S(1)}, bf16[128,512]{1,0:T(8,128)(2,1)}, u32[]{:S(2)}) copy-start(bf16[128,512]{1,0:T(8,128)(2,1)} %grad_ref.1) | copy-start | bytes 393220
  3.0 24.5 %all-to-all-start = ((bf16[32,72,128]{2,1,0:T(8,128)(2,1)}), bf16[32,72,128]{2,1,0:T(8,128)(2,1)S(1)}, u32[]{:S(2)}, u32[]{:S(2)}) async-start(bf16[32,72,128]{2,1,0:T(8,128)(2,1)} %get-tuple-element.23), calls=%async_computation | async-start | bytes 1179648 | tf_op jit(solution)/shard_map/all_to_all | solution.py:597
  10.1 0.7 %copy-start.2 = (s32[1,128]{1,0:T(1,128)S(1)}, s32[1,128]{1,0:T(1,128)}, u32[]{:S(2)}) copy-start(s32[1,128]{1,0:T(1,128)} %get-tuple-element.21.slot_ref) | copy-start | bytes 1540
  10.8 5.7 %collective-permute-start = (bf16[128,128]{1,0:T(8,128)(2,1)S(1)}, bf16[128,128]{1,0:T(8,128)(2,1)S(1)}, u32[]{:S(2)}, u32[]{:S(2)}) collective-permute-start(bf16[128,128]{1,0:T(8,128)(2,1)S(1)} %get-tuple-element.24), channel_id=1, source_target_pairs={{0,0},{1,1},{2,4},{3,5},{4,2},{5,3},{6,6},{7,7},{8,8},{9,9},{10,12... | collective-permute-start | bytes 98312 | tf_op jit(solution)/shard_map/ppermute | solution.py:551
  14.4 2.4 %collective-permute-start.1 = (bf16[128,128]{1,0:T(8,128)(2,1)S(1)}, bf16[128,128]{1,0:T(8,128)(2,1)S(1)}, u32[]{:S(2)}, u32[]{:S(2)}) collective-permute-start(bf16[128,128]{1,0:T(8,128)(2,1)S(1)} %get-tuple-element.25), channel_id=1, source_target_pairs={{0,4},{1,5},{2,0},{3,1},{4,6},{5,7},{6,2},{7,3},{8,12},{9,13},{10,... | collective-permute-start | bytes 98312 | tf_op jit(solution)/shard_map/ppermute | solution.py:551
  14.4 4.7 %collective-permute-start.2 = (bf16[128,128]{1,0:T(8,128)(2,1)S(1)}, bf16[128,128]{1,0:T(8,128)(2,1)S(1)}, u32[]{:S(2)}, u32[]{:S(2)}) collective-permute-start(bf16[128,128]{1,0:T(8,128)(2,1)S(1)} %get-tuple-element.26), channel_id=1, source_target_pairs={{0,1},{1,0},{2,5},{3,4},{4,3},{5,2},{6,7},{7,6},{8,9},{9,8},{10,13... | collective-permute-start | bytes 98312 | tf_op jit(solution)/shard_map/ppermute | solution.py:551
  15.7 4.1 %collective-permute-start.3 = (bf16[128,128]{1,0:T(8,128)(2,1)S(1)}, bf16[128,128]{1,0:T(8,128)(2,1)S(1)}, u32[]{:S(2)}, u32[]{:S(2)}) collective-permute-start(bf16[128,128]{1,0:T(8,128)(2,1)S(1)} %get-tuple-element.27), channel_id=1, source_target_pairs={{0,5},{1,4},{2,1},{3,0},{4,7},{5,6},{6,3},{7,2},{8,13},{9,12},{10,... | collective-permute-start | bytes 98312 | tf_op jit(solution)/shard_map/ppermute | solution.py:551
  28.5 3.6 %collective-permute-start.6 = (f32[8,512]{1,0:T(8,128)S(1)}, f32[8,512]{1,0:T(8,128)S(1)}, u32[]{:S(2)}, u32[]{:S(2)}) collective-permute-start(f32[8,512]{1,0:T(8,128)S(1)} %get-tuple-element.34.refs_0_), channel_id=1, source_target_pairs={{0,5},{1,4},{2,7},{3,6},{4,1},{5,0},{6,3},{7,2},{8,13},{9,12},{10,... | collective-permute-start | bytes 49160 | tf_op jit(solution)/shard_map/ppermute | solution.py:551
  28.5 3.5 %collective-permute-start.5 = (f32[8,512]{1,0:T(8,128)S(1)}, f32[8,512]{1,0:T(8,128)S(1)}, u32[]{:S(2)}, u32[]{:S(2)}) collective-permute-start(f32[8,512]{1,0:T(8,128)S(1)} %get-tuple-element.34.refs_0_), channel_id=1, source_target_pairs={{0,1},{1,0},{2,3},{3,2},{4,5},{5,4},{6,7},{7,6},{8,9},{9,8},{10,11... | collective-permute-start | bytes 49160 | tf_op jit(solution)/shard_map/ppermute | solution.py:551
  30.5 1.5 %collective-permute-start.4 = (f32[8,512]{1,0:T(8,128)S(1)}, f32[8,512]{1,0:T(8,128)S(1)}, u32[]{:S(2)}, u32[]{:S(2)}) collective-permute-start(f32[8,512]{1,0:T(8,128)S(1)} %get-tuple-element.34.refs_0_), channel_id=1, source_target_pairs={{0,4},{1,5},{2,6},{3,7},{4,0},{5,1},{6,2},{7,3},{8,12},{9,13},{10,... | collective-permute-start | bytes 49160 | tf_op jit(solution)/shard_map/ppermute | solution.py:551
  34.5 19.8 %all-to-all-start.1 = ((bf16[32,16,512]{2,1,0:T(8,128)(2,1)}), bf16[32,16,512]{2,1,0:T(8,128)(2,1)S(1)}, u32[]{:S(2)}, u32[]{:S(2)}) async-start(bf16[32,16,512]{2,1,0:T(8,128)(2,1)} %bitcast.2), calls=%async_computation.1 | async-start | bytes 1048576 | tf_op jit(solution)/shard_map/all_to_all | solution.py:654
  38.0 6.0 %collective-permute-start.7 = (bf16[128,128]{1,0:T(8,128)(2,1)S(1)}, bf16[128,128]{1,0:T(8,128)(2,1)S(1)}, u32[]{:S(2)}, u32[]{:S(2)}) collective-permute-start(bf16[128,128]{1,0:T(8,128)(2,1)S(1)} %get-tuple-element.36), channel_id=1, source_target_pairs={{0,0},{1,1},{4,2},{5,3},{2,4},{3,5},{6,6},{7,7},{8,8},{9,9},{12,10... | collective-permute-start | bytes 98312 | tf_op jit(solution)/shard_map/ppermute | solution.py:551
  41.6 3.5 %collective-permute-start.8 = (bf16[128,128]{1,0:T(8,128)(2,1)S(1)}, bf16[128,128]{1,0:T(8,128)(2,1)S(1)}, u32[]{:S(2)}, u32[]{:S(2)}) collective-permute-start(bf16[128,128]{1,0:T(8,128)(2,1)S(1)} %get-tuple-element.37), channel_id=1, source_target_pairs={{4,0},{5,1},{0,2},{1,3},{6,4},{7,5},{2,6},{3,7},{12,8},{13,9},{8,1... | collective-permute-start | bytes 98312 | tf_op jit(solution)/shard_map/ppermute | solution.py:551
  41.6 5.3 %collective-permute-start.9 = (bf16[128,128]{1,0:T(8,128)(2,1)S(1)}, bf16[128,128]{1,0:T(8,128)(2,1)S(1)}, u32[]{:S(2)}, u32[]{:S(2)}) collective-permute-start(bf16[128,128]{1,0:T(8,128)(2,1)S(1)} %get-tuple-element.38), channel_id=1, source_target_pairs={{1,0},{0,1},{5,2},{4,3},{3,4},{2,5},{7,6},{6,7},{9,8},{8,9},{13,10... | collective-permute-start | bytes 98312 | tf_op jit(solution)/shard_map/ppermute | solution.py:551
  42.9 4.3 %collective-permute-start.10 = (bf16[128,128]{1,0:T(8,128)(2,1)S(1)}, bf16[128,128]{1,0:T(8,128)(2,1)S(1)}, u32[]{:S(2)}, u32[]{:S(2)}) collective-permute-start(bf16[128,128]{1,0:T(8,128)(2,1)S(1)} %get-tuple-element.39), channel_id=1, source_target_pairs={{5,0},{4,1},{1,2},{0,3},{7,4},{6,5},{3,6},{2,7},{13,8},{12,9},{9,1... | collective-permute-start | bytes 98312 | tf_op jit(solution)/shard_map/ppermute | solution.py:551

commit v4 on v3

--- a/solution.py
+++ b/solution.py
@@ -200,11 +200,16 @@
     return (layer_out, grad_read)
 
 
+STEP = 2
 LIMIT = pltpu.CompilerParams(vmem_limit_bytes=16 * 2**20)
 
 
 def device_of(owner, head):
     return (owner & ~1) | (head & 1), ((owner & 1) << 1) | (head >> 1)
+
+
+def chunk_of(dp_index, ctx_index, readers):
+    return ctx_index * readers + (dp_index & 1) * (readers // 2) + (dp_index >> 1)
 
 
 def turned(index):
@@ -299,7 +304,8 @@
     for owner in range(readers):
         for head in range(HEADS):
             dp_index, ctx_index = device_of(owner, head)
-            send_ref[ctx_index * readers + dp_index, 4 * per_pair :, :] = jnp.broadcast_to(
+            chunk = chunk_of(dp_index, ctx_index, readers)
+            send_ref[chunk, 4 * per_pair :, :] = jnp.broadcast_to(
                 tagged[owner : owner + 1], (extra, slots)
             )
     loads[2].wait()
@@ -310,7 +316,7 @@
             for owner in range(readers):
                 for side in range(2):
                     dp_index, ctx_index = device_of(owner, 2 * half + side)
-                    chunk = ctx_index * readers + dp_index
+                    chunk = chunk_of(dp_index, ctx_index, readers)
                     send_ref[chunk, part * per_pair : (part + 1) * per_pair, :] = rows[
                         owner * per_pair : (owner + 1) * per_pair, side * HD : (side + 1) * HD
                     ]
@@ -348,10 +354,26 @@
 
 
 def part_rows(rows_ref, part, first, last):
-    per_pair = HD // (rows_ref.shape[0] // HEADS)
     readers = rows_ref.shape[0] // HEADS
-    rows = rows_ref[first * readers : last * readers, part * per_pair : (part + 1) * per_pair, :]
-    return rows.reshape((last - first) * readers * per_pair, HD)
+    per_pair = HD // readers
+    span = slice(part * per_pair, (part + 1) * per_pair)
+    rows = [
+        rows_ref[chunk_of(reader, window, readers), span, :]
+        for window in range(first, last)
+        for reader in range(readers)
+    ]
+    return jnp.concatenate(rows, axis=0)
+
+
+def put_rows(out_ref, part, first, last, rows, readers):
+    per_pair = HD // readers
+    for window in range(first, last):
+        for reader in range(readers):
+            source = ((window - first) * readers + reader) * per_pair
+            target = chunk_of(reader, window, readers) * per_pair
+            out_ref[target : target + per_pair, part * HD : (part + 1) * HD] = rows[
+                source : source + per_pair
+            ].astype(jnp.bfloat16)
 
 
 def window_users(rows_ref, window):
@@ -361,16 +383,17 @@
     return jnp.sum(tags.astype(jnp.float32), axis=0)[:1]
 
 
-def visible_block(users, query_window):
-    size = users[0].shape[1]
-    query_users = jnp.broadcast_to(users[query_window], (size, size)).T
+def visible_block(users, first, last):
+    size = HD
+    query_users = [jnp.broadcast_to(users[window], (size, size)).T for window in range(first, last)]
+    query_users = jnp.concatenate(query_users, axis=0)
+    rows = lax.broadcasted_iota(jnp.int32, query_users.shape, 0)
+    columns = lax.broadcasted_iota(jnp.int32, query_users.shape, 1)
     blocks = []
-    for window in range(query_window + 1):
+    for window in range(last):
         block = (query_users == users[window]) & (query_users > 0.0)
-        if window == query_window:
-            rows = lax.broadcasted_iota(jnp.int32, (size, size), 0)
-            columns = lax.broadcasted_iota(jnp.int32, (size, size), 1)
-            block = block & (columns <= rows)
+        if window >= first:
+            block = block & (columns + (window - first) * size <= rows)
         blocks.append(block)
     return jnp.concatenate(blocks, axis=1)
 
@@ -378,51 +401,55 @@
 def forward_kernel(rows_ref, grads_ref, gain_ref, attended_ref, stats_ref):
     size = HD
     scale = HD ** (-0.5)
-    lane = lax.broadcasted_iota(jnp.int32, (size, HD), 1)
     users = [window_users(rows_ref, window) for window in range(HEADS)]
-    for window in range(HEADS):
-        here = slice(window * size, (window + 1) * size)
-        queries = part_rows(rows_ref, 1, window, window + 1)
-        scores = dot(queries, part_rows(rows_ref, 2, 0, window + 1), 1, 1) * scale
-        visible = visible_block(users, window)
+    for first in range(0, HEADS, STEP):
+        last = first + STEP
+        queries = part_rows(rows_ref, 1, first, last)
+        scores = dot(queries, part_rows(rows_ref, 2, 0, last), 1, 1) * scale
+        visible = visible_block(users, first, last)
         weights = jnp.where(visible, scores * jax.nn.sigmoid(scores), 0.0).astype(jnp.bfloat16)
-        attended = dot(weights, part_rows(rows_ref, 3, 0, window + 1), 1, 0)
-        attended_ref[here] = attended
-        grad_normed = (
-            grads_ref[here].astype(jnp.float32)
-            * gain_ref[...]
-            * part_rows(rows_ref, 0, window, window + 1).astype(jnp.float32)
-        )
-        mean = jnp.mean(attended, axis=1, keepdims=True)
-        centered = attended - mean
-        spread = jnp.sum(centered * centered, axis=1, keepdims=True)
-        grad_sum = jnp.sum(grad_normed, axis=1, keepdims=True)
-        cross = jnp.sum(grad_normed * centered, axis=1, keepdims=True)
-        packed = jnp.where(
-            lane == 0, mean, jnp.where(lane == 1, spread, jnp.where(lane == 2, grad_sum, cross))
-        )
-        stats_ref[:, here] = packed.T[:8]
+        block = dot(weights, part_rows(rows_ref, 3, 0, last), 1, 0)
+        attended_ref[first * size : last * size] = block
+        for window in range(first, last):
+            here = slice(window * size, (window + 1) * size)
+            attended = block[(window - first) * size : (window - first + 1) * size]
+            grad_normed = (
+                grads_ref[here].astype(jnp.float32)
+                * gain_ref[...]
+                * part_rows(rows_ref, 0, window, window + 1).astype(jnp.float32)
+            )
+            turned_att = attended.T
+            turned_grad = grad_normed.T
+            mean = jnp.mean(turned_att, axis=0, keepdims=True)
+            centered = turned_att - mean
+            spread = jnp.sum(centered * centered, axis=0, keepdims=True)
+            grad_sum = jnp.sum(turned_grad, axis=0, keepdims=True)
+            cross = jnp.sum(turned_grad * centered, axis=0, keepdims=True)
+            stats_ref[0:1, here] = mean
+            stats_ref[1:2, here] = spread
+            stats_ref[2:3, here] = grad_sum
+            stats_ref[3:4, here] = cross
+            stats_ref[4:8, here] = jnp.zeros((4, size), jnp.float32)
 
 
 def slope_kernel(rows_ref, slopes_ref, turned_slopes_ref, turned_weights_ref):
     size = HD
     scale = HD ** (-0.5)
     users = [window_users(rows_ref, window) for window in range(HEADS)]
-    for window in range(HEADS):
-        here = slice(window * size, (window + 1) * size)
-        upto = slice(0, (window + 1) * size)
-        queries = part_rows(rows_ref, 1, window, window + 1)
-        scores = dot(queries, part_rows(rows_ref, 2, 0, window + 1), 1, 1) * scale
+    for first in range(0, HEADS, STEP):
+        last = first + STEP
+        queries = part_rows(rows_ref, 1, first, last)
+        scores = dot(queries, part_rows(rows_ref, 2, 0, last), 1, 1) * scale
         sigmoid = jax.nn.sigmoid(scores)
         slopes = sigmoid * (1.0 + scores * (1.0 - sigmoid)) * scale
-        visible = visible_block(users, window)
+        visible = visible_block(users, first, last)
         slopes = jnp.where(visible, slopes, 0.0)
         weights = jnp.where(visible, scores * sigmoid, 0.0)
-        slopes_ref[here, upto] = slopes
-        for key_window in range(window + 1):
-            there = slice(key_window * size, (key_window + 1) * size)
-            turned_slopes_ref[there, here] = slopes[:, there].T
-            turned_weights_ref[there, here] = weights[:, there].T.astype(jnp.bfloat16)
+        slopes_ref[first * size : last * size, : last * size] = slopes
+        turned_slopes_ref[: last * size, first * size : last * size] = slopes.T
+        turned_weights_ref[: last * size, first * size : last * size] = weights.T.astype(
+            jnp.bfloat16
+        )
 
 
 def backward_kernel(
@@ -440,6 +467,7 @@
     layer_refs = refs[HEADS + 1 : 2 * HEADS + 1]
     layer_all, out_ref, out_grads, store_sems = refs[2 * HEADS + 1 :]
     head = my_place()[0]
+    readers = rows_ref.shape[0] // HEADS
     size = HD
     width = float(HEADS * HD)
     stats = [stat_ref[...] for stat_ref in stats_refs]
@@ -465,35 +493,32 @@
         grad_gain = grads_ref[here].astype(jnp.float32) * gain_ref[...]
         normed = (attended_ref[here] - packed[:, 0:1]) * packed[:, 1:2]
         layer_all[here] = (normed * gain_ref[...] * unit).astype(jnp.bfloat16)
-        out_ref[here, :HD] = (grad_gain * normed).astype(jnp.bfloat16)
+        put_rows(out_ref, 0, window, window + 1, grad_gain * normed, readers)
         out_grads[here] = (
             packed[:, 1:2] * (grad_gain * unit - packed[:, 2:3] - normed * packed[:, 3:4])
         ).astype(jnp.bfloat16)
     stores = []
-    for window in range(HEADS):
-        here = slice(window * size, (window + 1) * size)
-        upto = slice(0, (window + 1) * size)
-        after = slice(window * size, HEADS * size)
+    for first in range(0, HEADS, STEP):
+        last = first + STEP
+        here = slice(first * size, last * size)
+        upto = slice(0, last * size)
+        after = slice(first * size, HEADS * size)
         score_grads = (
-            dot(out_grads[here], part_rows(rows_ref, 3, 0, window + 1), 1, 1)
-            * slopes_ref[here, upto]
+            dot(out_grads[here], part_rows(rows_ref, 3, 0, last), 1, 1) * slopes_ref[here, upto]
         ).astype(jnp.bfloat16)
-        out_ref[here, HD : 2 * HD] = dot(
-            score_grads, part_rows(rows_ref, 2, 0, window + 1), 1, 0
-        ).astype(jnp.bfloat16)
+        query_grads = dot(score_grads, part_rows(rows_ref, 2, 0, last), 1, 0)
+        put_rows(out_ref, 1, first, last, query_grads, readers)
         turned_grads = (
-            dot(part_rows(rows_ref, 3, window, window + 1), out_grads[after], 1, 1)
+            dot(part_rows(rows_ref, 3, first, last), out_grads[after], 1, 1)
             * turned_slopes_ref[here, after]
         ).astype(jnp.bfloat16)
-        out_ref[here, 2 * HD : 3 * HD] = dot(
-            turned_grads, part_rows(rows_ref, 1, window, HEADS), 1, 0
-        ).astype(jnp.bfloat16)
-        out_ref[here, 3 * HD :] = dot(
-            turned_weights_ref[here, after], out_grads[after], 1, 0
-        ).astype(jnp.bfloat16)
-        span = pl.ds(window * size, size)
+        key_grads = dot(turned_grads, part_rows(rows_ref, 1, first, HEADS), 1, 0)
+        put_rows(out_ref, 2, first, last, key_grads, readers)
+        value_grads = dot(turned_weights_ref[here, after], out_grads[after], 1, 0)
+        put_rows(out_ref, 3, first, last, value_grads, readers)
+        span = pl.ds(first * size, STEP * size)
         stores.append(
-            pltpu.make_async_copy(out_ref.at[span], out_hbm.at[span], store_sems.at[window])
+            pltpu.make_async_copy(out_ref.at[span], out_hbm.at[span], store_sems.at[first])
         )
         stores[-1].start()
     for step, layer_ref in enumerate(layer_refs):
@@ -520,7 +545,7 @@
         chunks = []
         for owner in range(readers):
             dp_index, ctx_index = device_of(owner, head)
-            start = (ctx_index * readers + dp_index) * per_pair
+            start = chunk_of(dp_index, ctx_index, readers) * per_pair
             chunks.append(returned_ref[start : start + per_pair])
         heads.append(jnp.concatenate(chunks, axis=0))
     half = slots // 2
@@ -549,6 +574,17 @@
             pair = (dp_index * width + ctx_index, to_dp * width + to_ctx)
             pairs.append(pair[::-1] if back else pair)
     return lax.ppermute(value, ("dp", "ctx"), pairs)
+
+
+def exchange(chunks):
+    readers, width = lax.axis_size("dp"), lax.axis_size("ctx")
+    order = [None] * (readers * width)
+    for dp_index in range(readers):
+        for ctx_index in range(width):
+            order[chunk_of(dp_index, ctx_index, readers)] = dp_index * width + ctx_index
+    return lax.all_to_all(
+        chunks, ("dp", "ctx"), split_axis=0, concat_axis=0, tiled=True, axis_index_groups=[order]
+    )
 
 
 def swap(value, dp_bits, ctx_bits):
@@ -594,7 +630,7 @@
         ],
         name="slot_rows",
     )(owner_of, user_of.reshape(1, slots), proj_read)
-    rows = lax.all_to_all(outgoing, ("ctx", "dp"), split_axis=0, concat_axis=0, tiled=True)
+    rows = exchange(outgoing)
     *pieces, back = pl.pallas_call(
         columns_kernel,
         out_shape=(piece_shape,) * HEADS + (jax.ShapeDtypeStruct((slots, slots), jnp.bfloat16),),
@@ -651,7 +687,7 @@
         compiler_params=LIMIT,
         name="backward",
     )(rows, grads, gain, attended, *slopes, *all_stats)
-    returned = lax.all_to_all(results[0], ("ctx", "dp"), split_axis=0, concat_axis=0, tiled=True)
+    returned = exchange(results[0])
     layer_shape, grad_shape = (slots, HEADS * HD), (slots, 4 * HEADS * HD)
     return pl.pallas_call(
         functools.partial(unslot_kernel, per_pair=per_pair),

time: 56.1 us -> 54 us (0.963)
  waiting for transfers between devices: 22.7 us -> 20.8 us
  starting transfers between devices: 23.5 us -> 24.3 us
    ppermute x11, waiting for transfers between devices: 7.99 us -> 7 us  [send(): return lax.ppermute(value, ('dp', 'ctx'), pairs)]
    all_to_all x2, waiting for transfers between devices: 14.7 us -> 13.8 us  [exchange(): lax.all_to_all(chunks, ('dp', 'ctx'), split_axis=0, concat_axis=0, tiled=...]
    all_to_all x2, starting transfers between devices: 10.6 us -> 11.5 us  [exchange(): lax.all_to_all(chunks, ('dp', 'ctx'), split_axis=0, concat_axis=0, tiled=...]
where the time goes in v4:
time: 54 us; the launch traced here: 53.7 us
  starting transfers between devices  24.3 us (45%)
  waiting for transfers between devices  20.8 us (39%)
  Pallas kernels  7.13 us (13%)
  between operations  0.76 us (1%)
  local copies, waits for them, and re-layouts  0.73 us (1%)
    all_to_all x2, waiting for transfers between devices, exchange(): lax.all_to_all(chunks, ('dp', 'ctx'), split_axis=0, concat_axis=0, tiled=...  13.8 us
    ppermute x11, starting transfers between devices, send(): return lax.ppermute(value, ('dp', 'ctx'), pairs)  12.9 us
    all_to_all x2, starting transfers between devices, exchange(): lax.all_to_all(chunks, ('dp', 'ctx'), split_axis=0, concat_axis=0, tiled=...  11.5 us
    ppermute x11, waiting for transfers between devices, send(): return lax.ppermute(value, ('dp', 'ctx'), pairs)  7 us
    pallas_call x1, Pallas kernels, by_heads(): pl.pallas_call(functools.partial(slot_kernel, per_pair=per_pair), out_sha...  2.29 us
    pallas_call x1, Pallas kernels, by_heads(): pl.pallas_call(backward_kernel, out_shape=(jax.ShapeDtypeStruct((group_ro...  2.17 us
  transfers between devices with their start and end apart: 13, of which 11 were waited for; matrix products, arithmetic and copies ran while one was open for 0% of the time, Pallas kernels for 2%

profile of v4, /device:TPU:1, one launch (start us, length us, event | category | flops | bytes accessed | tf_op | source)
XLA Modules:
  0.0 53.7 jit_solution(15877737774242479238)
XLA Ops:
  0.6 2.3 %slot_rows.1 = (bf16[32,72,128]{2,1,0:T(8,128)(2,1)}, s32[1,128]{1,0:T(1,128)}) custom-call(s32[16]{0:T(128)} %owner_hbm.1, s32[1,128]{1,0:T(1,128)} %bitcast.6, bf16[128,2048]{1,0:T(8,128)(2,1)} %proj_hbm.1), custom_call_target="tpu_custom_call" | custom-call | tf_op jit(solution)/shard_map/slot_rows/pallas_call | solution.py:614
  3.0 7.1 %all-to-all-start = ((bf16[32,72,128]{2,1,0:T(8,128)(2,1)}), bf16[32,72,128]{2,1,0:T(8,128)(2,1)S(1)}, u32[]{:S(2)}, u32[]{:S(2)}) async-start(bf16[32,72,128]{2,1,0:T(8,128)(2,1)} %get-tuple-element.23), calls=%async_computation | async-start | bytes 1179648 | tf_op jit(solution)/shard_map/all_to_all | solution.py:585
  10.1 0.6 %copy-done.2 = s32[1,128]{1,0:T(1,128)S(1)} copy-done((s32[1,128]{1,0:T(1,128)S(1)}, s32[1,128]{1,0:T(1,128)}, u32[]{:S(2)}) %copy-start.2) | copy-done | bytes 536
  10.7 0.1 cut_columns.1
  10.8 3.5 %collective-permute-start = (bf16[128,128]{1,0:T(8,128)(2,1)S(1)}, bf16[128,128]{1,0:T(8,128)(2,1)S(1)}, u32[]{:S(2)}, u32[]{:S(2)}) collective-permute-start(bf16[128,128]{1,0:T(8,128)(2,1)S(1)} %get-tuple-element.24), channel_id=1, source_target_pairs={{0,0},{1,1},{2,4},{3,5},{4,2},{5,3},{6,6},{7,7},{8,8},{9,9},{10,12... | collective-permute-start | bytes 98312 | tf_op jit(solution)/shard_map/ppermute | solution.py:576
  14.4 0.0 collective-permute-start.1
  14.4 1.3 %collective-permute-start.2 = (bf16[128,128]{1,0:T(8,128)(2,1)S(1)}, bf16[128,128]{1,0:T(8,128)(2,1)S(1)}, u32[]{:S(2)}, u32[]{:S(2)}) collective-permute-start(bf16[128,128]{1,0:T(8,128)(2,1)S(1)} %get-tuple-element.26), channel_id=1, source_target_pairs={{0,1},{1,0},{2,5},{3,4},{4,3},{5,2},{6,7},{7,6},{8,9},{9,8},{10,13... | collective-permute-start | bytes 98312 | tf_op jit(solution)/shard_map/ppermute | solution.py:576
  15.7 0.1 collective-permute-start.3
  15.8 0.1 dynamic-slice_bitcast_fusion.gain_ref
  15.9 0.8 %collective-permute-done.refs_0_ = bf16[128,128]{1,0:T(8,128)(2,1)S(1)} collective-permute-done((bf16[128,128]{1,0:T(8,128)(2,1)S(1)}, bf16[128,128]{1,0:T(8,128)(2,1)S(1)}, u32[]{:S(2)}, u32[]{:S(2)}) %collective-permute-start) | collective-permute-done | bytes 32800 | tf_op jit(solution)/shard_map/ppermute | solution.py:576
  16.7 0.4 collective-permute-done.1.refs_1_
  17.1 2.0 %collective-permute-done.2.refs_2_ = bf16[128,128]{1,0:T(8,128)(2,1)S(1)} collective-permute-done((bf16[128,128]{1,0:T(8,128)(2,1)S(1)}, bf16[128,128]{1,0:T(8,128)(2,1)S(1)}, u32[]{:S(2)}, u32[]{:S(2)}) %collective-permute-start.2) | collective-permute-done | bytes 32800 | tf_op jit(solution)/shard_map/ppermute | solution.py:576
  19.1 0.4 collective-permute-done.3.refs_3_
  19.5 7.2 %all-to-all-done.rows_ref = bf16[32,72,128]{2,1,0:T(8,128)(2,1)S(1)} async-done(((bf16[32,72,128]{2,1,0:T(8,128)(2,1)}), bf16[32,72,128]{2,1,0:T(8,128)(2,1)S(1)}, u32[]{:S(2)}, u32[]{:S(2)}) %all-to-all-start) | async-done | bytes 589856 | tf_op jit(solution)/shard_map/all_to_all | solution.py:585
  26.8 0.7 %forward.1 = (f32[512,128]{1,0:T(8,128)S(1)}, f32[8,512]{1,0:T(8,128)S(1)}) custom-call(bf16[32,72,128]{2,1,0:T(8,128)(2,1)S(1)} %all-to-all-done.rows_ref, bf16[512,128]{1,0:T(8,128)(2,1)S(1)} %lay_group.1.grads_ref, f32[1,128]{1,0:T(1,128)S(1)} %dynamic-slice_bitcast_fusion.gain_ref), custom_call_target="tpu_custom_call" | custom-call | tf_op jit(solution)/shard_map/forward/pallas_call | solution.py:650
  27.5 0.4 collective-permute-start.6
  27.8 1.0 %collective-permute-start.5 = (f32[8,512]{1,0:T(8,128)S(1)}, f32[8,512]{1,0:T(8,128)S(1)}, u32[]{:S(2)}, u32[]{:S(2)}) collective-permute-start(f32[8,512]{1,0:T(8,128)S(1)} %get-tuple-element.34.refs_0_), channel_id=1, source_target_pairs={{0,1},{1,0},{2,3},{3,2},{4,5},{5,4},{6,7},{7,6},{8,9},{9,8},{10,11... | collective-permute-start | bytes 49160 | tf_op jit(solution)/shard_map/ppermute | solution.py:576
  28.8 0.9 %collective-permute-start.4 = (f32[8,512]{1,0:T(8,128)S(1)}, f32[8,512]{1,0:T(8,128)S(1)}, u32[]{:S(2)}, u32[]{:S(2)}) collective-permute-start(f32[8,512]{1,0:T(8,128)S(1)} %get-tuple-element.34.refs_0_), channel_id=1, source_target_pairs={{0,4},{1,5},{2,6},{3,7},{4,0},{5,1},{6,2},{7,3},{8,12},{9,13},{10,... | collective-permute-start | bytes 49160 | tf_op jit(solution)/shard_map/ppermute | solution.py:576
  29.7 0.8 %slopes.1 = (f32[512,512]{1,0:T(8,128)S(1)}, f32[512,512]{1,0:T(8,128)S(1)}, bf16[512,512]{1,0:T(8,128)(2,1)S(1)}) custom-call(bf16[32,72,128]{2,1,0:T(8,128)(2,1)S(1)} %all-to-all-done.rows_ref), custom_call_target="tpu_custom_call" | custom-call | tf_op jit(solution)/shard_map/slopes/pallas_call | solution.py:662
  30.5 0.2 collective-permute-done.6.refs_3_
  30.7 2.2 %backward.1 = (bf16[512,512]{1,0:T(8,128)(2,1)}, bf16[128,128]{1,0:T(8,128)(2,1)S(1)}, bf16[128,128]{1,0:T(8,128)(2,1)S(1)}, bf16[128,128]{1,0:T(8,128)(2,1)S(1)}, bf16[128,128]{1,0:T(8,128)(2,1)S(1)}) custom-call(bf16[32,72,128]{2,1,0:T(8,128)(2,1)S(1)} %all-to-all-done.rows_ref, bf16[512,128]{1,0:T(8,128)(2,1)S(1)} %lay_group.1.grads_ref, ...), custom_call_target="tpu_custom_call" | custom-call | tf_op jit(solution)/shard_map/backward/pallas_call | solution.py:675
  32.9 4.4 %all-to-all-start.1 = ((bf16[32,16,512]{2,1,0:T(8,128)(2,1)}), bf16[32,16,512]{2,1,0:T(8,128)(2,1)S(1)}, u32[]{:S(2)}, u32[]{:S(2)}) async-start(bf16[32,16,512]{2,1,0:T(8,128)(2,1)} %bitcast.2), calls=%async_computation.1 | async-start | bytes 1048576 | tf_op jit(solution)/shard_map/all_to_all | solution.py:585
  37.3 3.6 %collective-permute-start.7 = (bf16[128,128]{1,0:T(8,128)(2,1)S(1)}, bf16[128,128]{1,0:T(8,128)(2,1)S(1)}, u32[]{:S(2)}, u32[]{:S(2)}) collective-permute-start(bf16[128,128]{1,0:T(8,128)(2,1)S(1)} %get-tuple-element.36), channel_id=1, source_target_pairs={{0,0},{1,1},{4,2},{5,3},{2,4},{3,5},{6,6},{7,7},{8,8},{9,9},{12,10... | collective-permute-start | bytes 98312 | tf_op jit(solution)/shard_map/ppermute | solution.py:576
  40.8 0.0 collective-permute-start.8
  40.9 1.3 %collective-permute-start.9 = (bf16[128,128]{1,0:T(8,128)(2,1)S(1)}, bf16[128,128]{1,0:T(8,128)(2,1)S(1)}, u32[]{:S(2)}, u32[]{:S(2)}) collective-permute-start(bf16[128,128]{1,0:T(8,128)(2,1)S(1)} %get-tuple-element.38), channel_id=1, source_target_pairs={{1,0},{0,1},{5,2},{4,3},{3,4},{2,5},{7,6},{6,7},{9,8},{8,9},{13,10... | collective-permute-start | bytes 98312 | tf_op jit(solution)/shard_map/ppermute | solution.py:576
  42.1 0.8 %collective-permute-start.10 = (bf16[128,128]{1,0:T(8,128)(2,1)S(1)}, bf16[128,128]{1,0:T(8,128)(2,1)S(1)}, u32[]{:S(2)}, u32[]{:S(2)}) collective-permute-start(bf16[128,128]{1,0:T(8,128)(2,1)S(1)} %get-tuple-element.39), channel_id=1, source_target_pairs={{5,0},{4,1},{1,2},{0,3},{7,4},{6,5},{3,6},{2,7},{13,8},{12,9},{9,1... | collective-permute-start | bytes 98312 | tf_op jit(solution)/shard_map/ppermute | solution.py:576
  43.0 0.6 %collective-permute-done.7.refs_0_ = bf16[128,128]{1,0:T(8,128)(2,1)S(1)} collective-permute-done((bf16[128,128]{1,0:T(8,128)(2,1)S(1)}, bf16[128,128]{1,0:T(8,128)(2,1)S(1)}, u32[]{:S(2)}, u32[]{:S(2)}) %collective-permute-start.7) | collective-permute-done | bytes 32800 | tf_op jit(solution)/shard_map/ppermute | solution.py:576
  43.6 0.7 %collective-permute-done.8.refs_1_ = bf16[128,128]{1,0:T(8,128)(2,1)S(1)} collective-permute-done((bf16[128,128]{1,0:T(8,128)(2,1)S(1)}, bf16[128,128]{1,0:T(8,128)(2,1)S(1)}, u32[]{:S(2)}, u32[]{:S(2)}) %collective-permute-start.8) | collective-permute-done | bytes 32800 | tf_op jit(solution)/shard_map/ppermute | solution.py:576
  44.3 1.6 %collective-permute-done.9.refs_2_ = bf16[128,128]{1,0:T(8,128)(2,1)S(1)} collective-permute-done((bf16[128,128]{1,0:T(8,128)(2,1)S(1)}, bf16[128,128]{1,0:T(8,128)(2,1)S(1)}, u32[]{:S(2)}, u32[]{:S(2)}) %collective-permute-start.9) | collective-permute-done | bytes 32800 | tf_op jit(solution)/shard_map/ppermute | solution.py:576
  45.9 0.2 collective-permute-done.10.refs_3_
  46.2 6.5 %all-to-all-done.1 = bf16[32,16,512]{2,1,0:T(8,128)(2,1)S(1)} async-done(((bf16[32,16,512]{2,1,0:T(8,128)(2,1)}), bf16[32,16,512]{2,1,0:T(8,128)(2,1)S(1)}, u32[]{:S(2)}, u32[]{:S(2)}) %all-to-all-start.1) | async-done | bytes 524320 | tf_op jit(solution)/shard_map/all_to_all | solution.py:585
  52.7 1.0 %unslot_rows.1 = (bf16[128,512]{1,0:T(8,128)(2,1)}, bf16[128,2048]{1,0:T(8,128)(2,1)}) custom-call(bf16[128,128]{1,0:T(8,128)(2,1)S(1)} %get-tuple-element.22.back_ref, bf16[512,512]{1,0:T(8,128)(2,1)S(1)} %bitcast.5, bf16[128,128]{1,0:T(8,128)(2,1)S(1)} %collective-permute-done.7.refs_0_, bf16[128,128]{1,0:T(8,128)(2,1)S(1)} %collective-permute-done.8.refs_1_, ...), custom_call_target="tpu_custom_call" | custom-call | tf_op jit(solution)/shard_map/unslot_rows/pallas_call | solution.py:692
  (8 shorter events, 0.0 us)
Async XLA Ops:
  0.6 15.2 %copy-start = (f32[512]{0:T(512)S(1)}, f32[512]{0:T(512)}, u32[]{:S(2)}) copy-start(f32[512]{0:T(512)} %param.6) | copy-start | bytes 6148
  2.9 7.1 %copy-start.1 = (bf16[128,512]{1,0:T(8,128)(2,1)S(1)}, bf16[128,512]{1,0:T(8,128)(2,1)}, u32[]{:S(2)}) copy-start(bf16[128,512]{1,0:T(8,128)(2,1)} %grad_ref.1) | copy-start | bytes 393220
  3.0 23.8 %all-to-all-start = ((bf16[32,72,128]{2,1,0:T(8,128)(2,1)}), bf16[32,72,128]{2,1,0:T(8,128)(2,1)S(1)}, u32[]{:S(2)}, u32[]{:S(2)}) async-start(bf16[32,72,128]{2,1,0:T(8,128)(2,1)} %get-tuple-element.23), calls=%async_computation | async-start | bytes 1179648 | tf_op jit(solution)/shard_map/all_to_all | solution.py:585
  10.1 0.7 %copy-start.2 = (s32[1,128]{1,0:T(1,128)S(1)}, s32[1,128]{1,0:T(1,128)}, u32[]{:S(2)}) copy-start(s32[1,128]{1,0:T(1,128)} %get-tuple-element.21.slot_ref) | copy-start | bytes 1540
  10.8 5.9 %collective-permute-start = (bf16[128,128]{1,0:T(8,128)(2,1)S(1)}, bf16[128,128]{1,0:T(8,128)(2,1)S(1)}, u32[]{:S(2)}, u32[]{:S(2)}) collective-permute-start(bf16[128,128]{1,0:T(8,128)(2,1)S(1)} %get-tuple-element.24), channel_id=1, source_target_pairs={{0,0},{1,1},{2,4},{3,5},{4,2},{5,3},{6,6},{7,7},{8,8},{9,9},{10,12... | collective-permute-start | bytes 98312 | tf_op jit(solution)/shard_map/ppermute | solution.py:576
  14.4 2.7 %collective-permute-start.1 = (bf16[128,128]{1,0:T(8,128)(2,1)S(1)}, bf16[128,128]{1,0:T(8,128)(2,1)S(1)}, u32[]{:S(2)}, u32[]{:S(2)}) collective-permute-start(bf16[128,128]{1,0:T(8,128)(2,1)S(1)} %get-tuple-element.25), channel_id=1, source_target_pairs={{0,4},{1,5},{2,0},{3,1},{4,6},{5,7},{6,2},{7,3},{8,12},{9,13},{10,... | collective-permute-start | bytes 98312 | tf_op jit(solution)/shard_map/ppermute | solution.py:576
  14.4 4.7 %collective-permute-start.2 = (bf16[128,128]{1,0:T(8,128)(2,1)S(1)}, bf16[128,128]{1,0:T(8,128)(2,1)S(1)}, u32[]{:S(2)}, u32[]{:S(2)}) collective-permute-start(bf16[128,128]{1,0:T(8,128)(2,1)S(1)} %get-tuple-element.26), channel_id=1, source_target_pairs={{0,1},{1,0},{2,5},{3,4},{4,3},{5,2},{6,7},{7,6},{8,9},{9,8},{10,13... | collective-permute-start | bytes 98312 | tf_op jit(solution)/shard_map/ppermute | solution.py:576
  15.7 3.8 %collective-permute-start.3 = (bf16[128,128]{1,0:T(8,128)(2,1)S(1)}, bf16[128,128]{1,0:T(8,128)(2,1)S(1)}, u32[]{:S(2)}, u32[]{:S(2)}) collective-permute-start(bf16[128,128]{1,0:T(8,128)(2,1)S(1)} %get-tuple-element.27), channel_id=1, source_target_pairs={{0,5},{1,4},{2,1},{3,0},{4,7},{5,6},{6,3},{7,2},{8,13},{9,12},{10,... | collective-permute-start | bytes 98312 | tf_op jit(solution)/shard_map/ppermute | solution.py:576
  27.5 3.2 %collective-permute-start.6 = (f32[8,512]{1,0:T(8,128)S(1)}, f32[8,512]{1,0:T(8,128)S(1)}, u32[]{:S(2)}, u32[]{:S(2)}) collective-permute-start(f32[8,512]{1,0:T(8,128)S(1)} %get-tuple-element.34.refs_0_), channel_id=1, source_target_pairs={{0,5},{1,4},{2,7},{3,6},{4,1},{5,0},{6,3},{7,2},{8,13},{9,12},{10,... | collective-permute-start | bytes 49160 | tf_op jit(solution)/shard_map/ppermute | solution.py:576
  27.8 2.9 %collective-permute-start.5 = (f32[8,512]{1,0:T(8,128)S(1)}, f32[8,512]{1,0:T(8,128)S(1)}, u32[]{:S(2)}, u32[]{:S(2)}) collective-permute-start(f32[8,512]{1,0:T(8,128)S(1)} %get-tuple-element.34.refs_0_), channel_id=1, source_target_pairs={{0,1},{1,0},{2,3},{3,2},{4,5},{5,4},{6,7},{7,6},{8,9},{9,8},{10,11... | collective-permute-start | bytes 49160 | tf_op jit(solution)/shard_map/ppermute | solution.py:576
  28.8 1.9 %collective-permute-start.4 = (f32[8,512]{1,0:T(8,128)S(1)}, f32[8,512]{1,0:T(8,128)S(1)}, u32[]{:S(2)}, u32[]{:S(2)}) collective-permute-start(f32[8,512]{1,0:T(8,128)S(1)} %get-tuple-element.34.refs_0_), channel_id=1, source_target_pairs={{0,4},{1,5},{2,6},{3,7},{4,0},{5,1},{6,2},{7,3},{8,12},{9,13},{10,... | collective-permute-start | bytes 49160 | tf_op jit(solution)/shard_map/ppermute | solution.py:576
  32.9 19.8 %all-to-all-start.1 = ((bf16[32,16,512]{2,1,0:T(8,128)(2,1)}), bf16[32,16,512]{2,1,0:T(8,128)(2,1)S(1)}, u32[]{:S(2)}, u32[]{:S(2)}) async-start(bf16[32,16,512]{2,1,0:T(8,128)(2,1)} %bitcast.2), calls=%async_computation.1 | async-start | bytes 1048576 | tf_op jit(solution)/shard_map/all_to_all | solution.py:585
  37.3 6.3 %collective-permute-start.7 = (bf16[128,128]{1,0:T(8,128)(2,1)S(1)}, bf16[128,128]{1,0:T(8,128)(2,1)S(1)}, u32[]{:S(2)}, u32[]{:S(2)}) collective-permute-start(bf16[128,128]{1,0:T(8,128)(2,1)S(1)} %get-tuple-element.36), channel_id=1, source_target_pairs={{0,0},{1,1},{4,2},{5,3},{2,4},{3,5},{6,6},{7,7},{8,8},{9,9},{12,10... | collective-permute-start | bytes 98312 | tf_op jit(solution)/shard_map/ppermute | solution.py:576
  40.8 3.5 %collective-permute-start.8 = (bf16[128,128]{1,0:T(8,128)(2,1)S(1)}, bf16[128,128]{1,0:T(8,128)(2,1)S(1)}, u32[]{:S(2)}, u32[]{:S(2)}) collective-permute-start(bf16[128,128]{1,0:T(8,128)(2,1)S(1)} %get-tuple-element.37), channel_id=1, source_target_pairs={{4,0},{5,1},{0,2},{1,3},{6,4},{7,5},{2,6},{3,7},{12,8},{13,9},{8,1... | collective-permute-start | bytes 98312 | tf_op jit(solution)/shard_map/ppermute | solution.py:576
  40.9 5.1 %collective-permute-start.9 = (bf16[128,128]{1,0:T(8,128)(2,1)S(1)}, bf16[128,128]{1,0:T(8,128)(2,1)S(1)}, u32[]{:S(2)}, u32[]{:S(2)}) collective-permute-start(bf16[128,128]{1,0:T(8,128)(2,1)S(1)} %get-tuple-element.38), channel_id=1, source_target_pairs={{1,0},{0,1},{5,2},{4,3},{3,4},{2,5},{7,6},{6,7},{9,8},{8,9},{13,10... | collective-permute-start | bytes 98312 | tf_op jit(solution)/shard_map/ppermute | solution.py:576
  42.1 4.0 %collective-permute-start.10 = (bf16[128,128]{1,0:T(8,128)(2,1)S(1)}, bf16[128,128]{1,0:T(8,128)(2,1)S(1)}, u32[]{:S(2)}, u32[]{:S(2)}) collective-permute-start(bf16[128,128]{1,0:T(8,128)(2,1)S(1)} %get-tuple-element.39), channel_id=1, source_target_pairs={{5,0},{4,1},{1,2},{0,3},{7,4},{6,5},{3,6},{2,7},{13,8},{12,9},{9,1... | collective-permute-start | bytes 98312 | tf_op jit(solution)/shard_map/ppermute | solution.py:576

commit v5 on v4

--- a/solution.py
+++ b/solution.py
@@ -208,7 +208,14 @@
     return (owner & ~1) | (head & 1), ((owner & 1) << 1) | (head >> 1)
 
 
+SPANS = (3, 1, 2, 0)
+
+
 def chunk_of(dp_index, ctx_index, readers):
+    return turned(ctx_index) * readers + SPANS[dp_index >> 1] * 2 + (dp_index & 1)
+
+
+def chunk_back(dp_index, ctx_index, readers):
     return ctx_index * readers + (dp_index & 1) * (readers // 2) + (dp_index >> 1)
 
 
@@ -321,7 +328,7 @@
                         owner * per_pair : (owner + 1) * per_pair, side * HD : (side + 1) * HD
                     ]
         for ctx_index in (half, 2 + half):
-            span = pl.ds(ctx_index * readers, readers)
+            span = pl.ds(turned(ctx_index) * readers, readers)
             stores.append(
                 pltpu.make_async_copy(
                     send_ref.at[span], send_hbm.at[span], store_sems.at[ctx_index]
@@ -370,7 +377,7 @@
     for window in range(first, last):
         for reader in range(readers):
             source = ((window - first) * readers + reader) * per_pair
-            target = chunk_of(reader, window, readers) * per_pair
+            target = chunk_back(reader, window, readers) * per_pair
             out_ref[target : target + per_pair, part * HD : (part + 1) * HD] = rows[
                 source : source + per_pair
             ].astype(jnp.bfloat16)
@@ -379,7 +386,8 @@
 def window_users(rows_ref, window):
     readers = rows_ref.shape[0] // HEADS
     per_pair = HD // readers
-    tags = rows_ref[window * readers : (window + 1) * readers, 4 * per_pair :, :]
+    first = turned(window) * readers
+    tags = rows_ref[first : first + readers, 4 * per_pair :, :]
     return jnp.sum(tags.astype(jnp.float32), axis=0)[:1]
 
 
@@ -465,7 +473,7 @@
     stats_refs = refs[:HEADS]
     out_hbm = refs[HEADS]
     layer_refs = refs[HEADS + 1 : 2 * HEADS + 1]
-    layer_all, out_ref, out_grads, store_sems = refs[2 * HEADS + 1 :]
+    layer_all, out_ref, store_sems = refs[2 * HEADS + 1 :]
     head = my_place()[0]
     readers = rows_ref.shape[0] // HEADS
     size = HD
@@ -478,6 +486,7 @@
     cross = sum(stat[3:4] + (stat[0:1] - mean) * stat[2:3] for stat in stats)
     mean_cross = cross * inv_std / width
     row = lax.broadcasted_iota(jnp.int32, (size, size), 0)
+    out_grads = []
     for window in range(HEADS):
         here = slice(window * size, (window + 1) * size)
         packed = jnp.where(
@@ -494,9 +503,10 @@
         normed = (attended_ref[here] - packed[:, 0:1]) * packed[:, 1:2]
         layer_all[here] = (normed * gain_ref[...] * unit).astype(jnp.bfloat16)
         put_rows(out_ref, 0, window, window + 1, grad_gain * normed, readers)
-        out_grads[here] = (
+        out_grads.append(
             packed[:, 1:2] * (grad_gain * unit - packed[:, 2:3] - normed * packed[:, 3:4])
-        ).astype(jnp.bfloat16)
+        )
+    out_grads = jnp.concatenate(out_grads, axis=0).astype(jnp.bfloat16)
     stores = []
     for first in range(0, HEADS, STEP):
         last = first + STEP
@@ -516,11 +526,12 @@
         put_rows(out_ref, 2, first, last, key_grads, readers)
         value_grads = dot(turned_weights_ref[here, after], out_grads[after], 1, 0)
         put_rows(out_ref, 3, first, last, value_grads, readers)
-        span = pl.ds(first * size, STEP * size)
-        stores.append(
-            pltpu.make_async_copy(out_ref.at[span], out_hbm.at[span], store_sems.at[first])
-        )
-        stores[-1].start()
+        for window in range(first, last):
+            span = pl.ds(window * size, size)
+            stores.append(
+                pltpu.make_async_copy(out_ref.at[span], out_hbm.at[span], store_sems.at[window])
+            )
+            stores[-1].start()
     for step, layer_ref in enumerate(layer_refs):
         start = pl.multiple_of(turned(head ^ step) * size, size)
         layer_ref[...] = layer_all[pl.ds(start, size), :]
@@ -545,7 +556,7 @@
         chunks = []
         for owner in range(readers):
             dp_index, ctx_index = device_of(owner, head)
-            start = chunk_of(dp_index, ctx_index, readers) * per_pair
+            start = chunk_back(dp_index, ctx_index, readers) * per_pair
             chunks.append(returned_ref[start : start + per_pair])
         heads.append(jnp.concatenate(chunks, axis=0))
     half = slots // 2
@@ -576,12 +587,12 @@
     return lax.ppermute(value, ("dp", "ctx"), pairs)
 
 
-def exchange(chunks):
+def exchange(chunks, place):
     readers, width = lax.axis_size("dp"), lax.axis_size("ctx")
     order = [None] * (readers * width)
     for dp_index in range(readers):
         for ctx_index in range(width):
-            order[chunk_of(dp_index, ctx_index, readers)] = dp_index * width + ctx_index
+            order[place(dp_index, ctx_index, readers)] = dp_index * width + ctx_index
     return lax.all_to_all(
         chunks, ("dp", "ctx"), split_axis=0, concat_axis=0, tiled=True, axis_index_groups=[order]
     )
@@ -630,7 +641,7 @@
         ],
         name="slot_rows",
     )(owner_of, user_of.reshape(1, slots), proj_read)
-    rows = exchange(outgoing)
+    rows = exchange(outgoing, chunk_of)
     *pieces, back = pl.pallas_call(
         columns_kernel,
         out_shape=(piece_shape,) * HEADS + (jax.ShapeDtypeStruct((slots, slots), jnp.bfloat16),),
@@ -681,13 +692,12 @@
         scratch_shapes=[
             pltpu.VMEM((group_rows, HD), jnp.bfloat16),
             pltpu.VMEM((group_rows, width), jnp.bfloat16),
-            pltpu.VMEM((group_rows, HD), jnp.bfloat16),
             pltpu.SemaphoreType.DMA((HEADS,)),
         ],
         compiler_params=LIMIT,
         name="backward",
     )(rows, grads, gain, attended, *slopes, *all_stats)
-    returned = exchange(results[0])
+    returned = exchange(results[0], chunk_back)
     layer_shape, grad_shape = (slots, HEADS * HD), (slots, 4 * HEADS * HD)
     return pl.pallas_call(
         functools.partial(unslot_kernel, per_pair=per_pair),
@@ -710,5 +720,6 @@
 def solution(mesh):
     in_specs = (P(("dp", "ctx"), None), P(), P(), P(("dp", "ctx")), P(("dp", "ctx"), None))
     out_specs = (P(("dp", "ctx"), None), P(("dp", "ctx"), None))
-    local = by_heads if mesh.shape["ctx"] == HEADS else windowed
+    fits = mesh.shape["ctx"] == HEADS and mesh.shape["dp"] == 2 * len(SPANS)
+    local = by_heads if fits else windowed
     return jax.shard_map(local, mesh=mesh, in_specs=in_specs, out_specs=out_specs, check_vma=False)

time: 54 us -> 53.3 us (0.987)
  starting transfers between devices: 24.3 us -> 23 us
  waiting for transfers between devices: 20.8 us -> 21.4 us
    ppermute x11, waiting for transfers between devices: 7 us -> 9.07 us  [send(): return lax.ppermute(value, ('dp', 'ctx'), pairs)]
    all_to_all x2, starting transfers between devices: 11.5 us -> 9.7 us  [exchange(): lax.all_to_all(chunks, ('dp', 'ctx'), split_axis=0, concat_axis=0, tiled=...]
    all_to_all x2, waiting for transfers between devices: 13.8 us -> 12.4 us  [exchange(): lax.all_to_all(chunks, ('dp', 'ctx'), split_axis=0, concat_axis=0, tiled=...]
where the time goes in v5:
time: 53.3 us; the launch traced here: 53 us
  starting transfers between devices  23 us (43%)
  waiting for transfers between devices  21.4 us (40%)
  Pallas kernels  7.08 us (13%)
  between operations  0.76 us (1%)
  local copies, waits for them, and re-layouts  0.73 us (1%)
    ppermute x11, starting transfers between devices, send(): return lax.ppermute(value, ('dp', 'ctx'), pairs)  13.3 us
    all_to_all x2, waiting for transfers between devices, exchange(): lax.all_to_all(chunks, ('dp', 'ctx'), split_axis=0, concat_axis=0, tiled=...  12.4 us
    all_to_all x2, starting transfers between devices, exchange(): lax.all_to_all(chunks, ('dp', 'ctx'), split_axis=0, concat_axis=0, tiled=...  9.7 us
    ppermute x11, waiting for transfers between devices, send(): return lax.ppermute(value, ('dp', 'ctx'), pairs)  9.07 us
    pallas_call x1, Pallas kernels, by_heads(): pl.pallas_call(functools.partial(slot_kernel, per_pair=per_pair), out_sha...  2.29 us
    pallas_call x1, Pallas kernels, by_heads(): pl.pallas_call(backward_kernel, out_shape=(jax.ShapeDtypeStruct((group_ro...  2.12 us
  transfers between devices with their start and end apart: 13, of which 11 were waited for; matrix products, arithmetic and copies ran while one was open for 0% of the time, Pallas kernels for 2%

profile of v5, /device:TPU:1, one launch (start us, length us, event | category | flops | bytes accessed | tf_op | source)
XLA Modules:
  0.0 53.0 jit_solution(1095966010879088834)
XLA Ops:
  0.6 2.3 %slot_rows.1 = (bf16[32,72,128]{2,1,0:T(8,128)(2,1)}, s32[1,128]{1,0:T(1,128)}) custom-call(s32[16]{0:T(128)} %owner_hbm.1, s32[1,128]{1,0:T(1,128)} %bitcast.6, bf16[128,2048]{1,0:T(8,128)(2,1)} %proj_hbm.1), custom_call_target="tpu_custom_call" | custom-call | tf_op jit(solution)/shard_map/slot_rows/pallas_call | solution.py:625
  3.0 7.1 %all-to-all-start = ((bf16[32,72,128]{2,1,0:T(8,128)(2,1)}), bf16[32,72,128]{2,1,0:T(8,128)(2,1)S(1)}, u32[]{:S(2)}, u32[]{:S(2)}) async-start(bf16[32,72,128]{2,1,0:T(8,128)(2,1)} %get-tuple-element.23), calls=%async_computation | async-start | bytes 1179648 | tf_op jit(solution)/shard_map/all_to_all | solution.py:596
  10.1 0.6 %copy-done.2 = s32[1,128]{1,0:T(1,128)S(1)} copy-done((s32[1,128]{1,0:T(1,128)S(1)}, s32[1,128]{1,0:T(1,128)}, u32[]{:S(2)}) %copy-start.2) | copy-done | bytes 536
  10.7 0.1 cut_columns.1
  10.8 3.5 %collective-permute-start = (bf16[128,128]{1,0:T(8,128)(2,1)S(1)}, bf16[128,128]{1,0:T(8,128)(2,1)S(1)}, u32[]{:S(2)}, u32[]{:S(2)}) collective-permute-start(bf16[128,128]{1,0:T(8,128)(2,1)S(1)} %get-tuple-element.24), channel_id=1, source_target_pairs={{0,0},{1,1},{2,4},{3,5},{4,2},{5,3},{6,6},{7,7},{8,8},{9,9},{10,12... | collective-permute-start | bytes 98312 | tf_op jit(solution)/shard_map/ppermute | solution.py:587
  14.4 0.0 collective-permute-start.1
  14.4 1.3 %collective-permute-start.2 = (bf16[128,128]{1,0:T(8,128)(2,1)S(1)}, bf16[128,128]{1,0:T(8,128)(2,1)S(1)}, u32[]{:S(2)}, u32[]{:S(2)}) collective-permute-start(bf16[128,128]{1,0:T(8,128)(2,1)S(1)} %get-tuple-element.26), channel_id=1, source_target_pairs={{0,1},{1,0},{2,5},{3,4},{4,3},{5,2},{6,7},{7,6},{8,9},{9,8},{10,13... | collective-permute-start | bytes 98312 | tf_op jit(solution)/shard_map/ppermute | solution.py:587
  15.7 0.1 collective-permute-start.3
  15.8 0.1 dynamic-slice_bitcast_fusion.gain_ref
  15.9 1.1 %collective-permute-done.refs_0_ = bf16[128,128]{1,0:T(8,128)(2,1)S(1)} collective-permute-done((bf16[128,128]{1,0:T(8,128)(2,1)S(1)}, bf16[128,128]{1,0:T(8,128)(2,1)S(1)}, u32[]{:S(2)}, u32[]{:S(2)}) %collective-permute-start) | collective-permute-done | bytes 32800 | tf_op jit(solution)/shard_map/ppermute | solution.py:587
  17.0 2.9 %collective-permute-done.2.refs_2_ = bf16[128,128]{1,0:T(8,128)(2,1)S(1)} collective-permute-done((bf16[128,128]{1,0:T(8,128)(2,1)S(1)}, bf16[128,128]{1,0:T(8,128)(2,1)S(1)}, u32[]{:S(2)}, u32[]{:S(2)}) %collective-permute-start.2) | collective-permute-done | bytes 32800 | tf_op jit(solution)/shard_map/ppermute | solution.py:587
  19.9 0.7 %collective-permute-done.3.refs_3_ = bf16[128,128]{1,0:T(8,128)(2,1)S(1)} collective-permute-done((bf16[128,128]{1,0:T(8,128)(2,1)S(1)}, bf16[128,128]{1,0:T(8,128)(2,1)S(1)}, u32[]{:S(2)}, u32[]{:S(2)}) %collective-permute-start.3) | collective-permute-done | bytes 32800 | tf_op jit(solution)/shard_map/ppermute | solution.py:587
  20.5 5.8 %all-to-all-done.rows_ref = bf16[32,72,128]{2,1,0:T(8,128)(2,1)S(1)} async-done(((bf16[32,72,128]{2,1,0:T(8,128)(2,1)}), bf16[32,72,128]{2,1,0:T(8,128)(2,1)S(1)}, u32[]{:S(2)}, u32[]{:S(2)}) %all-to-all-start) | async-done | bytes 589856 | tf_op jit(solution)/shard_map/all_to_all | solution.py:596
  26.4 0.7 %forward.1 = (f32[512,128]{1,0:T(8,128)S(1)}, f32[8,512]{1,0:T(8,128)S(1)}) custom-call(bf16[32,72,128]{2,1,0:T(8,128)(2,1)S(1)} %all-to-all-done.rows_ref, bf16[512,128]{1,0:T(8,128)(2,1)S(1)} %lay_group.1.grads_ref, f32[1,128]{1,0:T(1,128)S(1)} %dynamic-slice_bitcast_fusion.gain_ref), custom_call_target="tpu_custom_call" | custom-call | tf_op jit(solution)/shard_map/forward/pallas_call | solution.py:661
  27.1 2.2 %collective-permute-start.6 = (f32[8,512]{1,0:T(8,128)S(1)}, f32[8,512]{1,0:T(8,128)S(1)}, u32[]{:S(2)}, u32[]{:S(2)}) collective-permute-start(f32[8,512]{1,0:T(8,128)S(1)} %get-tuple-element.34.refs_0_), channel_id=1, source_target_pairs={{0,5},{1,4},{2,7},{3,6},{4,1},{5,0},{6,3},{7,2},{8,13},{9,12},{10,... | collective-permute-start | bytes 49160 | tf_op jit(solution)/shard_map/ppermute | solution.py:587
  29.3 0.3 collective-permute-start.5
  29.6 0.2 collective-permute-start.4
  29.8 0.8 %slopes.1 = (f32[512,512]{1,0:T(8,128)S(1)}, f32[512,512]{1,0:T(8,128)S(1)}, bf16[512,512]{1,0:T(8,128)(2,1)S(1)}) custom-call(bf16[32,72,128]{2,1,0:T(8,128)(2,1)S(1)} %all-to-all-done.rows_ref), custom_call_target="tpu_custom_call" | custom-call | tf_op jit(solution)/shard_map/slopes/pallas_call | solution.py:673
  30.6 0.5 %collective-permute-done.6.refs_3_ = f32[8,512]{1,0:T(8,128)S(1)} collective-permute-done((f32[8,512]{1,0:T(8,128)S(1)}, f32[8,512]{1,0:T(8,128)S(1)}, u32[]{:S(2)}, u32[]{:S(2)}) %collective-permute-start.6) | collective-permute-done | bytes 16416 | tf_op jit(solution)/shard_map/ppermute | solution.py:587
  31.1 0.8 %collective-permute-done.5.refs_2_ = f32[8,512]{1,0:T(8,128)S(1)} collective-permute-done((f32[8,512]{1,0:T(8,128)S(1)}, f32[8,512]{1,0:T(8,128)S(1)}, u32[]{:S(2)}, u32[]{:S(2)}) %collective-permute-start.5) | collective-permute-done | bytes 16416 | tf_op jit(solution)/shard_map/ppermute | solution.py:587
  31.9 2.1 %backward.1 = (bf16[512,512]{1,0:T(8,128)(2,1)}, bf16[128,128]{1,0:T(8,128)(2,1)S(1)}, bf16[128,128]{1,0:T(8,128)(2,1)S(1)}, bf16[128,128]{1,0:T(8,128)(2,1)S(1)}, bf16[128,128]{1,0:T(8,128)(2,1)S(1)}) custom-call(bf16[32,72,128]{2,1,0:T(8,128)(2,1)S(1)} %all-to-all-done.rows_ref, bf16[512,128]{1,0:T(8,128)(2,1)S(1)} %lay_group.1.grads_ref, ...), custom_call_target="tpu_custom_call" | custom-call | tf_op jit(solution)/shard_map/backward/pallas_call | solution.py:686
  34.0 2.6 %all-to-all-start.1 = ((bf16[32,16,512]{2,1,0:T(8,128)(2,1)}), bf16[32,16,512]{2,1,0:T(8,128)(2,1)S(1)}, u32[]{:S(2)}, u32[]{:S(2)}) async-start(bf16[32,16,512]{2,1,0:T(8,128)(2,1)} %bitcast.2), calls=%async_computation.1 | async-start | bytes 1048576 | tf_op jit(solution)/shard_map/all_to_all | solution.py:596
  36.6 3.5 %collective-permute-start.7 = (bf16[128,128]{1,0:T(8,128)(2,1)S(1)}, bf16[128,128]{1,0:T(8,128)(2,1)S(1)}, u32[]{:S(2)}, u32[]{:S(2)}) collective-permute-start(bf16[128,128]{1,0:T(8,128)(2,1)S(1)} %get-tuple-element.36), channel_id=1, source_target_pairs={{0,0},{1,1},{4,2},{5,3},{2,4},{3,5},{6,6},{7,7},{8,8},{9,9},{12,10... | collective-permute-start | bytes 98312 | tf_op jit(solution)/shard_map/ppermute | solution.py:587
  40.2 0.0 collective-permute-start.8
  40.2 1.3 %collective-permute-start.9 = (bf16[128,128]{1,0:T(8,128)(2,1)S(1)}, bf16[128,128]{1,0:T(8,128)(2,1)S(1)}, u32[]{:S(2)}, u32[]{:S(2)}) collective-permute-start(bf16[128,128]{1,0:T(8,128)(2,1)S(1)} %get-tuple-element.38), channel_id=1, source_target_pairs={{1,0},{0,1},{5,2},{4,3},{3,4},{2,5},{7,6},{6,7},{9,8},{8,9},{13,10... | collective-permute-start | bytes 98312 | tf_op jit(solution)/shard_map/ppermute | solution.py:587
  41.5 0.8 %collective-permute-start.10 = (bf16[128,128]{1,0:T(8,128)(2,1)S(1)}, bf16[128,128]{1,0:T(8,128)(2,1)S(1)}, u32[]{:S(2)}, u32[]{:S(2)}) collective-permute-start(bf16[128,128]{1,0:T(8,128)(2,1)S(1)} %get-tuple-element.39), channel_id=1, source_target_pairs={{5,0},{4,1},{1,2},{0,3},{7,4},{6,5},{3,6},{2,7},{13,8},{12,9},{9,1... | collective-permute-start | bytes 98312 | tf_op jit(solution)/shard_map/ppermute | solution.py:587
  42.3 0.6 %collective-permute-done.7.refs_0_ = bf16[128,128]{1,0:T(8,128)(2,1)S(1)} collective-permute-done((bf16[128,128]{1,0:T(8,128)(2,1)S(1)}, bf16[128,128]{1,0:T(8,128)(2,1)S(1)}, u32[]{:S(2)}, u32[]{:S(2)}) %collective-permute-start.7) | collective-permute-done | bytes 32800 | tf_op jit(solution)/shard_map/ppermute | solution.py:587
  42.9 0.8 %collective-permute-done.8.refs_1_ = bf16[128,128]{1,0:T(8,128)(2,1)S(1)} collective-permute-done((bf16[128,128]{1,0:T(8,128)(2,1)S(1)}, bf16[128,128]{1,0:T(8,128)(2,1)S(1)}, u32[]{:S(2)}, u32[]{:S(2)}) %collective-permute-start.8) | collective-permute-done | bytes 32800 | tf_op jit(solution)/shard_map/ppermute | solution.py:587
  43.7 1.5 %collective-permute-done.9.refs_2_ = bf16[128,128]{1,0:T(8,128)(2,1)S(1)} collective-permute-done((bf16[128,128]{1,0:T(8,128)(2,1)S(1)}, bf16[128,128]{1,0:T(8,128)(2,1)S(1)}, u32[]{:S(2)}, u32[]{:S(2)}) %collective-permute-start.9) | collective-permute-done | bytes 32800 | tf_op jit(solution)/shard_map/ppermute | solution.py:587
  45.2 0.3 collective-permute-done.10.refs_3_
  45.5 6.5 %all-to-all-done.1 = bf16[32,16,512]{2,1,0:T(8,128)(2,1)S(1)} async-done(((bf16[32,16,512]{2,1,0:T(8,128)(2,1)}), bf16[32,16,512]{2,1,0:T(8,128)(2,1)S(1)}, u32[]{:S(2)}, u32[]{:S(2)}) %all-to-all-start.1) | async-done | bytes 524320 | tf_op jit(solution)/shard_map/all_to_all | solution.py:596
  52.0 1.0 %unslot_rows.1 = (bf16[128,512]{1,0:T(8,128)(2,1)}, bf16[128,2048]{1,0:T(8,128)(2,1)}) custom-call(bf16[128,128]{1,0:T(8,128)(2,1)S(1)} %get-tuple-element.22.back_ref, bf16[512,512]{1,0:T(8,128)(2,1)S(1)} %bitcast.5, bf16[128,128]{1,0:T(8,128)(2,1)S(1)} %collective-permute-done.7.refs_0_, bf16[128,128]{1,0:T(8,128)(2,1)S(1)} %collective-permute-done.8.refs_1_, ...), custom_call_target="tpu_custom_call" | custom-call | tf_op jit(solution)/shard_map/unslot_rows/pallas_call | solution.py:702
  (8 shorter events, 0.0 us)
Async XLA Ops:
  0.6 15.2 %copy-start = (f32[512]{0:T(512)S(1)}, f32[512]{0:T(512)}, u32[]{:S(2)}) copy-start(f32[512]{0:T(512)} %param.6) | copy-start | bytes 6148
  2.9 7.1 %copy-start.1 = (bf16[128,512]{1,0:T(8,128)(2,1)S(1)}, bf16[128,512]{1,0:T(8,128)(2,1)}, u32[]{:S(2)}) copy-start(bf16[128,512]{1,0:T(8,128)(2,1)} %grad_ref.1) | copy-start | bytes 393220
  3.0 23.4 %all-to-all-start = ((bf16[32,72,128]{2,1,0:T(8,128)(2,1)}), bf16[32,72,128]{2,1,0:T(8,128)(2,1)S(1)}, u32[]{:S(2)}, u32[]{:S(2)}) async-start(bf16[32,72,128]{2,1,0:T(8,128)(2,1)} %get-tuple-element.23), calls=%async_computation | async-start | bytes 1179648 | tf_op jit(solution)/shard_map/all_to_all | solution.py:596
  10.1 0.7 %copy-start.2 = (s32[1,128]{1,0:T(1,128)S(1)}, s32[1,128]{1,0:T(1,128)}, u32[]{:S(2)}) copy-start(s32[1,128]{1,0:T(1,128)} %get-tuple-element.21.slot_ref) | copy-start | bytes 1540
  10.8 6.1 %collective-permute-start = (bf16[128,128]{1,0:T(8,128)(2,1)S(1)}, bf16[128,128]{1,0:T(8,128)(2,1)S(1)}, u32[]{:S(2)}, u32[]{:S(2)}) collective-permute-start(bf16[128,128]{1,0:T(8,128)(2,1)S(1)} %get-tuple-element.24), channel_id=1, source_target_pairs={{0,0},{1,1},{2,4},{3,5},{4,2},{5,3},{6,6},{7,7},{8,8},{9,9},{10,12... | collective-permute-start | bytes 98312 | tf_op jit(solution)/shard_map/ppermute | solution.py:587
  14.4 2.6 %collective-permute-start.1 = (bf16[128,128]{1,0:T(8,128)(2,1)S(1)}, bf16[128,128]{1,0:T(8,128)(2,1)S(1)}, u32[]{:S(2)}, u32[]{:S(2)}) collective-permute-start(bf16[128,128]{1,0:T(8,128)(2,1)S(1)} %get-tuple-element.25), channel_id=1, source_target_pairs={{0,4},{1,5},{2,0},{3,1},{4,6},{5,7},{6,2},{7,3},{8,12},{9,13},{10,... | collective-permute-start | bytes 98312 | tf_op jit(solution)/shard_map/ppermute | solution.py:587
  14.4 5.4 %collective-permute-start.2 = (bf16[128,128]{1,0:T(8,128)(2,1)S(1)}, bf16[128,128]{1,0:T(8,128)(2,1)S(1)}, u32[]{:S(2)}, u32[]{:S(2)}) collective-permute-start(bf16[128,128]{1,0:T(8,128)(2,1)S(1)} %get-tuple-element.26), channel_id=1, source_target_pairs={{0,1},{1,0},{2,5},{3,4},{4,3},{5,2},{6,7},{7,6},{8,9},{9,8},{10,13... | collective-permute-start | bytes 98312 | tf_op jit(solution)/shard_map/ppermute | solution.py:587
  15.7 4.8 %collective-permute-start.3 = (bf16[128,128]{1,0:T(8,128)(2,1)S(1)}, bf16[128,128]{1,0:T(8,128)(2,1)S(1)}, u32[]{:S(2)}, u32[]{:S(2)}) collective-permute-start(bf16[128,128]{1,0:T(8,128)(2,1)S(1)} %get-tuple-element.27), channel_id=1, source_target_pairs={{0,5},{1,4},{2,1},{3,0},{4,7},{5,6},{6,3},{7,2},{8,13},{9,12},{10,... | collective-permute-start | bytes 98312 | tf_op jit(solution)/shard_map/ppermute | solution.py:587
  27.1 4.0 %collective-permute-start.6 = (f32[8,512]{1,0:T(8,128)S(1)}, f32[8,512]{1,0:T(8,128)S(1)}, u32[]{:S(2)}, u32[]{:S(2)}) collective-permute-start(f32[8,512]{1,0:T(8,128)S(1)} %get-tuple-element.34.refs_0_), channel_id=1, source_target_pairs={{0,5},{1,4},{2,7},{3,6},{4,1},{5,0},{6,3},{7,2},{8,13},{9,12},{10,... | collective-permute-start | bytes 49160 | tf_op jit(solution)/shard_map/ppermute | solution.py:587
  29.3 2.6 %collective-permute-start.5 = (f32[8,512]{1,0:T(8,128)S(1)}, f32[8,512]{1,0:T(8,128)S(1)}, u32[]{:S(2)}, u32[]{:S(2)}) collective-permute-start(f32[8,512]{1,0:T(8,128)S(1)} %get-tuple-element.34.refs_0_), channel_id=1, source_target_pairs={{0,1},{1,0},{2,3},{3,2},{4,5},{5,4},{6,7},{7,6},{8,9},{9,8},{10,11... | collective-permute-start | bytes 49160 | tf_op jit(solution)/shard_map/ppermute | solution.py:587
  29.6 2.3 %collective-permute-start.4 = (f32[8,512]{1,0:T(8,128)S(1)}, f32[8,512]{1,0:T(8,128)S(1)}, u32[]{:S(2)}, u32[]{:S(2)}) collective-permute-start(f32[8,512]{1,0:T(8,128)S(1)} %get-tuple-element.34.refs_0_), channel_id=1, source_target_pairs={{0,4},{1,5},{2,6},{3,7},{4,0},{5,1},{6,2},{7,3},{8,12},{9,13},{10,... | collective-permute-start | bytes 49160 | tf_op jit(solution)/shard_map/ppermute | solution.py:587
  34.0 18.0 %all-to-all-start.1 = ((bf16[32,16,512]{2,1,0:T(8,128)(2,1)}), bf16[32,16,512]{2,1,0:T(8,128)(2,1)S(1)}, u32[]{:S(2)}, u32[]{:S(2)}) async-start(bf16[32,16,512]{2,1,0:T(8,128)(2,1)} %bitcast.2), calls=%async_computation.1 | async-start | bytes 1048576 | tf_op jit(solution)/shard_map/all_to_all | solution.py:596
  36.6 6.3 %collective-permute-start.7 = (bf16[128,128]{1,0:T(8,128)(2,1)S(1)}, bf16[128,128]{1,0:T(8,128)(2,1)S(1)}, u32[]{:S(2)}, u32[]{:S(2)}) collective-permute-start(bf16[128,128]{1,0:T(8,128)(2,1)S(1)} %get-tuple-element.36), channel_id=1, source_target_pairs={{0,0},{1,1},{4,2},{5,3},{2,4},{3,5},{6,6},{7,7},{8,8},{9,9},{12,10... | collective-permute-start | bytes 98312 | tf_op jit(solution)/shard_map/ppermute | solution.py:587
  40.2 3.6 %collective-permute-start.8 = (bf16[128,128]{1,0:T(8,128)(2,1)S(1)}, bf16[128,128]{1,0:T(8,128)(2,1)S(1)}, u32[]{:S(2)}, u32[]{:S(2)}) collective-permute-start(bf16[128,128]{1,0:T(8,128)(2,1)S(1)} %get-tuple-element.37), channel_id=1, source_target_pairs={{4,0},{5,1},{0,2},{1,3},{6,4},{7,5},{2,6},{3,7},{12,8},{13,9},{8,1... | collective-permute-start | bytes 98312 | tf_op jit(solution)/shard_map/ppermute | solution.py:587
  40.2 5.0 %collective-permute-start.9 = (bf16[128,128]{1,0:T(8,128)(2,1)S(1)}, bf16[128,128]{1,0:T(8,128)(2,1)S(1)}, u32[]{:S(2)}, u32[]{:S(2)}) collective-permute-start(bf16[128,128]{1,0:T(8,128)(2,1)S(1)} %get-tuple-element.38), channel_id=1, source_target_pairs={{1,0},{0,1},{5,2},{4,3},{3,4},{2,5},{7,6},{6,7},{9,8},{8,9},{13,10... | collective-permute-start | bytes 98312 | tf_op jit(solution)/shard_map/ppermute | solution.py:587
  41.5 4.0 %collective-permute-start.10 = (bf16[128,128]{1,0:T(8,128)(2,1)S(1)}, bf16[128,128]{1,0:T(8,128)(2,1)S(1)}, u32[]{:S(2)}, u32[]{:S(2)}) collective-permute-start(bf16[128,128]{1,0:T(8,128)(2,1)S(1)} %get-tuple-element.39), channel_id=1, source_target_pairs={{5,0},{4,1},{1,2},{0,3},{7,4},{6,5},{3,6},{2,7},{13,8},{12,9},{9,1... | collective-permute-start | bytes 98312 | tf_op jit(solution)/shard_map/ppermute | solution.py:587

commit v6 on v5

--- a/solution.py
+++ b/solution.py
@@ -284,12 +284,7 @@
         copy.start()
     my_dp = lax.axis_index("dp")
     source = lax.broadcasted_iota(jnp.int32, (slots, slots), 0)
-    target = lax.broadcasted_iota(jnp.int32, (slots, slots), 1)
     owner_range = lax.broadcasted_iota(jnp.int32, (readers, slots), 0)
-    by_owner = lax.div(lax.broadcasted_iota(jnp.int32, (readers, slots), 1), per_pair)
-    to_lane = (lax.div(target, per_pair) == my_dp) & (
-        lax.rem(target, per_pair) == lax.rem(source, per_pair)
-    )
     loads[0].wait()
     loads[1].wait()
     users = user_ref[...]
@@ -303,10 +298,9 @@
     stores = [pltpu.make_async_copy(slot_ref, slot_hbm, store_sems.at[HEADS])]
     stores[0].start()
     placed = (source == slot).astype(jnp.bfloat16)
-    tagged = jnp.broadcast_to((users + 1).astype(jnp.float32), (readers, slots))
-    tagged = dot(tagged.astype(jnp.bfloat16), placed, 1, 1)
-    tagged = jnp.where(by_owner == owner_range, tagged, 0.0).astype(jnp.bfloat16)
-    tagged = dot(tagged, to_lane.astype(jnp.bfloat16), 1, 0).astype(jnp.bfloat16)
+    tagged = (hits * (users + 1).astype(jnp.float32)).astype(jnp.bfloat16)
+    to_lane = (source == my_dp * per_pair + ranks).astype(jnp.bfloat16)
+    tagged = dot(tagged, to_lane, 1, 1).astype(jnp.bfloat16)
     extra = send_ref.shape[1] - 4 * per_pair
     for owner in range(readers):
         for head in range(HEADS):

time: 53.3 us -> 53.2 us (level)
  no operation moved by 1% of the time
where the time goes in v6:
time: 53.2 us; the launch traced here: 52.9 us
  starting transfers between devices  23 us (43%)
  waiting for transfers between devices  21.4 us (40%)
  Pallas kernels  6.96 us (13%)
  between operations  0.76 us (1%)
  local copies, waits for them, and re-layouts  0.73 us (1%)
    ppermute x11, starting transfers between devices, send(): return lax.ppermute(value, ('dp', 'ctx'), pairs)  13.3 us
    all_to_all x2, waiting for transfers between devices, exchange(): lax.all_to_all(chunks, ('dp', 'ctx'), split_axis=0, concat_axis=0, tiled=...  12.3 us
    all_to_all x2, starting transfers between devices, exchange(): lax.all_to_all(chunks, ('dp', 'ctx'), split_axis=0, concat_axis=0, tiled=...  9.7 us
    ppermute x11, waiting for transfers between devices, send(): return lax.ppermute(value, ('dp', 'ctx'), pairs)  9.06 us
    pallas_call x1, Pallas kernels, by_heads(): pl.pallas_call(functools.partial(slot_kernel, per_pair=per_pair), out_sha...  2.18 us
    pallas_call x1, Pallas kernels, by_heads(): pl.pallas_call(backward_kernel, out_shape=(jax.ShapeDtypeStruct((group_ro...  2.12 us
  transfers between devices with their start and end apart: 13, of which 11 were waited for; matrix products, arithmetic and copies ran while one was open for 0% of the time, Pallas kernels for 2%

profile of v6, /device:TPU:1, one launch (start us, length us, event | category | flops | bytes accessed | tf_op | source)
XLA Modules:
  0.0 52.9 jit_solution(3884288251689917016)
XLA Ops:
  0.6 2.2 %slot_rows.1 = (bf16[32,72,128]{2,1,0:T(8,128)(2,1)}, s32[1,128]{1,0:T(1,128)}) custom-call(s32[16]{0:T(128)} %owner_hbm.1, s32[1,128]{1,0:T(1,128)} %bitcast.6, bf16[128,2048]{1,0:T(8,128)(2,1)} %proj_hbm.1), custom_call_target="tpu_custom_call" | custom-call | tf_op jit(solution)/shard_map/slot_rows/pallas_call | solution.py:619
  2.8 7.1 %all-to-all-start = ((bf16[32,72,128]{2,1,0:T(8,128)(2,1)}), bf16[32,72,128]{2,1,0:T(8,128)(2,1)S(1)}, u32[]{:S(2)}, u32[]{:S(2)}) async-start(bf16[32,72,128]{2,1,0:T(8,128)(2,1)} %get-tuple-element.23), calls=%async_computation | async-start | bytes 1179648 | tf_op jit(solution)/shard_map/all_to_all | solution.py:590
  10.0 0.6 %copy-done.2 = s32[1,128]{1,0:T(1,128)S(1)} copy-done((s32[1,128]{1,0:T(1,128)S(1)}, s32[1,128]{1,0:T(1,128)}, u32[]{:S(2)}) %copy-start.2) | copy-done | bytes 536
  10.6 0.1 cut_columns.1
  10.7 3.5 %collective-permute-start = (bf16[128,128]{1,0:T(8,128)(2,1)S(1)}, bf16[128,128]{1,0:T(8,128)(2,1)S(1)}, u32[]{:S(2)}, u32[]{:S(2)}) collective-permute-start(bf16[128,128]{1,0:T(8,128)(2,1)S(1)} %get-tuple-element.24), channel_id=1, source_target_pairs={{0,0},{1,1},{2,4},{3,5},{4,2},{5,3},{6,6},{7,7},{8,8},{9,9},{10,12... | collective-permute-start | bytes 98312 | tf_op jit(solution)/shard_map/ppermute | solution.py:581
  14.3 0.0 collective-permute-start.1
  14.3 1.3 %collective-permute-start.2 = (bf16[128,128]{1,0:T(8,128)(2,1)S(1)}, bf16[128,128]{1,0:T(8,128)(2,1)S(1)}, u32[]{:S(2)}, u32[]{:S(2)}) collective-permute-start(bf16[128,128]{1,0:T(8,128)(2,1)S(1)} %get-tuple-element.26), channel_id=1, source_target_pairs={{0,1},{1,0},{2,5},{3,4},{4,3},{5,2},{6,7},{7,6},{8,9},{9,8},{10,13... | collective-permute-start | bytes 98312 | tf_op jit(solution)/shard_map/ppermute | solution.py:581
  15.6 0.1 collective-permute-start.3
  15.7 0.1 dynamic-slice_bitcast_fusion.gain_ref
  15.8 1.1 %collective-permute-done.refs_0_ = bf16[128,128]{1,0:T(8,128)(2,1)S(1)} collective-permute-done((bf16[128,128]{1,0:T(8,128)(2,1)S(1)}, bf16[128,128]{1,0:T(8,128)(2,1)S(1)}, u32[]{:S(2)}, u32[]{:S(2)}) %collective-permute-start) | collective-permute-done | bytes 32800 | tf_op jit(solution)/shard_map/ppermute | solution.py:581
  16.8 2.9 %collective-permute-done.2.refs_2_ = bf16[128,128]{1,0:T(8,128)(2,1)S(1)} collective-permute-done((bf16[128,128]{1,0:T(8,128)(2,1)S(1)}, bf16[128,128]{1,0:T(8,128)(2,1)S(1)}, u32[]{:S(2)}, u32[]{:S(2)}) %collective-permute-start.2) | collective-permute-done | bytes 32800 | tf_op jit(solution)/shard_map/ppermute | solution.py:581
  19.7 0.7 %collective-permute-done.3.refs_3_ = bf16[128,128]{1,0:T(8,128)(2,1)S(1)} collective-permute-done((bf16[128,128]{1,0:T(8,128)(2,1)S(1)}, bf16[128,128]{1,0:T(8,128)(2,1)S(1)}, u32[]{:S(2)}, u32[]{:S(2)}) %collective-permute-start.3) | collective-permute-done | bytes 32800 | tf_op jit(solution)/shard_map/ppermute | solution.py:581
  20.4 5.8 %all-to-all-done.rows_ref = bf16[32,72,128]{2,1,0:T(8,128)(2,1)S(1)} async-done(((bf16[32,72,128]{2,1,0:T(8,128)(2,1)}), bf16[32,72,128]{2,1,0:T(8,128)(2,1)S(1)}, u32[]{:S(2)}, u32[]{:S(2)}) %all-to-all-start) | async-done | bytes 589856 | tf_op jit(solution)/shard_map/all_to_all | solution.py:590
  26.3 0.7 %forward.1 = (f32[512,128]{1,0:T(8,128)S(1)}, f32[8,512]{1,0:T(8,128)S(1)}) custom-call(bf16[32,72,128]{2,1,0:T(8,128)(2,1)S(1)} %all-to-all-done.rows_ref, bf16[512,128]{1,0:T(8,128)(2,1)S(1)} %lay_group.1.grads_ref, f32[1,128]{1,0:T(1,128)S(1)} %dynamic-slice_bitcast_fusion.gain_ref), custom_call_target="tpu_custom_call" | custom-call | tf_op jit(solution)/shard_map/forward/pallas_call | solution.py:655
  27.0 2.2 %collective-permute-start.6 = (f32[8,512]{1,0:T(8,128)S(1)}, f32[8,512]{1,0:T(8,128)S(1)}, u32[]{:S(2)}, u32[]{:S(2)}) collective-permute-start(f32[8,512]{1,0:T(8,128)S(1)} %get-tuple-element.34.refs_0_), channel_id=1, source_target_pairs={{0,5},{1,4},{2,7},{3,6},{4,1},{5,0},{6,3},{7,2},{8,13},{9,12},{10,... | collective-permute-start | bytes 49160 | tf_op jit(solution)/shard_map/ppermute | solution.py:581
  29.2 0.3 collective-permute-start.5
  29.4 0.2 collective-permute-start.4
  29.7 0.8 %slopes.1 = (f32[512,512]{1,0:T(8,128)S(1)}, f32[512,512]{1,0:T(8,128)S(1)}, bf16[512,512]{1,0:T(8,128)(2,1)S(1)}) custom-call(bf16[32,72,128]{2,1,0:T(8,128)(2,1)S(1)} %all-to-all-done.rows_ref), custom_call_target="tpu_custom_call" | custom-call | tf_op jit(solution)/shard_map/slopes/pallas_call | solution.py:667
  30.5 0.5 collective-permute-done.6.refs_3_
  31.0 0.8 %collective-permute-done.5.refs_2_ = f32[8,512]{1,0:T(8,128)S(1)} collective-permute-done((f32[8,512]{1,0:T(8,128)S(1)}, f32[8,512]{1,0:T(8,128)S(1)}, u32[]{:S(2)}, u32[]{:S(2)}) %collective-permute-start.5) | collective-permute-done | bytes 16416 | tf_op jit(solution)/shard_map/ppermute | solution.py:581
  31.8 2.1 %backward.1 = (bf16[512,512]{1,0:T(8,128)(2,1)}, bf16[128,128]{1,0:T(8,128)(2,1)S(1)}, bf16[128,128]{1,0:T(8,128)(2,1)S(1)}, bf16[128,128]{1,0:T(8,128)(2,1)S(1)}, bf16[128,128]{1,0:T(8,128)(2,1)S(1)}) custom-call(bf16[32,72,128]{2,1,0:T(8,128)(2,1)S(1)} %all-to-all-done.rows_ref, bf16[512,128]{1,0:T(8,128)(2,1)S(1)} %lay_group.1.grads_ref, ...), custom_call_target="tpu_custom_call" | custom-call | tf_op jit(solution)/shard_map/backward/pallas_call | solution.py:680
  33.9 2.6 %all-to-all-start.1 = ((bf16[32,16,512]{2,1,0:T(8,128)(2,1)}), bf16[32,16,512]{2,1,0:T(8,128)(2,1)S(1)}, u32[]{:S(2)}, u32[]{:S(2)}) async-start(bf16[32,16,512]{2,1,0:T(8,128)(2,1)} %bitcast.2), calls=%async_computation.1 | async-start | bytes 1048576 | tf_op jit(solution)/shard_map/all_to_all | solution.py:590
  36.5 3.5 %collective-permute-start.7 = (bf16[128,128]{1,0:T(8,128)(2,1)S(1)}, bf16[128,128]{1,0:T(8,128)(2,1)S(1)}, u32[]{:S(2)}, u32[]{:S(2)}) collective-permute-start(bf16[128,128]{1,0:T(8,128)(2,1)S(1)} %get-tuple-element.36), channel_id=1, source_target_pairs={{0,0},{1,1},{4,2},{5,3},{2,4},{3,5},{6,6},{7,7},{8,8},{9,9},{12,10... | collective-permute-start | bytes 98312 | tf_op jit(solution)/shard_map/ppermute | solution.py:581
  40.1 0.0 collective-permute-start.8
  40.1 1.3 %collective-permute-start.9 = (bf16[128,128]{1,0:T(8,128)(2,1)S(1)}, bf16[128,128]{1,0:T(8,128)(2,1)S(1)}, u32[]{:S(2)}, u32[]{:S(2)}) collective-permute-start(bf16[128,128]{1,0:T(8,128)(2,1)S(1)} %get-tuple-element.38), channel_id=1, source_target_pairs={{1,0},{0,1},{5,2},{4,3},{3,4},{2,5},{7,6},{6,7},{9,8},{8,9},{13,10... | collective-permute-start | bytes 98312 | tf_op jit(solution)/shard_map/ppermute | solution.py:581
  41.4 0.8 %collective-permute-start.10 = (bf16[128,128]{1,0:T(8,128)(2,1)S(1)}, bf16[128,128]{1,0:T(8,128)(2,1)S(1)}, u32[]{:S(2)}, u32[]{:S(2)}) collective-permute-start(bf16[128,128]{1,0:T(8,128)(2,1)S(1)} %get-tuple-element.39), channel_id=1, source_target_pairs={{5,0},{4,1},{1,2},{0,3},{7,4},{6,5},{3,6},{2,7},{13,8},{12,9},{9,1... | collective-permute-start | bytes 98312 | tf_op jit(solution)/shard_map/ppermute | solution.py:581
  42.2 0.6 %collective-permute-done.7.refs_0_ = bf16[128,128]{1,0:T(8,128)(2,1)S(1)} collective-permute-done((bf16[128,128]{1,0:T(8,128)(2,1)S(1)}, bf16[128,128]{1,0:T(8,128)(2,1)S(1)}, u32[]{:S(2)}, u32[]{:S(2)}) %collective-permute-start.7) | collective-permute-done | bytes 32800 | tf_op jit(solution)/shard_map/ppermute | solution.py:581
  42.8 0.8 %collective-permute-done.8.refs_1_ = bf16[128,128]{1,0:T(8,128)(2,1)S(1)} collective-permute-done((bf16[128,128]{1,0:T(8,128)(2,1)S(1)}, bf16[128,128]{1,0:T(8,128)(2,1)S(1)}, u32[]{:S(2)}, u32[]{:S(2)}) %collective-permute-start.8) | collective-permute-done | bytes 32800 | tf_op jit(solution)/shard_map/ppermute | solution.py:581
  43.6 1.5 %collective-permute-done.9.refs_2_ = bf16[128,128]{1,0:T(8,128)(2,1)S(1)} collective-permute-done((bf16[128,128]{1,0:T(8,128)(2,1)S(1)}, bf16[128,128]{1,0:T(8,128)(2,1)S(1)}, u32[]{:S(2)}, u32[]{:S(2)}) %collective-permute-start.9) | collective-permute-done | bytes 32800 | tf_op jit(solution)/shard_map/ppermute | solution.py:581
  45.1 0.3 collective-permute-done.10.refs_3_
  45.4 6.5 %all-to-all-done.1 = bf16[32,16,512]{2,1,0:T(8,128)(2,1)S(1)} async-done(((bf16[32,16,512]{2,1,0:T(8,128)(2,1)}), bf16[32,16,512]{2,1,0:T(8,128)(2,1)S(1)}, u32[]{:S(2)}, u32[]{:S(2)}) %all-to-all-start.1) | async-done | bytes 524320 | tf_op jit(solution)/shard_map/all_to_all | solution.py:590
  51.9 1.0 %unslot_rows.1 = (bf16[128,512]{1,0:T(8,128)(2,1)}, bf16[128,2048]{1,0:T(8,128)(2,1)}) custom-call(bf16[128,128]{1,0:T(8,128)(2,1)S(1)} %get-tuple-element.22.back_ref, bf16[512,512]{1,0:T(8,128)(2,1)S(1)} %bitcast.5, bf16[128,128]{1,0:T(8,128)(2,1)S(1)} %collective-permute-done.7.refs_0_, bf16[128,128]{1,0:T(8,128)(2,1)S(1)} %collective-permute-done.8.refs_1_, ...), custom_call_target="tpu_custom_call" | custom-call | tf_op jit(solution)/shard_map/unslot_rows/pallas_call | solution.py:696
  (8 shorter events, 0.0 us)
Async XLA Ops:
  0.6 15.1 %copy-start = (f32[512]{0:T(512)S(1)}, f32[512]{0:T(512)}, u32[]{:S(2)}) copy-start(f32[512]{0:T(512)} %param.6) | copy-start | bytes 6148
  2.8 7.1 %copy-start.1 = (bf16[128,512]{1,0:T(8,128)(2,1)S(1)}, bf16[128,512]{1,0:T(8,128)(2,1)}, u32[]{:S(2)}) copy-start(bf16[128,512]{1,0:T(8,128)(2,1)} %grad_ref.1) | copy-start | bytes 393220
  2.8 23.4 %all-to-all-start = ((bf16[32,72,128]{2,1,0:T(8,128)(2,1)}), bf16[32,72,128]{2,1,0:T(8,128)(2,1)S(1)}, u32[]{:S(2)}, u32[]{:S(2)}) async-start(bf16[32,72,128]{2,1,0:T(8,128)(2,1)} %get-tuple-element.23), calls=%async_computation | async-start | bytes 1179648 | tf_op jit(solution)/shard_map/all_to_all | solution.py:590
  10.0 0.7 %copy-start.2 = (s32[1,128]{1,0:T(1,128)S(1)}, s32[1,128]{1,0:T(1,128)}, u32[]{:S(2)}) copy-start(s32[1,128]{1,0:T(1,128)} %get-tuple-element.21.slot_ref) | copy-start | bytes 1540
  10.7 6.1 %collective-permute-start = (bf16[128,128]{1,0:T(8,128)(2,1)S(1)}, bf16[128,128]{1,0:T(8,128)(2,1)S(1)}, u32[]{:S(2)}, u32[]{:S(2)}) collective-permute-start(bf16[128,128]{1,0:T(8,128)(2,1)S(1)} %get-tuple-element.24), channel_id=1, source_target_pairs={{0,0},{1,1},{2,4},{3,5},{4,2},{5,3},{6,6},{7,7},{8,8},{9,9},{10,12... | collective-permute-start | bytes 98312 | tf_op jit(solution)/shard_map/ppermute | solution.py:581
  14.3 2.6 %collective-permute-start.1 = (bf16[128,128]{1,0:T(8,128)(2,1)S(1)}, bf16[128,128]{1,0:T(8,128)(2,1)S(1)}, u32[]{:S(2)}, u32[]{:S(2)}) collective-permute-start(bf16[128,128]{1,0:T(8,128)(2,1)S(1)} %get-tuple-element.25), channel_id=1, source_target_pairs={{0,4},{1,5},{2,0},{3,1},{4,6},{5,7},{6,2},{7,3},{8,12},{9,13},{10,... | collective-permute-start | bytes 98312 | tf_op jit(solution)/shard_map/ppermute | solution.py:581
  14.3 5.4 %collective-permute-start.2 = (bf16[128,128]{1,0:T(8,128)(2,1)S(1)}, bf16[128,128]{1,0:T(8,128)(2,1)S(1)}, u32[]{:S(2)}, u32[]{:S(2)}) collective-permute-start(bf16[128,128]{1,0:T(8,128)(2,1)S(1)} %get-tuple-element.26), channel_id=1, source_target_pairs={{0,1},{1,0},{2,5},{3,4},{4,3},{5,2},{6,7},{7,6},{8,9},{9,8},{10,13... | collective-permute-start | bytes 98312 | tf_op jit(solution)/shard_map/ppermute | solution.py:581
  15.6 4.8 %collective-permute-start.3 = (bf16[128,128]{1,0:T(8,128)(2,1)S(1)}, bf16[128,128]{1,0:T(8,128)(2,1)S(1)}, u32[]{:S(2)}, u32[]{:S(2)}) collective-permute-start(bf16[128,128]{1,0:T(8,128)(2,1)S(1)} %get-tuple-element.27), channel_id=1, source_target_pairs={{0,5},{1,4},{2,1},{3,0},{4,7},{5,6},{6,3},{7,2},{8,13},{9,12},{10,... | collective-permute-start | bytes 98312 | tf_op jit(solution)/shard_map/ppermute | solution.py:581
  27.0 4.0 %collective-permute-start.6 = (f32[8,512]{1,0:T(8,128)S(1)}, f32[8,512]{1,0:T(8,128)S(1)}, u32[]{:S(2)}, u32[]{:S(2)}) collective-permute-start(f32[8,512]{1,0:T(8,128)S(1)} %get-tuple-element.34.refs_0_), channel_id=1, source_target_pairs={{0,5},{1,4},{2,7},{3,6},{4,1},{5,0},{6,3},{7,2},{8,13},{9,12},{10,... | collective-permute-start | bytes 49160 | tf_op jit(solution)/shard_map/ppermute | solution.py:581
  29.2 2.6 %collective-permute-start.5 = (f32[8,512]{1,0:T(8,128)S(1)}, f32[8,512]{1,0:T(8,128)S(1)}, u32[]{:S(2)}, u32[]{:S(2)}) collective-permute-start(f32[8,512]{1,0:T(8,128)S(1)} %get-tuple-element.34.refs_0_), channel_id=1, source_target_pairs={{0,1},{1,0},{2,3},{3,2},{4,5},{5,4},{6,7},{7,6},{8,9},{9,8},{10,11... | collective-permute-start | bytes 49160 | tf_op jit(solution)/shard_map/ppermute | solution.py:581
  29.4 2.3 %collective-permute-start.4 = (f32[8,512]{1,0:T(8,128)S(1)}, f32[8,512]{1,0:T(8,128)S(1)}, u32[]{:S(2)}, u32[]{:S(2)}) collective-permute-start(f32[8,512]{1,0:T(8,128)S(1)} %get-tuple-element.34.refs_0_), channel_id=1, source_target_pairs={{0,4},{1,5},{2,6},{3,7},{4,0},{5,1},{6,2},{7,3},{8,12},{9,13},{10,... | collective-permute-start | bytes 49160 | tf_op jit(solution)/shard_map/ppermute | solution.py:581
  33.9 18.0 %all-to-all-start.1 = ((bf16[32,16,512]{2,1,0:T(8,128)(2,1)}), bf16[32,16,512]{2,1,0:T(8,128)(2,1)S(1)}, u32[]{:S(2)}, u32[]{:S(2)}) async-start(bf16[32,16,512]{2,1,0:T(8,128)(2,1)} %bitcast.2), calls=%async_computation.1 | async-start | bytes 1048576 | tf_op jit(solution)/shard_map/all_to_all | solution.py:590
  36.5 6.3 %collective-permute-start.7 = (bf16[128,128]{1,0:T(8,128)(2,1)S(1)}, bf16[128,128]{1,0:T(8,128)(2,1)S(1)}, u32[]{:S(2)}, u32[]{:S(2)}) collective-permute-start(bf16[128,128]{1,0:T(8,128)(2,1)S(1)} %get-tuple-element.36), channel_id=1, source_target_pairs={{0,0},{1,1},{4,2},{5,3},{2,4},{3,5},{6,6},{7,7},{8,8},{9,9},{12,10... | collective-permute-start | bytes 98312 | tf_op jit(solution)/shard_map/ppermute | solution.py:581
  40.1 3.6 %collective-permute-start.8 = (bf16[128,128]{1,0:T(8,128)(2,1)S(1)}, bf16[128,128]{1,0:T(8,128)(2,1)S(1)}, u32[]{:S(2)}, u32[]{:S(2)}) collective-permute-start(bf16[128,128]{1,0:T(8,128)(2,1)S(1)} %get-tuple-element.37), channel_id=1, source_target_pairs={{4,0},{5,1},{0,2},{1,3},{6,4},{7,5},{2,6},{3,7},{12,8},{13,9},{8,1... | collective-permute-start | bytes 98312 | tf_op jit(solution)/shard_map/ppermute | solution.py:581
  40.1 5.0 %collective-permute-start.9 = (bf16[128,128]{1,0:T(8,128)(2,1)S(1)}, bf16[128,128]{1,0:T(8,128)(2,1)S(1)}, u32[]{:S(2)}, u32[]{:S(2)}) collective-permute-start(bf16[128,128]{1,0:T(8,128)(2,1)S(1)} %get-tuple-element.38), channel_id=1, source_target_pairs={{1,0},{0,1},{5,2},{4,3},{3,4},{2,5},{7,6},{6,7},{9,8},{8,9},{13,10... | collective-permute-start | bytes 98312 | tf_op jit(solution)/shard_map/ppermute | solution.py:581
  41.4 4.0 %collective-permute-start.10 = (bf16[128,128]{1,0:T(8,128)(2,1)S(1)}, bf16[128,128]{1,0:T(8,128)(2,1)S(1)}, u32[]{:S(2)}, u32[]{:S(2)}) collective-permute-start(bf16[128,128]{1,0:T(8,128)(2,1)S(1)} %get-tuple-element.39), channel_id=1, source_target_pairs={{5,0},{4,1},{1,2},{0,3},{7,4},{6,5},{3,6},{2,7},{13,8},{12,9},{9,1... | collective-permute-start | bytes 98312 | tf_op jit(solution)/shard_map/ppermute | solution.py:581

commit v7 on v6

--- a/solution.py
+++ b/solution.py
@@ -431,7 +431,6 @@
             stats_ref[1:2, here] = spread
             stats_ref[2:3, here] = grad_sum
             stats_ref[3:4, here] = cross
-            stats_ref[4:8, here] = jnp.zeros((4, size), jnp.float32)
 
 
 def slope_kernel(rows_ref, slopes_ref, turned_slopes_ref, turned_weights_ref):
@@ -479,27 +478,25 @@
     mean_grad = sum(stat[2:3] for stat in stats) / width
     cross = sum(stat[3:4] + (stat[0:1] - mean) * stat[2:3] for stat in stats)
     mean_cross = cross * inv_std / width
-    row = lax.broadcasted_iota(jnp.int32, (size, size), 0)
+    packed = [
+        stat[:, window * size : (window + 1) * size]
+        for window in range(HEADS)
+        for stat in (mean, inv_std, mean_grad, mean_cross)
+    ]
+    packed.append(jnp.zeros((size - len(packed), size), jnp.float32))
+    packed = jnp.concatenate(packed, axis=0).T
     out_grads = []
     for window in range(HEADS):
         here = slice(window * size, (window + 1) * size)
-        packed = jnp.where(
-            row == 0,
-            mean[:, here],
-            jnp.where(
-                row == 1,
-                inv_std[:, here],
-                jnp.where(row == 2, mean_grad[:, here], mean_cross[:, here]),
-            ),
-        ).T
+        row_mean, row_inv, row_grad, row_cross = [
+            packed[:, 4 * window + index : 4 * window + index + 1] for index in range(4)
+        ]
         unit = part_rows(rows_ref, 0, window, window + 1).astype(jnp.float32)
         grad_gain = grads_ref[here].astype(jnp.float32) * gain_ref[...]
-        normed = (attended_ref[here] - packed[:, 0:1]) * packed[:, 1:2]
+        normed = (attended_ref[here] - row_mean) * row_inv
         layer_all[here] = (normed * gain_ref[...] * unit).astype(jnp.bfloat16)
         put_rows(out_ref, 0, window, window + 1, grad_gain * normed, readers)
-        out_grads.append(
-            packed[:, 1:2] * (grad_gain * unit - packed[:, 2:3] - normed * packed[:, 3:4])
-        )
+        out_grads.append(row_inv * (grad_gain * unit - row_grad - normed * row_cross))
     out_grads = jnp.concatenate(out_grads, axis=0).astype(jnp.bfloat16)
     stores = []
     for first in range(0, HEADS, STEP):
@@ -656,7 +653,7 @@
         forward_kernel,
         out_shape=(
             jax.ShapeDtypeStruct((group_rows, HD), jnp.float32),
-            jax.ShapeDtypeStruct((8, group_rows), jnp.float32),
+            jax.ShapeDtypeStruct((4, group_rows), jnp.float32),
         ),
         in_specs=vmem(3),
         out_specs=tuple(vmem(2)),

time: 53.2 us -> 53 us (level)
  no operation moved by 1% of the time
where the time goes in v7:
time: 53 us; the launch traced here: 52.7 us
  starting transfers between devices  23 us (43%)
  waiting for transfers between devices  21.3 us (40%)
  Pallas kernels  6.86 us (13%)
  between operations  0.76 us (1%)
  local copies, waits for them, and re-layouts  0.73 us (1%)
    ppermute x11, starting transfers between devices, send(): return lax.ppermute(value, ('dp', 'ctx'), pairs)  13.3 us
    all_to_all x2, waiting for transfers between devices, exchange(): lax.all_to_all(chunks, ('dp', 'ctx'), split_axis=0, concat_axis=0, tiled=...  12.4 us
    all_to_all x2, starting transfers between devices, exchange(): lax.all_to_all(chunks, ('dp', 'ctx'), split_axis=0, concat_axis=0, tiled=...  9.7 us
    ppermute x11, waiting for transfers between devices, send(): return lax.ppermute(value, ('dp', 'ctx'), pairs)  8.98 us
    pallas_call x1, Pallas kernels, by_heads(): pl.pallas_call(functools.partial(slot_kernel, per_pair=per_pair), out_sha...  2.18 us
    pallas_call x1, Pallas kernels, by_heads(): pl.pallas_call(backward_kernel, out_shape=(jax.ShapeDtypeStruct((group_ro...  2.02 us
  transfers between devices with their start and end apart: 13, of which 11 were waited for; matrix products, arithmetic and copies ran while one was open for 0% of the time, Pallas kernels for 2%

profile of v7, /device:TPU:1, one launch (start us, length us, event | category | flops | bytes accessed | tf_op | source)
XLA Modules:
  0.0 52.7 jit_solution(17936988205347187005)
XLA Ops:
  0.6 2.2 %slot_rows.1 = (bf16[32,72,128]{2,1,0:T(8,128)(2,1)}, s32[1,128]{1,0:T(1,128)}) custom-call(s32[16]{0:T(128)} %owner_hbm.1, s32[1,128]{1,0:T(1,128)} %bitcast.6, bf16[128,2048]{1,0:T(8,128)(2,1)} %proj_hbm.1), custom_call_target="tpu_custom_call" | custom-call | tf_op jit(solution)/shard_map/slot_rows/pallas_call | solution.py:616
  2.8 7.1 %all-to-all-start = ((bf16[32,72,128]{2,1,0:T(8,128)(2,1)}), bf16[32,72,128]{2,1,0:T(8,128)(2,1)S(1)}, u32[]{:S(2)}, u32[]{:S(2)}) async-start(bf16[32,72,128]{2,1,0:T(8,128)(2,1)} %get-tuple-element.23), calls=%async_computation | async-start | bytes 1179648 | tf_op jit(solution)/shard_map/all_to_all | solution.py:587
  10.0 0.6 %copy-done.2 = s32[1,128]{1,0:T(1,128)S(1)} copy-done((s32[1,128]{1,0:T(1,128)S(1)}, s32[1,128]{1,0:T(1,128)}, u32[]{:S(2)}) %copy-start.2) | copy-done | bytes 536
  10.6 0.1 cut_columns.1
  10.7 3.5 %collective-permute-start = (bf16[128,128]{1,0:T(8,128)(2,1)S(1)}, bf16[128,128]{1,0:T(8,128)(2,1)S(1)}, u32[]{:S(2)}, u32[]{:S(2)}) collective-permute-start(bf16[128,128]{1,0:T(8,128)(2,1)S(1)} %get-tuple-element.24), channel_id=1, source_target_pairs={{0,0},{1,1},{2,4},{3,5},{4,2},{5,3},{6,6},{7,7},{8,8},{9,9},{10,12... | collective-permute-start | bytes 98312 | tf_op jit(solution)/shard_map/ppermute | solution.py:578
  14.3 0.0 collective-permute-start.1
  14.3 1.3 %collective-permute-start.2 = (bf16[128,128]{1,0:T(8,128)(2,1)S(1)}, bf16[128,128]{1,0:T(8,128)(2,1)S(1)}, u32[]{:S(2)}, u32[]{:S(2)}) collective-permute-start(bf16[128,128]{1,0:T(8,128)(2,1)S(1)} %get-tuple-element.26), channel_id=1, source_target_pairs={{0,1},{1,0},{2,5},{3,4},{4,3},{5,2},{6,7},{7,6},{8,9},{9,8},{10,13... | collective-permute-start | bytes 98312 | tf_op jit(solution)/shard_map/ppermute | solution.py:578
  15.6 0.1 collective-permute-start.3
  15.7 0.1 dynamic-slice_bitcast_fusion.gain_ref
  15.8 1.1 %collective-permute-done.refs_0_ = bf16[128,128]{1,0:T(8,128)(2,1)S(1)} collective-permute-done((bf16[128,128]{1,0:T(8,128)(2,1)S(1)}, bf16[128,128]{1,0:T(8,128)(2,1)S(1)}, u32[]{:S(2)}, u32[]{:S(2)}) %collective-permute-start) | collective-permute-done | bytes 32800 | tf_op jit(solution)/shard_map/ppermute | solution.py:578
  16.8 2.9 %collective-permute-done.2.refs_2_ = bf16[128,128]{1,0:T(8,128)(2,1)S(1)} collective-permute-done((bf16[128,128]{1,0:T(8,128)(2,1)S(1)}, bf16[128,128]{1,0:T(8,128)(2,1)S(1)}, u32[]{:S(2)}, u32[]{:S(2)}) %collective-permute-start.2) | collective-permute-done | bytes 32800 | tf_op jit(solution)/shard_map/ppermute | solution.py:578
  19.7 0.7 %collective-permute-done.3.refs_3_ = bf16[128,128]{1,0:T(8,128)(2,1)S(1)} collective-permute-done((bf16[128,128]{1,0:T(8,128)(2,1)S(1)}, bf16[128,128]{1,0:T(8,128)(2,1)S(1)}, u32[]{:S(2)}, u32[]{:S(2)}) %collective-permute-start.3) | collective-permute-done | bytes 32800 | tf_op jit(solution)/shard_map/ppermute | solution.py:578
  20.4 5.8 %all-to-all-done.rows_ref = bf16[32,72,128]{2,1,0:T(8,128)(2,1)S(1)} async-done(((bf16[32,72,128]{2,1,0:T(8,128)(2,1)}), bf16[32,72,128]{2,1,0:T(8,128)(2,1)S(1)}, u32[]{:S(2)}, u32[]{:S(2)}) %all-to-all-start) | async-done | bytes 589856 | tf_op jit(solution)/shard_map/all_to_all | solution.py:587
  26.3 0.7 %forward.1 = (f32[512,128]{1,0:T(8,128)S(1)}, f32[4,512]{1,0:T(4,128)S(1)}) custom-call(bf16[32,72,128]{2,1,0:T(8,128)(2,1)S(1)} %all-to-all-done.rows_ref, bf16[512,128]{1,0:T(8,128)(2,1)S(1)} %lay_group.1.grads_ref, f32[1,128]{1,0:T(1,128)S(1)} %dynamic-slice_bitcast_fusion.gain_ref), custom_call_target="tpu_custom_call" | custom-call | tf_op jit(solution)/shard_map/forward/pallas_call | solution.py:652
  27.0 2.2 %collective-permute-start.6 = (f32[4,512]{1,0:T(4,128)S(1)}, f32[4,512]{1,0:T(4,128)S(1)}, u32[]{:S(2)}, u32[]{:S(2)}) collective-permute-start(f32[4,512]{1,0:T(4,128)S(1)} %get-tuple-element.34.refs_0_), channel_id=1, source_target_pairs={{0,5},{1,4},{2,7},{3,6},{4,1},{5,0},{6,3},{7,2},{8,13},{9,12},{10,... | collective-permute-start | bytes 24584 | tf_op jit(solution)/shard_map/ppermute | solution.py:578
  29.2 0.3 collective-permute-start.5
  29.4 0.2 collective-permute-start.4
  29.7 0.8 %slopes.1 = (f32[512,512]{1,0:T(8,128)S(1)}, f32[512,512]{1,0:T(8,128)S(1)}, bf16[512,512]{1,0:T(8,128)(2,1)S(1)}) custom-call(bf16[32,72,128]{2,1,0:T(8,128)(2,1)S(1)} %all-to-all-done.rows_ref), custom_call_target="tpu_custom_call" | custom-call | tf_op jit(solution)/shard_map/slopes/pallas_call | solution.py:664
  30.5 0.4 collective-permute-done.6.refs_3_
  30.8 0.9 %collective-permute-done.5.refs_2_ = f32[4,512]{1,0:T(4,128)S(1)} collective-permute-done((f32[4,512]{1,0:T(4,128)S(1)}, f32[4,512]{1,0:T(4,128)S(1)}, u32[]{:S(2)}, u32[]{:S(2)}) %collective-permute-start.5) | collective-permute-done | bytes 8224 | tf_op jit(solution)/shard_map/ppermute | solution.py:578
  31.7 2.0 %backward.1 = (bf16[512,512]{1,0:T(8,128)(2,1)}, bf16[128,128]{1,0:T(8,128)(2,1)S(1)}, bf16[128,128]{1,0:T(8,128)(2,1)S(1)}, bf16[128,128]{1,0:T(8,128)(2,1)S(1)}, bf16[128,128]{1,0:T(8,128)(2,1)S(1)}) custom-call(bf16[32,72,128]{2,1,0:T(8,128)(2,1)S(1)} %all-to-all-done.rows_ref, bf16[512,128]{1,0:T(8,128)(2,1)S(1)} %lay_group.1.grads_ref, ...), custom_call_target="tpu_custom_call" | custom-call | tf_op jit(solution)/shard_map/backward/pallas_call | solution.py:677
  33.7 2.6 %all-to-all-start.1 = ((bf16[32,16,512]{2,1,0:T(8,128)(2,1)}), bf16[32,16,512]{2,1,0:T(8,128)(2,1)S(1)}, u32[]{:S(2)}, u32[]{:S(2)}) async-start(bf16[32,16,512]{2,1,0:T(8,128)(2,1)} %bitcast.2), calls=%async_computation.1 | async-start | bytes 1048576 | tf_op jit(solution)/shard_map/all_to_all | solution.py:587
  36.3 3.5 %collective-permute-start.7 = (bf16[128,128]{1,0:T(8,128)(2,1)S(1)}, bf16[128,128]{1,0:T(8,128)(2,1)S(1)}, u32[]{:S(2)}, u32[]{:S(2)}) collective-permute-start(bf16[128,128]{1,0:T(8,128)(2,1)S(1)} %get-tuple-element.36), channel_id=1, source_target_pairs={{0,0},{1,1},{4,2},{5,3},{2,4},{3,5},{6,6},{7,7},{8,8},{9,9},{12,10... | collective-permute-start | bytes 98312 | tf_op jit(solution)/shard_map/ppermute | solution.py:578
  39.9 0.0 collective-permute-start.8
  39.9 1.3 %collective-permute-start.9 = (bf16[128,128]{1,0:T(8,128)(2,1)S(1)}, bf16[128,128]{1,0:T(8,128)(2,1)S(1)}, u32[]{:S(2)}, u32[]{:S(2)}) collective-permute-start(bf16[128,128]{1,0:T(8,128)(2,1)S(1)} %get-tuple-element.38), channel_id=1, source_target_pairs={{1,0},{0,1},{5,2},{4,3},{3,4},{2,5},{7,6},{6,7},{9,8},{8,9},{13,10... | collective-permute-start | bytes 98312 | tf_op jit(solution)/shard_map/ppermute | solution.py:578
  41.2 0.8 %collective-permute-start.10 = (bf16[128,128]{1,0:T(8,128)(2,1)S(1)}, bf16[128,128]{1,0:T(8,128)(2,1)S(1)}, u32[]{:S(2)}, u32[]{:S(2)}) collective-permute-start(bf16[128,128]{1,0:T(8,128)(2,1)S(1)} %get-tuple-element.39), channel_id=1, source_target_pairs={{5,0},{4,1},{1,2},{0,3},{7,4},{6,5},{3,6},{2,7},{13,8},{12,9},{9,1... | collective-permute-start | bytes 98312 | tf_op jit(solution)/shard_map/ppermute | solution.py:578
  42.0 0.6 %collective-permute-done.7.refs_0_ = bf16[128,128]{1,0:T(8,128)(2,1)S(1)} collective-permute-done((bf16[128,128]{1,0:T(8,128)(2,1)S(1)}, bf16[128,128]{1,0:T(8,128)(2,1)S(1)}, u32[]{:S(2)}, u32[]{:S(2)}) %collective-permute-start.7) | collective-permute-done | bytes 32800 | tf_op jit(solution)/shard_map/ppermute | solution.py:578
  42.6 0.8 %collective-permute-done.8.refs_1_ = bf16[128,128]{1,0:T(8,128)(2,1)S(1)} collective-permute-done((bf16[128,128]{1,0:T(8,128)(2,1)S(1)}, bf16[128,128]{1,0:T(8,128)(2,1)S(1)}, u32[]{:S(2)}, u32[]{:S(2)}) %collective-permute-start.8) | collective-permute-done | bytes 32800 | tf_op jit(solution)/shard_map/ppermute | solution.py:578
  43.4 1.5 %collective-permute-done.9.refs_2_ = bf16[128,128]{1,0:T(8,128)(2,1)S(1)} collective-permute-done((bf16[128,128]{1,0:T(8,128)(2,1)S(1)}, bf16[128,128]{1,0:T(8,128)(2,1)S(1)}, u32[]{:S(2)}, u32[]{:S(2)}) %collective-permute-start.9) | collective-permute-done | bytes 32800 | tf_op jit(solution)/shard_map/ppermute | solution.py:578
  44.9 0.3 collective-permute-done.10.refs_3_
  45.2 6.5 %all-to-all-done.1 = bf16[32,16,512]{2,1,0:T(8,128)(2,1)S(1)} async-done(((bf16[32,16,512]{2,1,0:T(8,128)(2,1)}), bf16[32,16,512]{2,1,0:T(8,128)(2,1)S(1)}, u32[]{:S(2)}, u32[]{:S(2)}) %all-to-all-start.1) | async-done | bytes 524320 | tf_op jit(solution)/shard_map/all_to_all | solution.py:587
  51.7 1.0 %unslot_rows.1 = (bf16[128,512]{1,0:T(8,128)(2,1)}, bf16[128,2048]{1,0:T(8,128)(2,1)}) custom-call(bf16[128,128]{1,0:T(8,128)(2,1)S(1)} %get-tuple-element.22.back_ref, bf16[512,512]{1,0:T(8,128)(2,1)S(1)} %bitcast.5, bf16[128,128]{1,0:T(8,128)(2,1)S(1)} %collective-permute-done.7.refs_0_, bf16[128,128]{1,0:T(8,128)(2,1)S(1)} %collective-permute-done.8.refs_1_, ...), custom_call_target="tpu_custom_call" | custom-call | tf_op jit(solution)/shard_map/unslot_rows/pallas_call | solution.py:693
  (8 shorter events, 0.0 us)
Async XLA Ops:
  0.6 15.1 %copy-start = (f32[512]{0:T(512)S(1)}, f32[512]{0:T(512)}, u32[]{:S(2)}) copy-start(f32[512]{0:T(512)} %param.6) | copy-start | bytes 6148
  2.8 7.1 %copy-start.1 = (bf16[128,512]{1,0:T(8,128)(2,1)S(1)}, bf16[128,512]{1,0:T(8,128)(2,1)}, u32[]{:S(2)}) copy-start(bf16[128,512]{1,0:T(8,128)(2,1)} %grad_ref.1) | copy-start | bytes 393220
  2.8 23.4 %all-to-all-start = ((bf16[32,72,128]{2,1,0:T(8,128)(2,1)}), bf16[32,72,128]{2,1,0:T(8,128)(2,1)S(1)}, u32[]{:S(2)}, u32[]{:S(2)}) async-start(bf16[32,72,128]{2,1,0:T(8,128)(2,1)} %get-tuple-element.23), calls=%async_computation | async-start | bytes 1179648 | tf_op jit(solution)/shard_map/all_to_all | solution.py:587
  10.0 0.7 %copy-start.2 = (s32[1,128]{1,0:T(1,128)S(1)}, s32[1,128]{1,0:T(1,128)}, u32[]{:S(2)}) copy-start(s32[1,128]{1,0:T(1,128)} %get-tuple-element.21.slot_ref) | copy-start | bytes 1540
  10.7 6.1 %collective-permute-start = (bf16[128,128]{1,0:T(8,128)(2,1)S(1)}, bf16[128,128]{1,0:T(8,128)(2,1)S(1)}, u32[]{:S(2)}, u32[]{:S(2)}) collective-permute-start(bf16[128,128]{1,0:T(8,128)(2,1)S(1)} %get-tuple-element.24), channel_id=1, source_target_pairs={{0,0},{1,1},{2,4},{3,5},{4,2},{5,3},{6,6},{7,7},{8,8},{9,9},{10,12... | collective-permute-start | bytes 98312 | tf_op jit(solution)/shard_map/ppermute | solution.py:578
  14.3 2.6 %collective-permute-start.1 = (bf16[128,128]{1,0:T(8,128)(2,1)S(1)}, bf16[128,128]{1,0:T(8,128)(2,1)S(1)}, u32[]{:S(2)}, u32[]{:S(2)}) collective-permute-start(bf16[128,128]{1,0:T(8,128)(2,1)S(1)} %get-tuple-element.25), channel_id=1, source_target_pairs={{0,4},{1,5},{2,0},{3,1},{4,6},{5,7},{6,2},{7,3},{8,12},{9,13},{10,... | collective-permute-start | bytes 98312 | tf_op jit(solution)/shard_map/ppermute | solution.py:578
  14.3 5.4 %collective-permute-start.2 = (bf16[128,128]{1,0:T(8,128)(2,1)S(1)}, bf16[128,128]{1,0:T(8,128)(2,1)S(1)}, u32[]{:S(2)}, u32[]{:S(2)}) collective-permute-start(bf16[128,128]{1,0:T(8,128)(2,1)S(1)} %get-tuple-element.26), channel_id=1, source_target_pairs={{0,1},{1,0},{2,5},{3,4},{4,3},{5,2},{6,7},{7,6},{8,9},{9,8},{10,13... | collective-permute-start | bytes 98312 | tf_op jit(solution)/shard_map/ppermute | solution.py:578
  15.6 4.8 %collective-permute-start.3 = (bf16[128,128]{1,0:T(8,128)(2,1)S(1)}, bf16[128,128]{1,0:T(8,128)(2,1)S(1)}, u32[]{:S(2)}, u32[]{:S(2)}) collective-permute-start(bf16[128,128]{1,0:T(8,128)(2,1)S(1)} %get-tuple-element.27), channel_id=1, source_target_pairs={{0,5},{1,4},{2,1},{3,0},{4,7},{5,6},{6,3},{7,2},{8,13},{9,12},{10,... | collective-permute-start | bytes 98312 | tf_op jit(solution)/shard_map/ppermute | solution.py:578
  27.0 3.9 %collective-permute-start.6 = (f32[4,512]{1,0:T(4,128)S(1)}, f32[4,512]{1,0:T(4,128)S(1)}, u32[]{:S(2)}, u32[]{:S(2)}) collective-permute-start(f32[4,512]{1,0:T(4,128)S(1)} %get-tuple-element.34.refs_0_), channel_id=1, source_target_pairs={{0,5},{1,4},{2,7},{3,6},{4,1},{5,0},{6,3},{7,2},{8,13},{9,12},{10,... | collective-permute-start | bytes 24584 | tf_op jit(solution)/shard_map/ppermute | solution.py:578
  29.2 2.5 %collective-permute-start.5 = (f32[4,512]{1,0:T(4,128)S(1)}, f32[4,512]{1,0:T(4,128)S(1)}, u32[]{:S(2)}, u32[]{:S(2)}) collective-permute-start(f32[4,512]{1,0:T(4,128)S(1)} %get-tuple-element.34.refs_0_), channel_id=1, source_target_pairs={{0,1},{1,0},{2,3},{3,2},{4,5},{5,4},{6,7},{7,6},{8,9},{9,8},{10,11... | collective-permute-start | bytes 24584 | tf_op jit(solution)/shard_map/ppermute | solution.py:578
  29.4 2.2 %collective-permute-start.4 = (f32[4,512]{1,0:T(4,128)S(1)}, f32[4,512]{1,0:T(4,128)S(1)}, u32[]{:S(2)}, u32[]{:S(2)}) collective-permute-start(f32[4,512]{1,0:T(4,128)S(1)} %get-tuple-element.34.refs_0_), channel_id=1, source_target_pairs={{0,4},{1,5},{2,6},{3,7},{4,0},{5,1},{6,2},{7,3},{8,12},{9,13},{10,... | collective-permute-start | bytes 24584 | tf_op jit(solution)/shard_map/ppermute | solution.py:578
  33.7 18.0 %all-to-all-start.1 = ((bf16[32,16,512]{2,1,0:T(8,128)(2,1)}), bf16[32,16,512]{2,1,0:T(8,128)(2,1)S(1)}, u32[]{:S(2)}, u32[]{:S(2)}) async-start(bf16[32,16,512]{2,1,0:T(8,128)(2,1)} %bitcast.2), calls=%async_computation.1 | async-start | bytes 1048576 | tf_op jit(solution)/shard_map/all_to_all | solution.py:587
  36.3 6.3 %collective-permute-start.7 = (bf16[128,128]{1,0:T(8,128)(2,1)S(1)}, bf16[128,128]{1,0:T(8,128)(2,1)S(1)}, u32[]{:S(2)}, u32[]{:S(2)}) collective-permute-start(bf16[128,128]{1,0:T(8,128)(2,1)S(1)} %get-tuple-element.36), channel_id=1, source_target_pairs={{0,0},{1,1},{4,2},{5,3},{2,4},{3,5},{6,6},{7,7},{8,8},{9,9},{12,10... | collective-permute-start | bytes 98312 | tf_op jit(solution)/shard_map/ppermute | solution.py:578
  39.9 3.6 %collective-permute-start.8 = (bf16[128,128]{1,0:T(8,128)(2,1)S(1)}, bf16[128,128]{1,0:T(8,128)(2,1)S(1)}, u32[]{:S(2)}, u32[]{:S(2)}) collective-permute-start(bf16[128,128]{1,0:T(8,128)(2,1)S(1)} %get-tuple-element.37), channel_id=1, source_target_pairs={{4,0},{5,1},{0,2},{1,3},{6,4},{7,5},{2,6},{3,7},{12,8},{13,9},{8,1... | collective-permute-start | bytes 98312 | tf_op jit(solution)/shard_map/ppermute | solution.py:578
  39.9 5.0 %collective-permute-start.9 = (bf16[128,128]{1,0:T(8,128)(2,1)S(1)}, bf16[128,128]{1,0:T(8,128)(2,1)S(1)}, u32[]{:S(2)}, u32[]{:S(2)}) collective-permute-start(bf16[128,128]{1,0:T(8,128)(2,1)S(1)} %get-tuple-element.38), channel_id=1, source_target_pairs={{1,0},{0,1},{5,2},{4,3},{3,4},{2,5},{7,6},{6,7},{9,8},{8,9},{13,10... | collective-permute-start | bytes 98312 | tf_op jit(solution)/shard_map/ppermute | solution.py:578
  41.2 4.0 %collective-permute-start.10 = (bf16[128,128]{1,0:T(8,128)(2,1)S(1)}, bf16[128,128]{1,0:T(8,128)(2,1)S(1)}, u32[]{:S(2)}, u32[]{:S(2)}) collective-permute-start(bf16[128,128]{1,0:T(8,128)(2,1)S(1)} %get-tuple-element.39), channel_id=1, source_target_pairs={{5,0},{4,1},{1,2},{0,3},{7,4},{6,5},{3,6},{2,7},{13,8},{12,9},{9,1... | collective-permute-start | bytes 98312 | tf_op jit(solution)/shard_map/ppermute | solution.py:578

commit v8 on v7

--- a/solution.py
+++ b/solution.py
@@ -433,10 +433,25 @@
             stats_ref[3:4, here] = cross
 
 
-def slope_kernel(rows_ref, slopes_ref, turned_slopes_ref, turned_weights_ref):
+def slope_kernel(
+    rows_ref,
+    grads_ref,
+    gain_ref,
+    slopes_ref,
+    turned_slopes_ref,
+    turned_weights_ref,
+    gate_ref,
+    grad_gain_ref,
+    grad_normed_ref,
+):
     size = HD
     scale = HD ** (-0.5)
     users = [window_users(rows_ref, window) for window in range(HEADS)]
+    gate = part_rows(rows_ref, 0, 0, HEADS).astype(jnp.float32) * gain_ref[...]
+    grads = grads_ref[...].astype(jnp.float32)
+    gate_ref[...] = gate
+    grad_gain_ref[...] = grads * gain_ref[...]
+    grad_normed_ref[...] = grads * gate
     for first in range(0, HEADS, STEP):
         last = first + STEP
         queries = part_rows(rows_ref, 1, first, last)
@@ -455,12 +470,13 @@
 
 def backward_kernel(
     rows_ref,
-    grads_ref,
-    gain_ref,
     attended_ref,
     slopes_ref,
     turned_slopes_ref,
     turned_weights_ref,
+    gate_ref,
+    grad_gain_ref,
+    grad_normed_ref,
     *refs,
 ):
     stats_refs = refs[:HEADS]
@@ -491,12 +507,10 @@
         row_mean, row_inv, row_grad, row_cross = [
             packed[:, 4 * window + index : 4 * window + index + 1] for index in range(4)
         ]
-        unit = part_rows(rows_ref, 0, window, window + 1).astype(jnp.float32)
-        grad_gain = grads_ref[here].astype(jnp.float32) * gain_ref[...]
         normed = (attended_ref[here] - row_mean) * row_inv
-        layer_all[here] = (normed * gain_ref[...] * unit).astype(jnp.bfloat16)
-        put_rows(out_ref, 0, window, window + 1, grad_gain * normed, readers)
-        out_grads.append(row_inv * (grad_gain * unit - row_grad - normed * row_cross))
+        layer_all[here] = (normed * gate_ref[here]).astype(jnp.bfloat16)
+        put_rows(out_ref, 0, window, window + 1, grad_gain_ref[here] * normed, readers)
+        out_grads.append(row_inv * (grad_normed_ref[here] - row_grad - normed * row_cross))
     out_grads = jnp.concatenate(out_grads, axis=0).astype(jnp.bfloat16)
     stores = []
     for first in range(0, HEADS, STEP):
@@ -667,18 +681,19 @@
             jax.ShapeDtypeStruct((group_rows, group_rows), jnp.float32),
             jax.ShapeDtypeStruct((group_rows, group_rows), jnp.float32),
             jax.ShapeDtypeStruct((group_rows, group_rows), jnp.bfloat16),
-        ),
-        in_specs=vmem(1),
-        out_specs=tuple(vmem(3)),
+        )
+        + (jax.ShapeDtypeStruct((group_rows, HD), jnp.float32),) * 3,
+        in_specs=vmem(3),
+        out_specs=tuple(vmem(6)),
         compiler_params=LIMIT,
         name="slopes",
-    )(late_rows)
+    )(late_rows, grads, gain)
     all_stats = [stats, swap(stats, 1, 0), swap(stats, 0, 1), swap(stats, 1, 1)]
     results = pl.pallas_call(
         backward_kernel,
         out_shape=(jax.ShapeDtypeStruct((group_rows, width), jnp.bfloat16),)
         + (piece_shape,) * HEADS,
-        in_specs=vmem(7 + HEADS),
+        in_specs=vmem(8 + HEADS),
         out_specs=tuple(hbm(1) + vmem(HEADS)),
         scratch_shapes=[
             pltpu.VMEM((group_rows, HD), jnp.bfloat16),
@@ -687,7 +702,7 @@
         ],
         compiler_params=LIMIT,
         name="backward",
-    )(rows, grads, gain, attended, *slopes, *all_stats)
+    )(rows, attended, *slopes, *all_stats)
     returned = exchange(results[0], chunk_back)
     layer_shape, grad_shape = (slots, HEADS * HD), (slots, 4 * HEADS * HD)
     return pl.pallas_call(

time: 53 us -> 53 us (level)
  no operation moved by 1% of the time
where the time goes in v8:
time: 53 us; the launch traced here: 52.7 us
  starting transfers between devices  23 us (43%)
  waiting for transfers between devices  21.3 us (40%)
  Pallas kernels  6.9 us (13%)
  between operations  0.76 us (1%)
  local copies, waits for them, and re-layouts  0.73 us (1%)
    ppermute x11, starting transfers between devices, send(): return lax.ppermute(value, ('dp', 'ctx'), pairs)  13.3 us
    all_to_all x2, waiting for transfers between devices, exchange(): lax.all_to_all(chunks, ('dp', 'ctx'), split_axis=0, concat_axis=0, tiled=...  12.3 us
    all_to_all x2, starting transfers between devices, exchange(): lax.all_to_all(chunks, ('dp', 'ctx'), split_axis=0, concat_axis=0, tiled=...  9.7 us
    ppermute x11, waiting for transfers between devices, send(): return lax.ppermute(value, ('dp', 'ctx'), pairs)  8.93 us
    pallas_call x1, Pallas kernels, by_heads(): pl.pallas_call(functools.partial(slot_kernel, per_pair=per_pair), out_sha...  2.18 us
    pallas_call x1, Pallas kernels, by_heads(): pl.pallas_call(backward_kernel, out_shape=(jax.ShapeDtypeStruct((group_ro...  2.02 us
  transfers between devices with their start and end apart: 13, of which 11 were waited for; matrix products, arithmetic and copies ran while one was open for 0% of the time, Pallas kernels for 2%

profile of v8, /device:TPU:1, one launch (start us, length us, event | category | flops | bytes accessed | tf_op | source)
XLA Modules:
  0.0 52.7 jit_solution(2711828327890805452)
XLA Ops:
  0.6 2.2 %slot_rows.1 = (bf16[32,72,128]{2,1,0:T(8,128)(2,1)}, s32[1,128]{1,0:T(1,128)}) custom-call(s32[16]{0:T(128)} %owner_hbm.1, s32[1,128]{1,0:T(1,128)} %bitcast.6, bf16[128,2048]{1,0:T(8,128)(2,1)} %proj_hbm.1), custom_call_target="tpu_custom_call" | custom-call | tf_op jit(solution)/shard_map/slot_rows/pallas_call | solution.py:630
  2.8 7.1 %all-to-all-start = ((bf16[32,72,128]{2,1,0:T(8,128)(2,1)}), bf16[32,72,128]{2,1,0:T(8,128)(2,1)S(1)}, u32[]{:S(2)}, u32[]{:S(2)}) async-start(bf16[32,72,128]{2,1,0:T(8,128)(2,1)} %get-tuple-element.26), calls=%async_computation | async-start | bytes 1179648 | tf_op jit(solution)/shard_map/all_to_all | solution.py:601
  10.0 0.6 %copy-done.2 = s32[1,128]{1,0:T(1,128)S(1)} copy-done((s32[1,128]{1,0:T(1,128)S(1)}, s32[1,128]{1,0:T(1,128)}, u32[]{:S(2)}) %copy-start.2) | copy-done | bytes 536
  10.6 0.1 cut_columns.1
  10.7 3.5 %collective-permute-start = (bf16[128,128]{1,0:T(8,128)(2,1)S(1)}, bf16[128,128]{1,0:T(8,128)(2,1)S(1)}, u32[]{:S(2)}, u32[]{:S(2)}) collective-permute-start(bf16[128,128]{1,0:T(8,128)(2,1)S(1)} %get-tuple-element.27), channel_id=1, source_target_pairs={{0,0},{1,1},{2,4},{3,5},{4,2},{5,3},{6,6},{7,7},{8,8},{9,9},{10,12... | collective-permute-start | bytes 98312 | tf_op jit(solution)/shard_map/ppermute | solution.py:592
  14.3 0.0 collective-permute-start.1
  14.3 1.3 %collective-permute-start.2 = (bf16[128,128]{1,0:T(8,128)(2,1)S(1)}, bf16[128,128]{1,0:T(8,128)(2,1)S(1)}, u32[]{:S(2)}, u32[]{:S(2)}) collective-permute-start(bf16[128,128]{1,0:T(8,128)(2,1)S(1)} %get-tuple-element.29), channel_id=1, source_target_pairs={{0,1},{1,0},{2,5},{3,4},{4,3},{5,2},{6,7},{7,6},{8,9},{9,8},{10,13... | collective-permute-start | bytes 98312 | tf_op jit(solution)/shard_map/ppermute | solution.py:592
  15.6 0.1 collective-permute-start.3
  15.7 0.1 dynamic-slice_bitcast_fusion.gain_ref
  15.8 1.1 %collective-permute-done.refs_0_ = bf16[128,128]{1,0:T(8,128)(2,1)S(1)} collective-permute-done((bf16[128,128]{1,0:T(8,128)(2,1)S(1)}, bf16[128,128]{1,0:T(8,128)(2,1)S(1)}, u32[]{:S(2)}, u32[]{:S(2)}) %collective-permute-start) | collective-permute-done | bytes 32800 | tf_op jit(solution)/shard_map/ppermute | solution.py:592
  16.8 2.9 %collective-permute-done.2.refs_2_ = bf16[128,128]{1,0:T(8,128)(2,1)S(1)} collective-permute-done((bf16[128,128]{1,0:T(8,128)(2,1)S(1)}, bf16[128,128]{1,0:T(8,128)(2,1)S(1)}, u32[]{:S(2)}, u32[]{:S(2)}) %collective-permute-start.2) | collective-permute-done | bytes 32800 | tf_op jit(solution)/shard_map/ppermute | solution.py:592
  19.7 0.7 %collective-permute-done.3.refs_3_ = bf16[128,128]{1,0:T(8,128)(2,1)S(1)} collective-permute-done((bf16[128,128]{1,0:T(8,128)(2,1)S(1)}, bf16[128,128]{1,0:T(8,128)(2,1)S(1)}, u32[]{:S(2)}, u32[]{:S(2)}) %collective-permute-start.3) | collective-permute-done | bytes 32800 | tf_op jit(solution)/shard_map/ppermute | solution.py:592
  20.4 5.8 %all-to-all-done.rows_ref = bf16[32,72,128]{2,1,0:T(8,128)(2,1)S(1)} async-done(((bf16[32,72,128]{2,1,0:T(8,128)(2,1)}), bf16[32,72,128]{2,1,0:T(8,128)(2,1)S(1)}, u32[]{:S(2)}, u32[]{:S(2)}) %all-to-all-start) | async-done | bytes 589856 | tf_op jit(solution)/shard_map/all_to_all | solution.py:601
  26.3 0.7 %forward.1 = (f32[512,128]{1,0:T(8,128)S(1)}, f32[4,512]{1,0:T(4,128)S(1)}) custom-call(bf16[32,72,128]{2,1,0:T(8,128)(2,1)S(1)} %all-to-all-done.rows_ref, bf16[512,128]{1,0:T(8,128)(2,1)S(1)} %lay_group.1.grads_ref, f32[1,128]{1,0:T(1,128)S(1)} %dynamic-slice_bitcast_fusion.gain_ref), custom_call_target="tpu_custom_call" | custom-call | tf_op jit(solution)/shard_map/forward/pallas_call | solution.py:666
  27.0 2.2 %collective-permute-start.6 = (f32[4,512]{1,0:T(4,128)S(1)}, f32[4,512]{1,0:T(4,128)S(1)}, u32[]{:S(2)}, u32[]{:S(2)}) collective-permute-start(f32[4,512]{1,0:T(4,128)S(1)} %get-tuple-element.40.refs_0_), channel_id=1, source_target_pairs={{0,5},{1,4},{2,7},{3,6},{4,1},{5,0},{6,3},{7,2},{8,13},{9,12},{10,... | collective-permute-start | bytes 24584 | tf_op jit(solution)/shard_map/ppermute | solution.py:592
  29.2 0.3 collective-permute-start.5
  29.4 0.2 collective-permute-start.4
  29.7 0.9 %slopes.1 = (f32[512,512]{1,0:T(8,128)S(1)}, f32[512,512]{1,0:T(8,128)S(1)}, bf16[512,512]{1,0:T(8,128)(2,1)S(1)}, f32[512,128]{1,0:T(8,128)S(1)}, f32[512,128]{1,0:T(8,128)S(1)}, /*index=5*/f32[512,128]{1,0:T(8,128)S(1)}) custom-call(bf16[32,72,128]{2,1,0:T(8,128)(2,1)S(1)} %all-to-all-done.rows_ref, bf16[512,128]{1,0:T(8,128)(2,1)S(1)} %lay_group.1.grads_ref, ...), custom_call_target="tpu_custom_call" | custom-call | tf_op jit(solution)/shard_map/slopes/pallas_call | solution.py:678
  30.5 0.3 collective-permute-done.6.refs_3_
  30.8 0.9 %collective-permute-done.5.refs_2_ = f32[4,512]{1,0:T(4,128)S(1)} collective-permute-done((f32[4,512]{1,0:T(4,128)S(1)}, f32[4,512]{1,0:T(4,128)S(1)}, u32[]{:S(2)}, u32[]{:S(2)}) %collective-permute-start.5) | collective-permute-done | bytes 8224 | tf_op jit(solution)/shard_map/ppermute | solution.py:592
  31.7 2.0 %backward.1 = (bf16[512,512]{1,0:T(8,128)(2,1)}, bf16[128,128]{1,0:T(8,128)(2,1)S(1)}, bf16[128,128]{1,0:T(8,128)(2,1)S(1)}, bf16[128,128]{1,0:T(8,128)(2,1)S(1)}, bf16[128,128]{1,0:T(8,128)(2,1)S(1)}) custom-call(bf16[32,72,128]{2,1,0:T(8,128)(2,1)S(1)} %all-to-all-done.rows_ref, f32[512,128]{1,0:T(8,128)S(1)} %get-tuple-element.31.attended_ref, ...), custom_call_target="tpu_custom_call" | custom-call | tf_op jit(solution)/shard_map/backward/pallas_call | solution.py:692
  33.7 2.6 %all-to-all-start.1 = ((bf16[32,16,512]{2,1,0:T(8,128)(2,1)}), bf16[32,16,512]{2,1,0:T(8,128)(2,1)S(1)}, u32[]{:S(2)}, u32[]{:S(2)}) async-start(bf16[32,16,512]{2,1,0:T(8,128)(2,1)} %bitcast.2), calls=%async_computation.1 | async-start | bytes 1048576 | tf_op jit(solution)/shard_map/all_to_all | solution.py:601
  36.3 3.5 %collective-permute-start.7 = (bf16[128,128]{1,0:T(8,128)(2,1)S(1)}, bf16[128,128]{1,0:T(8,128)(2,1)S(1)}, u32[]{:S(2)}, u32[]{:S(2)}) collective-permute-start(bf16[128,128]{1,0:T(8,128)(2,1)S(1)} %get-tuple-element.42), channel_id=1, source_target_pairs={{0,0},{1,1},{4,2},{5,3},{2,4},{3,5},{6,6},{7,7},{8,8},{9,9},{12,10... | collective-permute-start | bytes 98312 | tf_op jit(solution)/shard_map/ppermute | solution.py:592
  39.9 0.0 collective-permute-start.8
  39.9 1.3 %collective-permute-start.9 = (bf16[128,128]{1,0:T(8,128)(2,1)S(1)}, bf16[128,128]{1,0:T(8,128)(2,1)S(1)}, u32[]{:S(2)}, u32[]{:S(2)}) collective-permute-start(bf16[128,128]{1,0:T(8,128)(2,1)S(1)} %get-tuple-element.44), channel_id=1, source_target_pairs={{1,0},{0,1},{5,2},{4,3},{3,4},{2,5},{7,6},{6,7},{9,8},{8,9},{13,10... | collective-permute-start | bytes 98312 | tf_op jit(solution)/shard_map/ppermute | solution.py:592
  41.2 0.8 %collective-permute-start.10 = (bf16[128,128]{1,0:T(8,128)(2,1)S(1)}, bf16[128,128]{1,0:T(8,128)(2,1)S(1)}, u32[]{:S(2)}, u32[]{:S(2)}) collective-permute-start(bf16[128,128]{1,0:T(8,128)(2,1)S(1)} %get-tuple-element.45), channel_id=1, source_target_pairs={{5,0},{4,1},{1,2},{0,3},{7,4},{6,5},{3,6},{2,7},{13,8},{12,9},{9,1... | collective-permute-start | bytes 98312 | tf_op jit(solution)/shard_map/ppermute | solution.py:592
  42.0 0.6 %collective-permute-done.7.refs_0_ = bf16[128,128]{1,0:T(8,128)(2,1)S(1)} collective-permute-done((bf16[128,128]{1,0:T(8,128)(2,1)S(1)}, bf16[128,128]{1,0:T(8,128)(2,1)S(1)}, u32[]{:S(2)}, u32[]{:S(2)}) %collective-permute-start.7) | collective-permute-done | bytes 32800 | tf_op jit(solution)/shard_map/ppermute | solution.py:592
  42.6 0.8 %collective-permute-done.8.refs_1_ = bf16[128,128]{1,0:T(8,128)(2,1)S(1)} collective-permute-done((bf16[128,128]{1,0:T(8,128)(2,1)S(1)}, bf16[128,128]{1,0:T(8,128)(2,1)S(1)}, u32[]{:S(2)}, u32[]{:S(2)}) %collective-permute-start.8) | collective-permute-done | bytes 32800 | tf_op jit(solution)/shard_map/ppermute | solution.py:592
  43.4 1.5 %collective-permute-done.9.refs_2_ = bf16[128,128]{1,0:T(8,128)(2,1)S(1)} collective-permute-done((bf16[128,128]{1,0:T(8,128)(2,1)S(1)}, bf16[128,128]{1,0:T(8,128)(2,1)S(1)}, u32[]{:S(2)}, u32[]{:S(2)}) %collective-permute-start.9) | collective-permute-done | bytes 32800 | tf_op jit(solution)/shard_map/ppermute | solution.py:592
  44.9 0.3 collective-permute-done.10.refs_3_
  45.2 6.5 %all-to-all-done.1 = bf16[32,16,512]{2,1,0:T(8,128)(2,1)S(1)} async-done(((bf16[32,16,512]{2,1,0:T(8,128)(2,1)}), bf16[32,16,512]{2,1,0:T(8,128)(2,1)S(1)}, u32[]{:S(2)}, u32[]{:S(2)}) %all-to-all-start.1) | async-done | bytes 524320 | tf_op jit(solution)/shard_map/all_to_all | solution.py:601
  51.7 1.0 %unslot_rows.1 = (bf16[128,512]{1,0:T(8,128)(2,1)}, bf16[128,2048]{1,0:T(8,128)(2,1)}) custom-call(bf16[128,128]{1,0:T(8,128)(2,1)S(1)} %get-tuple-element.25.back_ref, bf16[512,512]{1,0:T(8,128)(2,1)S(1)} %bitcast.5, bf16[128,128]{1,0:T(8,128)(2,1)S(1)} %collective-permute-done.7.refs_0_, bf16[128,128]{1,0:T(8,128)(2,1)S(1)} %collective-permute-done.8.refs_1_, ...), custom_call_target="tpu_custom_call" | custom-call | tf_op jit(solution)/shard_map/unslot_rows/pallas_call | solution.py:708
  (8 shorter events, 0.0 us)
Async XLA Ops:
  0.6 15.1 %copy-start = (f32[512]{0:T(512)S(1)}, f32[512]{0:T(512)}, u32[]{:S(2)}) copy-start(f32[512]{0:T(512)} %param.6) | copy-start | bytes 6148
  2.8 7.1 %copy-start.1 = (bf16[128,512]{1,0:T(8,128)(2,1)S(1)}, bf16[128,512]{1,0:T(8,128)(2,1)}, u32[]{:S(2)}) copy-start(bf16[128,512]{1,0:T(8,128)(2,1)} %grad_ref.1) | copy-start | bytes 393220
  2.8 23.4 %all-to-all-start = ((bf16[32,72,128]{2,1,0:T(8,128)(2,1)}), bf16[32,72,128]{2,1,0:T(8,128)(2,1)S(1)}, u32[]{:S(2)}, u32[]{:S(2)}) async-start(bf16[32,72,128]{2,1,0:T(8,128)(2,1)} %get-tuple-element.26), calls=%async_computation | async-start | bytes 1179648 | tf_op jit(solution)/shard_map/all_to_all | solution.py:601
  10.0 0.7 %copy-start.2 = (s32[1,128]{1,0:T(1,128)S(1)}, s32[1,128]{1,0:T(1,128)}, u32[]{:S(2)}) copy-start(s32[1,128]{1,0:T(1,128)} %get-tuple-element.24.slot_ref) | copy-start | bytes 1540
  10.7 6.1 %collective-permute-start = (bf16[128,128]{1,0:T(8,128)(2,1)S(1)}, bf16[128,128]{1,0:T(8,128)(2,1)S(1)}, u32[]{:S(2)}, u32[]{:S(2)}) collective-permute-start(bf16[128,128]{1,0:T(8,128)(2,1)S(1)} %get-tuple-element.27), channel_id=1, source_target_pairs={{0,0},{1,1},{2,4},{3,5},{4,2},{5,3},{6,6},{7,7},{8,8},{9,9},{10,12... | collective-permute-start | bytes 98312 | tf_op jit(solution)/shard_map/ppermute | solution.py:592
  14.3 2.6 %collective-permute-start.1 = (bf16[128,128]{1,0:T(8,128)(2,1)S(1)}, bf16[128,128]{1,0:T(8,128)(2,1)S(1)}, u32[]{:S(2)}, u32[]{:S(2)}) collective-permute-start(bf16[128,128]{1,0:T(8,128)(2,1)S(1)} %get-tuple-element.28), channel_id=1, source_target_pairs={{0,4},{1,5},{2,0},{3,1},{4,6},{5,7},{6,2},{7,3},{8,12},{9,13},{10,... | collective-permute-start | bytes 98312 | tf_op jit(solution)/shard_map/ppermute | solution.py:592
  14.3 5.4 %collective-permute-start.2 = (bf16[128,128]{1,0:T(8,128)(2,1)S(1)}, bf16[128,128]{1,0:T(8,128)(2,1)S(1)}, u32[]{:S(2)}, u32[]{:S(2)}) collective-permute-start(bf16[128,128]{1,0:T(8,128)(2,1)S(1)} %get-tuple-element.29), channel_id=1, source_target_pairs={{0,1},{1,0},{2,5},{3,4},{4,3},{5,2},{6,7},{7,6},{8,9},{9,8},{10,13... | collective-permute-start | bytes 98312 | tf_op jit(solution)/shard_map/ppermute | solution.py:592
  15.6 4.8 %collective-permute-start.3 = (bf16[128,128]{1,0:T(8,128)(2,1)S(1)}, bf16[128,128]{1,0:T(8,128)(2,1)S(1)}, u32[]{:S(2)}, u32[]{:S(2)}) collective-permute-start(bf16[128,128]{1,0:T(8,128)(2,1)S(1)} %get-tuple-element.30), channel_id=1, source_target_pairs={{0,5},{1,4},{2,1},{3,0},{4,7},{5,6},{6,3},{7,2},{8,13},{9,12},{10,... | collective-permute-start | bytes 98312 | tf_op jit(solution)/shard_map/ppermute | solution.py:592
  27.0 3.9 %collective-permute-start.6 = (f32[4,512]{1,0:T(4,128)S(1)}, f32[4,512]{1,0:T(4,128)S(1)}, u32[]{:S(2)}, u32[]{:S(2)}) collective-permute-start(f32[4,512]{1,0:T(4,128)S(1)} %get-tuple-element.40.refs_0_), channel_id=1, source_target_pairs={{0,5},{1,4},{2,7},{3,6},{4,1},{5,0},{6,3},{7,2},{8,13},{9,12},{10,... | collective-permute-start | bytes 24584 | tf_op jit(solution)/shard_map/ppermute | solution.py:592
  29.2 2.5 %collective-permute-start.5 = (f32[4,512]{1,0:T(4,128)S(1)}, f32[4,512]{1,0:T(4,128)S(1)}, u32[]{:S(2)}, u32[]{:S(2)}) collective-permute-start(f32[4,512]{1,0:T(4,128)S(1)} %get-tuple-element.40.refs_0_), channel_id=1, source_target_pairs={{0,1},{1,0},{2,3},{3,2},{4,5},{5,4},{6,7},{7,6},{8,9},{9,8},{10,11... | collective-permute-start | bytes 24584 | tf_op jit(solution)/shard_map/ppermute | solution.py:592
  29.4 2.2 %collective-permute-start.4 = (f32[4,512]{1,0:T(4,128)S(1)}, f32[4,512]{1,0:T(4,128)S(1)}, u32[]{:S(2)}, u32[]{:S(2)}) collective-permute-start(f32[4,512]{1,0:T(4,128)S(1)} %get-tuple-element.40.refs_0_), channel_id=1, source_target_pairs={{0,4},{1,5},{2,6},{3,7},{4,0},{5,1},{6,2},{7,3},{8,12},{9,13},{10,... | collective-permute-start | bytes 24584 | tf_op jit(solution)/shard_map/ppermute | solution.py:592
  33.7 18.0 %all-to-all-start.1 = ((bf16[32,16,512]{2,1,0:T(8,128)(2,1)}), bf16[32,16,512]{2,1,0:T(8,128)(2,1)S(1)}, u32[]{:S(2)}, u32[]{:S(2)}) async-start(bf16[32,16,512]{2,1,0:T(8,128)(2,1)} %bitcast.2), calls=%async_computation.1 | async-start | bytes 1048576 | tf_op jit(solution)/shard_map/all_to_all | solution.py:601
  36.3 6.3 %collective-permute-start.7 = (bf16[128,128]{1,0:T(8,128)(2,1)S(1)}, bf16[128,128]{1,0:T(8,128)(2,1)S(1)}, u32[]{:S(2)}, u32[]{:S(2)}) collective-permute-start(bf16[128,128]{1,0:T(8,128)(2,1)S(1)} %get-tuple-element.42), channel_id=1, source_target_pairs={{0,0},{1,1},{4,2},{5,3},{2,4},{3,5},{6,6},{7,7},{8,8},{9,9},{12,10... | collective-permute-start | bytes 98312 | tf_op jit(solution)/shard_map/ppermute | solution.py:592
  39.9 3.6 %collective-permute-start.8 = (bf16[128,128]{1,0:T(8,128)(2,1)S(1)}, bf16[128,128]{1,0:T(8,128)(2,1)S(1)}, u32[]{:S(2)}, u32[]{:S(2)}) collective-permute-start(bf16[128,128]{1,0:T(8,128)(2,1)S(1)} %get-tuple-element.43), channel_id=1, source_target_pairs={{4,0},{5,1},{0,2},{1,3},{6,4},{7,5},{2,6},{3,7},{12,8},{13,9},{8,1... | collective-permute-start | bytes 98312 | tf_op jit(solution)/shard_map/ppermute | solution.py:592
  39.9 5.0 %collective-permute-start.9 = (bf16[128,128]{1,0:T(8,128)(2,1)S(1)}, bf16[128,128]{1,0:T(8,128)(2,1)S(1)}, u32[]{:S(2)}, u32[]{:S(2)}) collective-permute-start(bf16[128,128]{1,0:T(8,128)(2,1)S(1)} %get-tuple-element.44), channel_id=1, source_target_pairs={{1,0},{0,1},{5,2},{4,3},{3,4},{2,5},{7,6},{6,7},{9,8},{8,9},{13,10... | collective-permute-start | bytes 98312 | tf_op jit(solution)/shard_map/ppermute | solution.py:592
  41.2 4.0 %collective-permute-start.10 = (bf16[128,128]{1,0:T(8,128)(2,1)S(1)}, bf16[128,128]{1,0:T(8,128)(2,1)S(1)}, u32[]{:S(2)}, u32[]{:S(2)}) collective-permute-start(bf16[128,128]{1,0:T(8,128)(2,1)S(1)} %get-tuple-element.45), channel_id=1, source_target_pairs={{5,0},{4,1},{1,2},{0,3},{7,4},{6,5},{3,6},{2,7},{13,8},{12,9},{9,1... | collective-permute-start | bytes 98312 | tf_op jit(solution)/shard_map/ppermute | solution.py:592

commit v9 on v8

--- a/solution.py
+++ b/solution.py
@@ -404,8 +404,8 @@
     size = HD
     scale = HD ** (-0.5)
     users = [window_users(rows_ref, window) for window in range(HEADS)]
-    for first in range(0, HEADS, STEP):
-        last = first + STEP
+    for first in range(0, HEADS, HEADS):
+        last = first + HEADS
         queries = part_rows(rows_ref, 1, first, last)
         scores = dot(queries, part_rows(rows_ref, 2, 0, last), 1, 1) * scale
         visible = visible_block(users, first, last)

time: 53 us -> 53 us (level)
  no operation moved by 1% of the time
where the time goes in v9:
time: 53 us; the launch traced here: 52.7 us
  starting transfers between devices  23 us (43%)
  waiting for transfers between devices  21.3 us (40%)
  Pallas kernels  6.87 us (13%)
  between operations  0.76 us (1%)
  local copies, waits for them, and re-layouts  0.73 us (1%)
    ppermute x11, starting transfers between devices, send(): return lax.ppermute(value, ('dp', 'ctx'), pairs)  13.3 us
    all_to_all x2, waiting for transfers between devices, exchange(): lax.all_to_all(chunks, ('dp', 'ctx'), split_axis=0, concat_axis=0, tiled=...  12.4 us
    all_to_all x2, starting transfers between devices, exchange(): lax.all_to_all(chunks, ('dp', 'ctx'), split_axis=0, concat_axis=0, tiled=...  9.69 us
    ppermute x11, waiting for transfers between devices, send(): return lax.ppermute(value, ('dp', 'ctx'), pairs)  8.94 us
    pallas_call x1, Pallas kernels, by_heads(): pl.pallas_call(functools.partial(slot_kernel, per_pair=per_pair), out_sha...  2.18 us
    pallas_call x1, Pallas kernels, by_heads(): pl.pallas_call(backward_kernel, out_shape=(jax.ShapeDtypeStruct((group_ro...  2.02 us
  transfers between devices with their start and end apart: 13, of which 11 were waited for; matrix products, arithmetic and copies ran while one was open for 0% of the time, Pallas kernels for 2%

profile of v9, /device:TPU:1, one launch (start us, length us, event | category | flops | bytes accessed | tf_op | source)
XLA Modules:
  0.0 52.7 jit_solution(18139038128557112618)
XLA Ops:
  0.6 2.2 %slot_rows.1 = (bf16[32,72,128]{2,1,0:T(8,128)(2,1)}, s32[1,128]{1,0:T(1,128)}) custom-call(s32[16]{0:T(128)} %owner_hbm.1, s32[1,128]{1,0:T(1,128)} %bitcast.6, bf16[128,2048]{1,0:T(8,128)(2,1)} %proj_hbm.1), custom_call_target="tpu_custom_call" | custom-call | tf_op jit(solution)/shard_map/slot_rows/pallas_call | solution.py:630
  2.8 7.1 %all-to-all-start = ((bf16[32,72,128]{2,1,0:T(8,128)(2,1)}), bf16[32,72,128]{2,1,0:T(8,128)(2,1)S(1)}, u32[]{:S(2)}, u32[]{:S(2)}) async-start(bf16[32,72,128]{2,1,0:T(8,128)(2,1)} %get-tuple-element.26), calls=%async_computation | async-start | bytes 1179648 | tf_op jit(solution)/shard_map/all_to_all | solution.py:601
  10.0 0.6 %copy-done.2 = s32[1,128]{1,0:T(1,128)S(1)} copy-done((s32[1,128]{1,0:T(1,128)S(1)}, s32[1,128]{1,0:T(1,128)}, u32[]{:S(2)}) %copy-start.2) | copy-done | bytes 536
  10.6 0.1 cut_columns.1
  10.7 3.5 %collective-permute-start = (bf16[128,128]{1,0:T(8,128)(2,1)S(1)}, bf16[128,128]{1,0:T(8,128)(2,1)S(1)}, u32[]{:S(2)}, u32[]{:S(2)}) collective-permute-start(bf16[128,128]{1,0:T(8,128)(2,1)S(1)} %get-tuple-element.27), channel_id=1, source_target_pairs={{0,0},{1,1},{2,4},{3,5},{4,2},{5,3},{6,6},{7,7},{8,8},{9,9},{10,12... | collective-permute-start | bytes 98312 | tf_op jit(solution)/shard_map/ppermute | solution.py:592
  14.3 0.0 collective-permute-start.1
  14.3 1.3 %collective-permute-start.2 = (bf16[128,128]{1,0:T(8,128)(2,1)S(1)}, bf16[128,128]{1,0:T(8,128)(2,1)S(1)}, u32[]{:S(2)}, u32[]{:S(2)}) collective-permute-start(bf16[128,128]{1,0:T(8,128)(2,1)S(1)} %get-tuple-element.29), channel_id=1, source_target_pairs={{0,1},{1,0},{2,5},{3,4},{4,3},{5,2},{6,7},{7,6},{8,9},{9,8},{10,13... | collective-permute-start | bytes 98312 | tf_op jit(solution)/shard_map/ppermute | solution.py:592
  15.6 0.1 collective-permute-start.3
  15.7 0.1 dynamic-slice_bitcast_fusion.gain_ref
  15.8 1.1 %collective-permute-done.refs_0_ = bf16[128,128]{1,0:T(8,128)(2,1)S(1)} collective-permute-done((bf16[128,128]{1,0:T(8,128)(2,1)S(1)}, bf16[128,128]{1,0:T(8,128)(2,1)S(1)}, u32[]{:S(2)}, u32[]{:S(2)}) %collective-permute-start) | collective-permute-done | bytes 32800 | tf_op jit(solution)/shard_map/ppermute | solution.py:592
  16.8 2.9 %collective-permute-done.2.refs_2_ = bf16[128,128]{1,0:T(8,128)(2,1)S(1)} collective-permute-done((bf16[128,128]{1,0:T(8,128)(2,1)S(1)}, bf16[128,128]{1,0:T(8,128)(2,1)S(1)}, u32[]{:S(2)}, u32[]{:S(2)}) %collective-permute-start.2) | collective-permute-done | bytes 32800 | tf_op jit(solution)/shard_map/ppermute | solution.py:592
  19.7 0.7 %collective-permute-done.3.refs_3_ = bf16[128,128]{1,0:T(8,128)(2,1)S(1)} collective-permute-done((bf16[128,128]{1,0:T(8,128)(2,1)S(1)}, bf16[128,128]{1,0:T(8,128)(2,1)S(1)}, u32[]{:S(2)}, u32[]{:S(2)}) %collective-permute-start.3) | collective-permute-done | bytes 32800 | tf_op jit(solution)/shard_map/ppermute | solution.py:592
  20.4 5.8 %all-to-all-done.rows_ref = bf16[32,72,128]{2,1,0:T(8,128)(2,1)S(1)} async-done(((bf16[32,72,128]{2,1,0:T(8,128)(2,1)}), bf16[32,72,128]{2,1,0:T(8,128)(2,1)S(1)}, u32[]{:S(2)}, u32[]{:S(2)}) %all-to-all-start) | async-done | bytes 589856 | tf_op jit(solution)/shard_map/all_to_all | solution.py:601
  26.3 0.7 %forward.1 = (f32[512,128]{1,0:T(8,128)S(1)}, f32[4,512]{1,0:T(4,128)S(1)}) custom-call(bf16[32,72,128]{2,1,0:T(8,128)(2,1)S(1)} %all-to-all-done.rows_ref, bf16[512,128]{1,0:T(8,128)(2,1)S(1)} %lay_group.1.grads_ref, f32[1,128]{1,0:T(1,128)S(1)} %dynamic-slice_bitcast_fusion.gain_ref), custom_call_target="tpu_custom_call" | custom-call | tf_op jit(solution)/shard_map/forward/pallas_call | solution.py:666
  26.9 2.2 %collective-permute-start.6 = (f32[4,512]{1,0:T(4,128)S(1)}, f32[4,512]{1,0:T(4,128)S(1)}, u32[]{:S(2)}, u32[]{:S(2)}) collective-permute-start(f32[4,512]{1,0:T(4,128)S(1)} %get-tuple-element.40.refs_0_), channel_id=1, source_target_pairs={{0,5},{1,4},{2,7},{3,6},{4,1},{5,0},{6,3},{7,2},{8,13},{9,12},{10,... | collective-permute-start | bytes 24584 | tf_op jit(solution)/shard_map/ppermute | solution.py:592
  29.2 0.3 collective-permute-start.5
  29.4 0.2 collective-permute-start.4
  29.6 0.9 %slopes.1 = (f32[512,512]{1,0:T(8,128)S(1)}, f32[512,512]{1,0:T(8,128)S(1)}, bf16[512,512]{1,0:T(8,128)(2,1)S(1)}, f32[512,128]{1,0:T(8,128)S(1)}, f32[512,128]{1,0:T(8,128)S(1)}, /*index=5*/f32[512,128]{1,0:T(8,128)S(1)}) custom-call(bf16[32,72,128]{2,1,0:T(8,128)(2,1)S(1)} %all-to-all-done.rows_ref, bf16[512,128]{1,0:T(8,128)(2,1)S(1)} %lay_group.1.grads_ref, ...), custom_call_target="tpu_custom_call" | custom-call | tf_op jit(solution)/shard_map/slopes/pallas_call | solution.py:678
  30.5 0.3 collective-permute-done.6.refs_3_
  30.8 0.9 %collective-permute-done.5.refs_2_ = f32[4,512]{1,0:T(4,128)S(1)} collective-permute-done((f32[4,512]{1,0:T(4,128)S(1)}, f32[4,512]{1,0:T(4,128)S(1)}, u32[]{:S(2)}, u32[]{:S(2)}) %collective-permute-start.5) | collective-permute-done | bytes 8224 | tf_op jit(solution)/shard_map/ppermute | solution.py:592
  31.7 2.0 %backward.1 = (bf16[512,512]{1,0:T(8,128)(2,1)}, bf16[128,128]{1,0:T(8,128)(2,1)S(1)}, bf16[128,128]{1,0:T(8,128)(2,1)S(1)}, bf16[128,128]{1,0:T(8,128)(2,1)S(1)}, bf16[128,128]{1,0:T(8,128)(2,1)S(1)}) custom-call(bf16[32,72,128]{2,1,0:T(8,128)(2,1)S(1)} %all-to-all-done.rows_ref, f32[512,128]{1,0:T(8,128)S(1)} %get-tuple-element.31.attended_ref, ...), custom_call_target="tpu_custom_call" | custom-call | tf_op jit(solution)/shard_map/backward/pallas_call | solution.py:692
  33.7 2.6 %all-to-all-start.1 = ((bf16[32,16,512]{2,1,0:T(8,128)(2,1)}), bf16[32,16,512]{2,1,0:T(8,128)(2,1)S(1)}, u32[]{:S(2)}, u32[]{:S(2)}) async-start(bf16[32,16,512]{2,1,0:T(8,128)(2,1)} %bitcast.2), calls=%async_computation.1 | async-start | bytes 1048576 | tf_op jit(solution)/shard_map/all_to_all | solution.py:601
  36.3 3.5 %collective-permute-start.7 = (bf16[128,128]{1,0:T(8,128)(2,1)S(1)}, bf16[128,128]{1,0:T(8,128)(2,1)S(1)}, u32[]{:S(2)}, u32[]{:S(2)}) collective-permute-start(bf16[128,128]{1,0:T(8,128)(2,1)S(1)} %get-tuple-element.42), channel_id=1, source_target_pairs={{0,0},{1,1},{4,2},{5,3},{2,4},{3,5},{6,6},{7,7},{8,8},{9,9},{12,10... | collective-permute-start | bytes 98312 | tf_op jit(solution)/shard_map/ppermute | solution.py:592
  39.8 0.0 collective-permute-start.8
  39.9 1.3 %collective-permute-start.9 = (bf16[128,128]{1,0:T(8,128)(2,1)S(1)}, bf16[128,128]{1,0:T(8,128)(2,1)S(1)}, u32[]{:S(2)}, u32[]{:S(2)}) collective-permute-start(bf16[128,128]{1,0:T(8,128)(2,1)S(1)} %get-tuple-element.44), channel_id=1, source_target_pairs={{1,0},{0,1},{5,2},{4,3},{3,4},{2,5},{7,6},{6,7},{9,8},{8,9},{13,10... | collective-permute-start | bytes 98312 | tf_op jit(solution)/shard_map/ppermute | solution.py:592
  41.1 0.8 %collective-permute-start.10 = (bf16[128,128]{1,0:T(8,128)(2,1)S(1)}, bf16[128,128]{1,0:T(8,128)(2,1)S(1)}, u32[]{:S(2)}, u32[]{:S(2)}) collective-permute-start(bf16[128,128]{1,0:T(8,128)(2,1)S(1)} %get-tuple-element.45), channel_id=1, source_target_pairs={{5,0},{4,1},{1,2},{0,3},{7,4},{6,5},{3,6},{2,7},{13,8},{12,9},{9,1... | collective-permute-start | bytes 98312 | tf_op jit(solution)/shard_map/ppermute | solution.py:592
  42.0 0.6 %collective-permute-done.7.refs_0_ = bf16[128,128]{1,0:T(8,128)(2,1)S(1)} collective-permute-done((bf16[128,128]{1,0:T(8,128)(2,1)S(1)}, bf16[128,128]{1,0:T(8,128)(2,1)S(1)}, u32[]{:S(2)}, u32[]{:S(2)}) %collective-permute-start.7) | collective-permute-done | bytes 32800 | tf_op jit(solution)/shard_map/ppermute | solution.py:592
  42.6 0.8 %collective-permute-done.8.refs_1_ = bf16[128,128]{1,0:T(8,128)(2,1)S(1)} collective-permute-done((bf16[128,128]{1,0:T(8,128)(2,1)S(1)}, bf16[128,128]{1,0:T(8,128)(2,1)S(1)}, u32[]{:S(2)}, u32[]{:S(2)}) %collective-permute-start.8) | collective-permute-done | bytes 32800 | tf_op jit(solution)/shard_map/ppermute | solution.py:592
  43.4 1.5 %collective-permute-done.9.refs_2_ = bf16[128,128]{1,0:T(8,128)(2,1)S(1)} collective-permute-done((bf16[128,128]{1,0:T(8,128)(2,1)S(1)}, bf16[128,128]{1,0:T(8,128)(2,1)S(1)}, u32[]{:S(2)}, u32[]{:S(2)}) %collective-permute-start.9) | collective-permute-done | bytes 32800 | tf_op jit(solution)/shard_map/ppermute | solution.py:592
  44.9 0.3 collective-permute-done.10.refs_3_
  45.1 6.5 %all-to-all-done.1 = bf16[32,16,512]{2,1,0:T(8,128)(2,1)S(1)} async-done(((bf16[32,16,512]{2,1,0:T(8,128)(2,1)}), bf16[32,16,512]{2,1,0:T(8,128)(2,1)S(1)}, u32[]{:S(2)}, u32[]{:S(2)}) %all-to-all-start.1) | async-done | bytes 524320 | tf_op jit(solution)/shard_map/all_to_all | solution.py:601
  51.6 1.0 %unslot_rows.1 = (bf16[128,512]{1,0:T(8,128)(2,1)}, bf16[128,2048]{1,0:T(8,128)(2,1)}) custom-call(bf16[128,128]{1,0:T(8,128)(2,1)S(1)} %get-tuple-element.25.back_ref, bf16[512,512]{1,0:T(8,128)(2,1)S(1)} %bitcast.5, bf16[128,128]{1,0:T(8,128)(2,1)S(1)} %collective-permute-done.7.refs_0_, bf16[128,128]{1,0:T(8,128)(2,1)S(1)} %collective-permute-done.8.refs_1_, ...), custom_call_target="tpu_custom_call" | custom-call | tf_op jit(solution)/shard_map/unslot_rows/pallas_call | solution.py:708
  (8 shorter events, 0.0 us)
Async XLA Ops:
  0.6 15.1 %copy-start = (f32[512]{0:T(512)S(1)}, f32[512]{0:T(512)}, u32[]{:S(2)}) copy-start(f32[512]{0:T(512)} %param.6) | copy-start | bytes 6148
  2.8 7.1 %copy-start.1 = (bf16[128,512]{1,0:T(8,128)(2,1)S(1)}, bf16[128,512]{1,0:T(8,128)(2,1)}, u32[]{:S(2)}) copy-start(bf16[128,512]{1,0:T(8,128)(2,1)} %grad_ref.1) | copy-start | bytes 393220
  2.8 23.4 %all-to-all-start = ((bf16[32,72,128]{2,1,0:T(8,128)(2,1)}), bf16[32,72,128]{2,1,0:T(8,128)(2,1)S(1)}, u32[]{:S(2)}, u32[]{:S(2)}) async-start(bf16[32,72,128]{2,1,0:T(8,128)(2,1)} %get-tuple-element.26), calls=%async_computation | async-start | bytes 1179648 | tf_op jit(solution)/shard_map/all_to_all | solution.py:601
  10.0 0.7 %copy-start.2 = (s32[1,128]{1,0:T(1,128)S(1)}, s32[1,128]{1,0:T(1,128)}, u32[]{:S(2)}) copy-start(s32[1,128]{1,0:T(1,128)} %get-tuple-element.24.slot_ref) | copy-start | bytes 1540
  10.7 6.1 %collective-permute-start = (bf16[128,128]{1,0:T(8,128)(2,1)S(1)}, bf16[128,128]{1,0:T(8,128)(2,1)S(1)}, u32[]{:S(2)}, u32[]{:S(2)}) collective-permute-start(bf16[128,128]{1,0:T(8,128)(2,1)S(1)} %get-tuple-element.27), channel_id=1, source_target_pairs={{0,0},{1,1},{2,4},{3,5},{4,2},{5,3},{6,6},{7,7},{8,8},{9,9},{10,12... | collective-permute-start | bytes 98312 | tf_op jit(solution)/shard_map/ppermute | solution.py:592
  14.3 2.6 %collective-permute-start.1 = (bf16[128,128]{1,0:T(8,128)(2,1)S(1)}, bf16[128,128]{1,0:T(8,128)(2,1)S(1)}, u32[]{:S(2)}, u32[]{:S(2)}) collective-permute-start(bf16[128,128]{1,0:T(8,128)(2,1)S(1)} %get-tuple-element.28), channel_id=1, source_target_pairs={{0,4},{1,5},{2,0},{3,1},{4,6},{5,7},{6,2},{7,3},{8,12},{9,13},{10,... | collective-permute-start | bytes 98312 | tf_op jit(solution)/shard_map/ppermute | solution.py:592
  14.3 5.4 %collective-permute-start.2 = (bf16[128,128]{1,0:T(8,128)(2,1)S(1)}, bf16[128,128]{1,0:T(8,128)(2,1)S(1)}, u32[]{:S(2)}, u32[]{:S(2)}) collective-permute-start(bf16[128,128]{1,0:T(8,128)(2,1)S(1)} %get-tuple-element.29), channel_id=1, source_target_pairs={{0,1},{1,0},{2,5},{3,4},{4,3},{5,2},{6,7},{7,6},{8,9},{9,8},{10,13... | collective-permute-start | bytes 98312 | tf_op jit(solution)/shard_map/ppermute | solution.py:592
  15.6 4.8 %collective-permute-start.3 = (bf16[128,128]{1,0:T(8,128)(2,1)S(1)}, bf16[128,128]{1,0:T(8,128)(2,1)S(1)}, u32[]{:S(2)}, u32[]{:S(2)}) collective-permute-start(bf16[128,128]{1,0:T(8,128)(2,1)S(1)} %get-tuple-element.30), channel_id=1, source_target_pairs={{0,5},{1,4},{2,1},{3,0},{4,7},{5,6},{6,3},{7,2},{8,13},{9,12},{10,... | collective-permute-start | bytes 98312 | tf_op jit(solution)/shard_map/ppermute | solution.py:592
  26.9 3.9 %collective-permute-start.6 = (f32[4,512]{1,0:T(4,128)S(1)}, f32[4,512]{1,0:T(4,128)S(1)}, u32[]{:S(2)}, u32[]{:S(2)}) collective-permute-start(f32[4,512]{1,0:T(4,128)S(1)} %get-tuple-element.40.refs_0_), channel_id=1, source_target_pairs={{0,5},{1,4},{2,7},{3,6},{4,1},{5,0},{6,3},{7,2},{8,13},{9,12},{10,... | collective-permute-start | bytes 24584 | tf_op jit(solution)/shard_map/ppermute | solution.py:592
  29.2 2.5 %collective-permute-start.5 = (f32[4,512]{1,0:T(4,128)S(1)}, f32[4,512]{1,0:T(4,128)S(1)}, u32[]{:S(2)}, u32[]{:S(2)}) collective-permute-start(f32[4,512]{1,0:T(4,128)S(1)} %get-tuple-element.40.refs_0_), channel_id=1, source_target_pairs={{0,1},{1,0},{2,3},{3,2},{4,5},{5,4},{6,7},{7,6},{8,9},{9,8},{10,11... | collective-permute-start | bytes 24584 | tf_op jit(solution)/shard_map/ppermute | solution.py:592
  29.4 2.2 %collective-permute-start.4 = (f32[4,512]{1,0:T(4,128)S(1)}, f32[4,512]{1,0:T(4,128)S(1)}, u32[]{:S(2)}, u32[]{:S(2)}) collective-permute-start(f32[4,512]{1,0:T(4,128)S(1)} %get-tuple-element.40.refs_0_), channel_id=1, source_target_pairs={{0,4},{1,5},{2,6},{3,7},{4,0},{5,1},{6,2},{7,3},{8,12},{9,13},{10,... | collective-permute-start | bytes 24584 | tf_op jit(solution)/shard_map/ppermute | solution.py:592
  33.7 18.0 %all-to-all-start.1 = ((bf16[32,16,512]{2,1,0:T(8,128)(2,1)}), bf16[32,16,512]{2,1,0:T(8,128)(2,1)S(1)}, u32[]{:S(2)}, u32[]{:S(2)}) async-start(bf16[32,16,512]{2,1,0:T(8,128)(2,1)} %bitcast.2), calls=%async_computation.1 | async-start | bytes 1048576 | tf_op jit(solution)/shard_map/all_to_all | solution.py:601
  36.3 6.3 %collective-permute-start.7 = (bf16[128,128]{1,0:T(8,128)(2,1)S(1)}, bf16[128,128]{1,0:T(8,128)(2,1)S(1)}, u32[]{:S(2)}, u32[]{:S(2)}) collective-permute-start(bf16[128,128]{1,0:T(8,128)(2,1)S(1)} %get-tuple-element.42), channel_id=1, source_target_pairs={{0,0},{1,1},{4,2},{5,3},{2,4},{3,5},{6,6},{7,7},{8,8},{9,9},{12,10... | collective-permute-start | bytes 98312 | tf_op jit(solution)/shard_map/ppermute | solution.py:592
  39.8 3.6 %collective-permute-start.8 = (bf16[128,128]{1,0:T(8,128)(2,1)S(1)}, bf16[128,128]{1,0:T(8,128)(2,1)S(1)}, u32[]{:S(2)}, u32[]{:S(2)}) collective-permute-start(bf16[128,128]{1,0:T(8,128)(2,1)S(1)} %get-tuple-element.43), channel_id=1, source_target_pairs={{4,0},{5,1},{0,2},{1,3},{6,4},{7,5},{2,6},{3,7},{12,8},{13,9},{8,1... | collective-permute-start | bytes 98312 | tf_op jit(solution)/shard_map/ppermute | solution.py:592
  39.9 5.0 %collective-permute-start.9 = (bf16[128,128]{1,0:T(8,128)(2,1)S(1)}, bf16[128,128]{1,0:T(8,128)(2,1)S(1)}, u32[]{:S(2)}, u32[]{:S(2)}) collective-permute-start(bf16[128,128]{1,0:T(8,128)(2,1)S(1)} %get-tuple-element.44), channel_id=1, source_target_pairs={{1,0},{0,1},{5,2},{4,3},{3,4},{2,5},{7,6},{6,7},{9,8},{8,9},{13,10... | collective-permute-start | bytes 98312 | tf_op jit(solution)/shard_map/ppermute | solution.py:592
  41.1 4.0 %collective-permute-start.10 = (bf16[128,128]{1,0:T(8,128)(2,1)S(1)}, bf16[128,128]{1,0:T(8,128)(2,1)S(1)}, u32[]{:S(2)}, u32[]{:S(2)}) collective-permute-start(bf16[128,128]{1,0:T(8,128)(2,1)S(1)} %get-tuple-element.45), channel_id=1, source_target_pairs={{5,0},{4,1},{1,2},{0,3},{7,4},{6,5},{3,6},{2,7},{13,8},{12,9},{9,1... | collective-permute-start | bytes 98312 | tf_op jit(solution)/shard_map/ppermute | solution.py:592
